TPU v7x, 32 devices: a whole 2x2x4 slice. The times are simulated.
32 devices in a mesh: dp: 4 (over x, core), expert: 2 (over y), tensor: 4 (over z).
Axes of the slice: x: 2, y: 2, z: 4, core: 2. Of those that a mesh axis runs over, the one named last changes fastest.
Arguments:
- block_input: bfloat16 [4096, 1024], P(('dp', 'expert')), may hold values from -6 to 6
- first_gain: float32 [1024], replicated, may hold values from 0.5 to 1.5
- w_query: bfloat16 [1024, 1024], P(None, 'tensor'), may hold values from -0.1875 to 0.1875
- key_weight: bfloat16 [1024, 512], P(None, 'tensor'), may hold values from -0.1875 to 0.1875
- value_weight: bfloat16 [1024, 512], P(None, 'tensor'), may hold values from -0.1875 to 0.1875
- w_output: bfloat16 [1024, 1024], P('tensor'), may hold values from -1 to 1
- second_gain: float32 [1024], replicated, may hold values from 0.5 to 1.5
- w_router: bfloat16 [1024, 32], replicated, may hold values from -0.09375 to 0.09375
- w_gate: bfloat16 [32, 1024, 512], P('expert', None, 'tensor'), may hold values from -0.1875 to 0.1875
- w_up: bfloat16 [32, 1024, 512], P('expert', None, 'tensor'), may hold values from -0.1875 to 0.1875
- w_down: bfloat16 [32, 512, 1024], P('expert', 'tensor'), may hold values from -1 to 1
- expert_ids: int32 [4096, 8], P(('dp', 'expert')), may hold values from 0 to 31, as said below
- slot_index: int32 [4096, 8], P(('dp', 'expert')), may hold values from -1 to 127, as said below
- piece_start_offsets: int32 [4, 2], P('dp'), may hold values from 0 to 256
- upstream: bfloat16 [4096, 1024], P(('dp', 'expert')), may hold values from -6 to 6
Outputs:
- block_output: bfloat16 [4096, 1024], P(('dp', 'expert'), 'tensor')
- grad_input: bfloat16 [4096, 1024], P(('dp', 'expert'))
- grad_first: float32 [1024], replicated
- grad_query: float32 [1024, 1024], P(None, 'tensor')
- grad_key: float32 [1024, 512], P(None, 'tensor')
- grad_value: float32 [1024, 512], P(None, 'tensor')
- grad_output: float32 [1024, 1024], P('tensor')
- grad_second: float32 [1024], replicated
- grad_router: float32 [1024, 32], replicated
- grad_gate: float32 [32, 1024, 512], P('expert', None, 'tensor')
- grad_up: float32 [32, 1024, 512], P('expert', None, 'tensor')
- grad_down: float32 [32, 512, 1024], P('expert', 'tensor')
Inputs may be any that keep to these rules, and one draw needn't show every extreme that they name: `expert_ids`: each row names 8 different experts. `slot_index`: among the rows of one device, a pair (row, k) routed to expert e holds the number of earlier pairs of that device routed to e, rows in order and k in order within a row; a pair with 128 or more earlier ones holds -1. On every device some expert receives 128 pairs or more.
All inputs are finite; a program needn't handle non-finite values.
Results may differ from a plain program's by a relative error of at most 0.02.
Values may be sent and summed in bfloat16 or wider, within the bound.
A program may use at most 192 MiB of HBM per device.

v0:
```python
import math

import jax
import jax.numpy as jnp
from jax import lax
from jax.sharding import PartitionSpec as P

HEAD_SIZE = 64
TOPK = 8
PIC = 256


epsilon = 1e-06
rope_base = 10000.0
masked_score = -1e30


def rope_tables(positions):
    steps = jnp.arange(HEAD_SIZE // 2, dtype=jnp.float32)
    inverse = jnp.exp(steps * (-2.0 * math.log(rope_base) / HEAD_SIZE))
    angle = positions.astype(jnp.float32)[:, None] * inverse[None, :]
    return (jnp.cos(angle), jnp.sin(angle))


def apply_rotary(values, cosine_table, sine_table):
    half = values.shape[-1] // 2
    first = values[..., :half]
    second = values[..., half:]
    cosine_table = cosine_table[:, None, :]
    sine_table = sine_table[:, None, :]
    return jnp.concatenate(
        [first * cosine_table - second * sine_table, second * cosine_table + first * sine_table],
        axis=-1,
    )


def unrotate(values, cosine_table, sine_table):
    half = values.shape[-1] // 2
    first = values[..., :half]
    second = values[..., half:]
    cosine_table = cosine_table[:, None, :]
    sine_table = sine_table[:, None, :]
    return jnp.concatenate(
        [first * cosine_table + second * sine_table, second * cosine_table - first * sine_table],
        axis=-1,
    )


def piece_ids(positions, offsets):
    span = 2 * PIC
    window = positions // span
    within = positions - window * span
    count = offsets.shape[0]
    match = window[:, None] == jnp.arange(count, dtype=jnp.int32)[None, :]
    start = jnp.sum(jnp.where(match, offsets[None, :], 0), axis=1)
    inside = (window < count) & (within >= start) & (within < start + PIC)
    return jnp.where(inside, window, -1)


def matmul(left, right):
    return jnp.dot(left, right, preferred_element_type=jnp.float32)


def matmul_nt(left, right):
    return lax.dot_general(
        left, right, (((1,), (1,)), ((), ())), preferred_element_type=jnp.float32
    )


def matmul_tn(left, right):
    return lax.dot_general(
        left, right, (((0,), (0,)), ((), ())), preferred_element_type=jnp.float32
    )


def norm_scale(values):
    return lax.rsqrt(jnp.mean(values * values, axis=-1, keepdims=True) + epsilon)


def norm_back(grad, unit, scale, gain):
    weighted = grad * gain
    return scale * (weighted - unit * jnp.mean(weighted * unit, axis=-1, keepdims=True))


def per_device(
    block_input,
    first_gain,
    w_query,
    key_weight,
    value_weight,
    w_output,
    second_gain,
    w_router,
    w_gate,
    w_up,
    w_down,
    expert_ids,
    slot_index,
    piece_start_offsets,
    upstream,
):
    rows_here = block_input.shape[0]
    width = block_input.shape[1]
    groups = lax.axis_size("expert")
    length = rows_here * groups
    local_heads = w_query.shape[1] // HEAD_SIZE
    local_kv = key_weight.shape[1] // HEAD_SIZE
    sharing = local_heads // local_kv
    head_rows = sharing * rows_here
    experts_all = w_router.shape[1]
    capacity = TOPK * rows_here // experts_all
    slots_all = experts_all * capacity
    score_scale = HEAD_SIZE ** (-0.5)
    positions = lax.axis_index("expert") * rows_here + jnp.arange(rows_here, dtype=jnp.int32)
    cosine_table, sine_table = rope_tables(positions)
    inputs = block_input.astype(jnp.float32)
    first_scale = norm_scale(inputs)
    first_unit = inputs * first_scale
    first_normed = (first_unit * first_gain).astype(jnp.bfloat16)
    query_rot = apply_rotary(
        matmul(first_normed, w_query).reshape(rows_here, local_heads, HEAD_SIZE),
        cosine_table,
        sine_table,
    ).astype(jnp.bfloat16)
    key_rot = (
        apply_rotary(
            matmul(first_normed, key_weight).reshape(rows_here, local_kv, HEAD_SIZE),
            cosine_table,
            sine_table,
        )
        .astype(jnp.bfloat16)
        .reshape(rows_here, local_kv * HEAD_SIZE)
    )
    value_low = matmul(first_normed, value_weight).astype(jnp.bfloat16)
    keys_all, values_all = (
        lax.all_gather(key_rot, "expert", axis=0, tiled=True),
        lax.all_gather(value_low, "expert", axis=0, tiled=True),
    )
    block = min(512, length)
    blocks = length // block

    def by_block(array):
        return array.reshape(blocks, block, local_kv, HEAD_SIZE).transpose(0, 2, 1, 3)

    def by_rows(stacked):
        return stacked.transpose(0, 2, 1, 3).reshape(length, local_kv * HEAD_SIZE)

    def head_major(array):
        return (
            array.reshape(rows_here, local_kv, sharing, HEAD_SIZE)
            .transpose(1, 2, 0, 3)
            .reshape(local_kv, head_rows, HEAD_SIZE)
        )

    def row_major(array):
        return (
            array.reshape(local_kv, sharing, rows_here, HEAD_SIZE)
            .transpose(2, 0, 1, 3)
            .reshape(rows_here, local_heads * HEAD_SIZE)
        )

    key_blocks = by_block(keys_all)
    value_blocks = by_block(values_all)
    block_starts = jnp.arange(blocks, dtype=jnp.int32) * block
    query_heads = head_major(query_rot.reshape(rows_here, local_heads * HEAD_SIZE))
    offsets = piece_start_offsets[0]
    key_pieces = piece_ids(jnp.arange(length, dtype=jnp.int32), offsets)
    query_pieces = jnp.tile(piece_ids(positions, offsets), sharing)
    query_places = jnp.tile(positions, sharing)

    def block_scores(key_block, start):
        places = start + jnp.arange(block, dtype=jnp.int32)
        pieces = lax.dynamic_slice_in_dim(key_pieces, start, block)
        causal = places[None, :] <= query_places[:, None]
        same = (pieces[None, :] == query_pieces[:, None]) & (query_pieces[:, None] >= 0)
        scores = (
            jnp.einsum("hqd,hkd->hqk", query_heads, key_block, preferred_element_type=jnp.float32)
            * score_scale
        )
        return (scores, (causal | same)[None])

    def max_step(carry, operands):
        running_max, running_sum = carry
        key_block, start = operands
        scores, allowed = block_scores(key_block, start)
        scores = jnp.where(allowed, scores, masked_score)
        new_max = jnp.maximum(running_max, jnp.max(scores, axis=-1))
        weights = jnp.where(allowed, jnp.exp(scores - new_max[..., None]), 0.0)
        new_sum = running_sum * jnp.exp(running_max - new_max) + jnp.sum(weights, axis=-1)
        return ((new_max, new_sum), None)

    start_max = jnp.full((local_kv, head_rows), masked_score, jnp.float32)
    start_sum = jnp.zeros((local_kv, head_rows), jnp.float32)
    (row_max, row_sum), _ = lax.scan(max_step, (start_max, start_sum), (key_blocks, block_starts))
    log_total = row_max + jnp.log(row_sum)

    def block_probs(key_block, start):
        scores, allowed = block_scores(key_block, start)
        return jnp.where(allowed, jnp.exp(scores - log_total[..., None]), 0.0)

    def value_step(total, operands):
        key_block, value_block, start = operands
        probs = block_probs(key_block, start).astype(jnp.bfloat16)
        return (
            total
            + jnp.einsum("hqk,hkd->hqd", probs, value_block, preferred_element_type=jnp.float32),
            None,
        )

    mixed_output, _ = lax.scan(
        value_step,
        jnp.zeros((local_kv, head_rows, HEAD_SIZE), jnp.float32),
        (key_blocks, value_blocks, block_starts),
    )
    attended = row_major(mixed_output).astype(jnp.bfloat16)
    attention = lax.psum(matmul(attended, w_output), "tensor")
    residual = inputs + attention
    second_scale = norm_scale(residual)
    second_unit = residual * second_scale
    second_normed = (second_unit * second_gain).astype(jnp.bfloat16)
    logits = matmul(second_normed, w_router)
    chosen = jnp.take_along_axis(logits, expert_ids, axis=1)
    gates = jax.nn.softmax(chosen, axis=-1)
    row_ids = jnp.arange(rows_here, dtype=jnp.int32)
    flat = jnp.where(slot_index >= 0, expert_ids * capacity + slot_index, slots_all)
    selector = (
        jnp.zeros((slots_all, rows_here), jnp.bfloat16)
        .at[flat.reshape(-1), jnp.repeat(row_ids, TOPK)]
        .set(1.0, mode="drop")
    )
    dispatched = (
        matmul(selector, second_normed).astype(jnp.bfloat16).reshape(experts_all, capacity, width)
    )
    expert_rows = lax.all_to_all(dispatched, "expert", split_axis=0, concat_axis=1, tiled=True)
    gate_in = jnp.einsum("ebd,edf->ebf", expert_rows, w_gate, preferred_element_type=jnp.float32)
    up_in = jnp.einsum("ebd,edf->ebf", expert_rows, w_up, preferred_element_type=jnp.float32)
    sigmoid_gate = jax.nn.sigmoid(gate_in)
    silu_gate = gate_in * sigmoid_gate
    hidden = (silu_gate * up_in).astype(jnp.bfloat16)
    partial_out = jnp.einsum("ebf,efd->ebd", hidden, w_down, preferred_element_type=jnp.float32)
    expert_part = lax.psum_scatter(
        partial_out.astype(jnp.bfloat16), "tensor", scatter_dimension=2, tiled=True
    )
    returned = lax.all_to_all(expert_part, "expert", split_axis=1, concat_axis=0, tiled=True)
    quarter = returned.shape[2]
    padded_out = jnp.concatenate(
        [returned.reshape(slots_all, quarter), jnp.zeros((1, quarter), jnp.bfloat16)], axis=0
    )
    feature_start = lax.axis_index("tensor") * quarter
    grad_full = upstream.astype(jnp.float32)
    grad_part = lax.dynamic_slice_in_dim(grad_full, feature_start, quarter, 1)
    mixture = jnp.zeros((rows_here, quarter), jnp.float32)
    gate_terms = []
    for pick in range(TOPK):
        picked = padded_out[flat[:, pick]].astype(jnp.float32)
        mixture = mixture + gates[:, pick : pick + 1] * picked
        gate_terms.append(jnp.sum(grad_part * picked, axis=1))
    gate_part = jnp.stack(gate_terms, axis=1)
    block_output = (lax.dynamic_slice_in_dim(residual, feature_start, quarter, 1) + mixture).astype(
        jnp.bfloat16
    )
    slot_gates = (
        jnp.zeros((slots_all + 1,), jnp.float32)
        .at[flat.reshape(-1)]
        .set(gates.reshape(-1))[:slots_all]
    )
    grad_slots = (
        (matmul(selector, upstream) * slot_gates[:, None])
        .astype(jnp.bfloat16)
        .reshape(experts_all, capacity, width)
    )
    grad_rows_in = lax.all_to_all(grad_slots, "expert", split_axis=0, concat_axis=1, tiled=True)
    hidden_grad = jnp.einsum(
        "ebd,efd->ebf", grad_rows_in, w_down, preferred_element_type=jnp.float32
    )
    grad_down = jnp.einsum("ebf,ebd->efd", hidden, grad_rows_in, preferred_element_type=jnp.float32)
    gate_in_grad = (
        hidden_grad * up_in * (sigmoid_gate * (1.0 + gate_in * (1.0 - sigmoid_gate)))
    ).astype(jnp.bfloat16)
    up_in_grad = (hidden_grad * silu_gate).astype(jnp.bfloat16)
    grad_gate = jnp.einsum(
        "ebd,ebf->edf", expert_rows, gate_in_grad, preferred_element_type=jnp.float32
    )
    grad_up = jnp.einsum(
        "ebd,ebf->edf", expert_rows, up_in_grad, preferred_element_type=jnp.float32
    )
    rows_part = jnp.einsum("ebf,edf->ebd", gate_in_grad, w_gate, preferred_element_type=jnp.float32)
    rows_part = rows_part + jnp.einsum(
        "ebf,edf->ebd", up_in_grad, w_up, preferred_element_type=jnp.float32
    )
    rows_back = lax.all_to_all(
        rows_part.astype(jnp.bfloat16), "expert", split_axis=1, concat_axis=0, tiled=True
    ).astype(rows_part.dtype)
    padded_back = jnp.concatenate(
        [rows_back.reshape(slots_all, width), jnp.zeros((1, width), jnp.float32)], axis=0
    )
    second_part = jnp.zeros((rows_here, width), jnp.float32)
    for pick in range(TOPK):
        second_part = second_part + padded_back[flat[:, pick]]
    second_sum, gate_grads = (
        lax.psum(second_part.astype(jnp.bfloat16), "tensor").astype(jnp.float32),
        lax.psum(gate_part.astype(jnp.bfloat16), "tensor").astype(jnp.float32),
    )
    chosen_grad = gates * (gate_grads - jnp.sum(gates * gate_grads, axis=1, keepdims=True))
    expert_axis = jnp.arange(experts_all, dtype=jnp.int32)
    logit_grad = jnp.zeros((rows_here, experts_all), jnp.float32)
    for pick in range(TOPK):
        logit_grad = logit_grad + jnp.where(
            expert_ids[:, pick : pick + 1] == expert_axis[None, :],
            chosen_grad[:, pick : pick + 1],
            0.0,
        )
    logit_low = logit_grad.astype(jnp.bfloat16)
    grad_router = matmul_tn(second_normed, logit_low)
    second_grad = second_sum + matmul_nt(logit_low, w_router)
    grad_second = jnp.sum(second_grad * second_unit, axis=0)
    residual_grad = grad_full + norm_back(second_grad, second_unit, second_scale, second_gain)
    residual_low = residual_grad.astype(jnp.bfloat16)
    grad_output = matmul_tn(attended, residual_low)
    attended_grad = head_major(matmul_nt(residual_low, w_output).astype(jnp.bfloat16))

    def delta_step(total, operands):
        key_block, value_block, start = operands
        probs = block_probs(key_block, start)
        prob_grad = jnp.einsum(
            "hqd,hkd->hqk", attended_grad, value_block, preferred_element_type=jnp.float32
        )
        return (total + jnp.sum(probs * prob_grad, axis=-1), None)

    delta, _ = lax.scan(
        delta_step,
        jnp.zeros((local_kv, head_rows), jnp.float32),
        (key_blocks, value_blocks, block_starts),
    )

    def grad_step(query_total, operands):
        key_block, value_block, start = operands
        probs = block_probs(key_block, start)
        prob_grad = jnp.einsum(
            "hqd,hkd->hqk", attended_grad, value_block, preferred_element_type=jnp.float32
        )
        score_grad = (probs * (prob_grad - delta[..., None])).astype(jnp.bfloat16)
        query_total = (
            query_total
            + jnp.einsum("hqk,hkd->hqd", score_grad, key_block, preferred_element_type=jnp.float32)
            * score_scale
        )
        key_grad = (
            jnp.einsum("hqk,hqd->hkd", score_grad, query_heads, preferred_element_type=jnp.float32)
            * score_scale
        )
        value_grad = jnp.einsum(
            "hqk,hqd->hkd",
            probs.astype(jnp.bfloat16),
            attended_grad,
            preferred_element_type=jnp.float32,
        )
        return (query_total, (key_grad, value_grad))

    query_total, (key_stack, value_stack) = lax.scan(
        grad_step,
        jnp.zeros((local_kv, head_rows, HEAD_SIZE), jnp.float32),
        (key_blocks, value_blocks, block_starts),
    )
    key_back, value_back = (
        lax.psum_scatter(
            by_rows(key_stack).astype(jnp.bfloat16), "expert", scatter_dimension=0, tiled=True
        ).astype(jnp.float32),
        lax.psum_scatter(
            by_rows(value_stack).astype(jnp.bfloat16), "expert", scatter_dimension=0, tiled=True
        ).astype(jnp.float32),
    )
    query_grad = (
        unrotate(
            row_major(query_total).reshape(rows_here, local_heads, HEAD_SIZE),
            cosine_table,
            sine_table,
        )
        .astype(jnp.bfloat16)
        .reshape(rows_here, local_heads * HEAD_SIZE)
    )
    key_grad = (
        unrotate(key_back.reshape(rows_here, local_kv, HEAD_SIZE), cosine_table, sine_table)
        .astype(jnp.bfloat16)
        .reshape(rows_here, local_kv * HEAD_SIZE)
    )
    value_grad = value_back.astype(jnp.bfloat16)
    grad_query = matmul_tn(first_normed, query_grad)
    grad_key = matmul_tn(first_normed, key_grad)
    grad_value = matmul_tn(first_normed, value_grad)
    first_part = (
        matmul_nt(query_grad, w_query)
        + matmul_nt(key_grad, key_weight)
        + matmul_nt(value_grad, value_weight)
    )
    first_grad = lax.psum(first_part.astype(jnp.bfloat16), "tensor").astype(jnp.float32)
    grad_first = jnp.sum(first_grad * first_unit, axis=0)
    grad_input = (
        residual_grad + norm_back(first_grad, first_unit, first_scale, first_gain)
    ).astype(jnp.bfloat16)
    dense = lax.psum(
        (grad_query, grad_key, grad_value, grad_output, grad_router, grad_first, grad_second),
        ("dp", "expert"),
    )
    expert_sums = (
        lax.psum(grad_gate.astype(jnp.bfloat16), "dp").astype(jnp.float32),
        lax.psum(grad_up.astype(jnp.bfloat16), "dp").astype(jnp.float32),
        lax.psum(grad_down.astype(jnp.bfloat16), "dp").astype(jnp.float32),
    )
    return (
        block_output,
        grad_input,
        dense[5],
        dense[0],
        dense[1],
        dense[2],
        dense[3],
        dense[6],
        dense[4],
        expert_sums[0],
        expert_sums[1],
        expert_sums[2],
    )


def solution(mesh):
    placed = (
        P(("dp", "expert"), None),
        P(),
        P(None, "tensor"),
        P(None, "tensor"),
        P(None, "tensor"),
        P("tensor", None),
        P(),
        P(),
        P("expert", None, "tensor"),
        P("expert", None, "tensor"),
        P("expert", "tensor", None),
        P(("dp", "expert"), None),
        P(("dp", "expert"), None),
        P("dp", None),
        P(("dp", "expert"), None),
    )
    return jax.shard_map(
        per_device,
        mesh=mesh,
        in_specs=placed,
        out_specs=(
            P(("dp", "expert"), "tensor"),
            P(("dp", "expert"), None),
            P(),
            P(None, "tensor"),
            P(None, "tensor"),
            P(None, "tensor"),
            P("tensor", None),
            P(),
            P(),
            P("expert", None, "tensor"),
            P("expert", None, "tensor"),
            P("expert", "tensor", None),
        ),
        check_vma=False,
    )
```

profile of v0, /device:TPU:0, one launch (start us, length us, event | category | flops | bytes accessed | tf_op | source)
XLA Modules:
  0.0 1381.8 jit_solution(8354935656758748797)
XLA Ops:
  21.1 20.7 %while.50 = (s32[]{:T(128)}, f32[2,1024]{1,0:T(2,128)S(1)}, f32[2,1024]{1,0:T(2,128)S(1)}, s32[2]{0:T(128)S(1)}, s32[1024]{0:T(1024)S(1)}, /*index=5*/bf16[2,2,5...) while((s32[]{:T(128)}, f32[2,1024]{1,0:T(2,128)S(1)}, ...), condition=%wide.region_6.7_spmd.clone, body=%wide.region_3.6_spmd.clone.sunk | while | flops 144715264 | bytes 10514626 | solution.py:194
  48.3 11.1 while.51
  63.2 31.5 %scatter_custom_fusion.1 = bf16[2097152]{0:T(1024)(128)(2,1)} fusion(s32[4096]{0:T(1024)S(1)} %broadcast_select_fusion.1, bf16[4096]{0:T(1024)(128)(2,1)S(1)} %broadcast.572, bf16[]{:T(256)} %constant.173.clone.1), kind=kCustom, calls=%fused_computation.129 | custom fusion | bytes 4194306
  102.3 47.9 %all-reduce.11.cloned.1.call-done = f32[512,1024]{1,0:T(8,128)} async-done(((f32[512,1024]{1,0:T(8,128)}), f32[512,1024]{1,0:T(8,128)}) %all-reduce.11.cloned.1.call-update) | async-done | bytes 2097168 | tf_op jit(solution)/shard_map/psum | solution.py:216
  158.6 97.5 %all_to_all.60 = bf16[32,128,1024]{2,1,0:T(8,128)(2,1)} all-to-all(bf16[32,128,1024]{2,1,0:T(8,128)(2,1)S(1)} %bitcast.354), channel_id=1, replica_groups=mesh['dp'=4,'expert'=2,'tensor'=4] {'expert'}, dimensions={0} | all-to-all | bytes 16777216 | tf_op jit(solution)/shard_map/all_to_all | solution.py:234
  282.0 142.8 %reduce-scatter.4.cloned.1.call-done = bf16[16,256,256]{2,1,0:T(8,128)(2,1)} async-done(((bf16[16,256,1024]{2,1,0:T(8,128)(2,1)}), bf16[16,256,256]{2,1,0:T(8,128)(2,1)}) %reduce-scatter.4.cloned.1.call-update) | async-done | bytes 2097168 | tf_op jit(solution)/shard_map/reduce_scatter | solution.py:241
  437.7 33.0 %gather_fusion.16 = f32[4096]{0:T(1024)S(1)} fusion(f32[512,32]{0,1:T(8,128)S(1)} %fusion.142, s32[4096]{0:T(1024)S(1)} %reshape.836), kind=kCustom, calls=%fused_computation.16 | custom fusion | bytes 65536 | tf_op jit(solution)/shard_map/jit(take_along_axis)/gather | solution.py:222
  493.0 11.3 psum.100
  504.7 15.5 %scatter_custom_fusion = f32[4097]{0:T(1024)S(1)} fusion(s32[4096]{0:T(1024)S(1)} %bitcast.393, f32[4096]{0:T(1024)S(1)} %reshape.846, f32[]{:T(128)} %constant.96.clone.1), kind=kCustom, calls=%fused_computation.233 | custom fusion | bytes 16392 | tf_op jit(solution)/shard_map/scatter | solution.py:265
  527.2 95.2 %all_to_all.61 = bf16[32,128,1024]{2,1,0:T(8,128)(2,1)} all-to-all(bf16[32,128,1024]{2,1,0:T(8,128)(2,1)S(1)} %bitcast.353), channel_id=1, replica_groups=mesh['dp'=4,'expert'=2,'tensor'=4] {'expert'}, dimensions={0} | all-to-all | bytes 16777216 | tf_op jit(solution)/shard_map/all_to_all | solution.py:272
  646.9 12.8 add_convert_fusion
  659.7 11.8 copy.220
  678.7 89.7 %all-to-all-done.3 = bf16[16,256,1024]{2,0,1:T(8,128)(2,1)} async-done(((bf16[16,256,1024]{2,0,1:T(8,128)(2,1)}), bf16[16,256,1024]{2,0,1:T(8,128)(2,1)}, u32[]{:S(2)}, u32[]{:S(2)}) %all-to-all-start.3) | async-done | bytes 8388640 | tf_op jit(solution)/shard_map/all_to_all | solution.py:291
  768.4 11.5 copy.221
  779.9 11.4 pad_convert_fusion
  828.2 9.5 gather_fusion.11
  847.0 9.4 gather_fusion.8
  882.7 40.2 %all-reduce.13.cloned.1.call-done = bf16[512,1024]{1,0:T(8,128)(2,1)} async-done(((bf16[512,1024]{1,0:T(8,128)(2,1)}), bf16[512,1024]{1,0:T(8,128)(2,1)}) %all-reduce.13.cloned.1.call-update) | async-done | bytes 1048592 | tf_op jit(solution)/shard_map/psum | solution.py:301
  930.6 20.6 %while.52 = (s32[]{:T(128)}, f32[2,1024]{1,0:T(2,128)S(1)}, s32[2]{0:T(128)S(1)}, s32[1024]{0:T(1024)S(1)}, bf16[2,2,512,64]{2,3,1,0:T(8,128)(2,1)S(1)}, /*index...) while((s32[]{:T(128)}, f32[2,1024]{1,0:T(2,128)S(1)}, ...), condition=%wide.region_30.31_spmd.clone, body=%wide.region_28.30_spmd.clone.sunk | while | flops 275779072 | bytes 10318037 | solution.py:330
  951.2 33.7 %while.53 = (s32[]{:T(128)}, f32[2,1024,64]{1,2,0:T(8,128)}, bf16[2,2,512,64]{2,3,1,0:T(8,128)(2,1)}, bf16[2,2,512,64]{2,3,1,0:T(8,128)(2,1)}, s32[2]{0:T(128)S(...) while((s32[]{:T(128)}, f32[2,1024,64]{1,2,0:T(8,128)}, ...), condition=%wide.region_32.33_spmd.clone, body=%wide.region_31.32_spmd.clone.sunk | while | flops 684131840 | bytes 48705980 | solution.py:360
  1027.9 209.4 %all-reduce.19.cloned.1.call-done = (bf16[16,1024,128]{2,1,0:T(8,128)(2,1)}, bf16[16,1024,128]{2,1,0:T(8,128)(2,1)}, bf16[16,128,1024]{2,1,0:T(8,128)(2,1)}) async-done(((bf16[16,1024,128]{2,1,0:T(8,128)(2,1)}, bf16[16,1024,128]{2,1,0:T(8,128)(2,1)}, bf16[16,128,1024]{2,1,0:T(8,128)(2,1)}), (bf16[16,1024,128]{2,1,0:T(8,128)(2,1)}, bf16[16,1024,128]{2,1,0:T(8,128)(2,1)}, ...) | async-done | bytes 12582928 | tf_op jit(solution)/shard_map/psum | solution.py:406
  1252.5 39.7 %all-reduce.15.cloned.1.call-done = bf16[512,1024]{1,0:T(8,128)(2,1)} async-done(((bf16[512,1024]{1,0:T(8,128)(2,1)}), bf16[512,1024]{1,0:T(8,128)(2,1)}) %all-reduce.15.cloned.1.call-update) | async-done | bytes 1048592 | tf_op jit(solution)/shard_map/psum | solution.py:396
  1294.6 15.1 %all-reduce.2 = (f32[1024]{0:T(1024)}, f32[1024]{0:T(1024)}) all-reduce(f32[1024]{0:T(1024)S(1)} %get-tuple-element.650, f32[1024]{0:T(1024)S(1)} %copy-done.81), channel_id=1, replica_groups=mesh['dp'=4,'expert'=2,'tensor'=4] {'dp','expert'}, use_global_device_ids=true, to_apply=%region_38.39 | all-reduce | flops 2048 | bytes 16384 | tf_op jit(solution)/shard_map/psum | solution.py:401
  1312.8 56.3 %all-reduce.17.cloned.1.call-done = (f32[1024,256]{1,0:T(8,128)}, f32[1024,128]{1,0:T(8,128)}, f32[1024,128]{1,0:T(8,128)}, f32[256,1024]{1,0:T(8,128)}, f32[1024,32]{0,1:T(8,128)}) async-done(((f32[1024,256]{1,0:T(8,128)}, f32[1024,128]{1,0:T(8,128)}, f32[1024,128]{1,0:T(8,128)}, f32[256,1024]{1,0:T(8,128)}, f32[1024,32]{0,1:T(8,128)}), (f32[1024,256]{1,0:T(8,128)}, f32[1024,128]{1,0:T(8,128)}, ...) | async-done | bytes 3276816 | tf_op jit(solution)/shard_map/psum | solution.py:401
  (500 shorter events, 358.2 us)
Async XLA Ops:
  7.2 52.9 %copy-start = (bf16[256,1024]{1,0:T(8,128)(2,1)S(1)}, bf16[256,1024]{1,0:T(8,128)(2,1)}, u32[]{:S(2)}) copy-start(bf16[256,1024]{1,0:T(8,128)(2,1)} %param.28) | copy-start | bytes 1572868
  7.2 143.0 %all-reduce.11.cloned.1.call-start = ((), (), s32[]{:S(2)}) async-start(), calls=%async_computation.7 | async-start | bytes 4194304 | tf_op jit(solution)/shard_map/psum | solution.py:216
  62.0 362.8 %reduce-scatter.4.cloned.1.call-start = ((), (), s32[]{:S(2)}) async-start(), calls=%async_computation.8 | async-start | bytes 10485760 | tf_op jit(solution)/shard_map/reduce_scatter | solution.py:241
  102.3 51.3 %copy-start.74 = (f32[1024]{0:T(1024)S(1)}, f32[1024]{0:T(1024)}, u32[]{:S(2)}) copy-start(f32[1024]{0:T(1024)} %param.29) | copy-start | bytes 12292
  428.9 42.2 %all-to-all-start.1 = ((bf16[16,256,256]{2,0,1:T(8,128)(2,1)}), bf16[16,256,256]{2,0,1:T(8,128)(2,1)S(1)}, u32[]{:S(2)}, u32[]{:S(2)}) async-start(bf16[16,256,256]{2,0,1:T(8,128)(2,1)} %copy.216), calls=%async_computation.2 | async-start | bytes 4194304 | tf_op jit(solution)/shard_map/all_to_all | solution.py:244
  671.5 96.9 %all-to-all-start.3 = ((bf16[16,256,1024]{2,0,1:T(8,128)(2,1)}), bf16[16,256,1024]{2,0,1:T(8,128)(2,1)}, u32[]{:S(2)}, u32[]{:S(2)}) async-start(bf16[16,256,1024]{2,0,1:T(8,128)(2,1)} %copy.220), calls=%async_computation.4 | async-start | bytes 16777216 | tf_op jit(solution)/shard_map/all_to_all | solution.py:291
  678.5 244.3 %all-reduce.13.cloned.1.call-start = ((), (), s32[]{:S(2)}) async-start(), calls=%async_computation.9 | async-start | bytes 2097152 | tf_op jit(solution)/shard_map/psum | solution.py:301
  678.7 244.2 %copy-start.82 = (s32[512,1]{0,1:T(1,128)}, s32[512,1]{0,1:T(1,128)S(1)}, u32[]{:S(2)}) copy-start(s32[512,1]{0,1:T(1,128)S(1)} %get-tuple-element.785) | copy-start | bytes 6148
  678.7 244.2 %copy-start.84 = (s32[512,1]{0,1:T(1,128)}, s32[512,1]{0,1:T(1,128)S(1)}, u32[]{:S(2)}) copy-start(s32[512,1]{0,1:T(1,128)S(1)} %get-tuple-element.786) | copy-start | bytes 6148
  678.7 244.2 %copy-start.86 = (s32[512,1]{0,1:T(1,128)}, s32[512,1]{0,1:T(1,128)S(1)}, u32[]{:S(2)}) copy-start(s32[512,1]{0,1:T(1,128)S(1)} %get-tuple-element.787) | copy-start | bytes 6148
  678.7 244.2 %copy-start.88 = (s32[512,1]{0,1:T(1,128)}, s32[512,1]{0,1:T(1,128)S(1)}, u32[]{:S(2)}) copy-start(s32[512,1]{0,1:T(1,128)S(1)} %get-tuple-element.788) | copy-start | bytes 6148
  678.7 244.2 %copy-start.90 = (s32[512,1]{0,1:T(1,128)}, s32[512,1]{0,1:T(1,128)S(1)}, u32[]{:S(2)}) copy-start(s32[512,1]{0,1:T(1,128)S(1)} %get-tuple-element.789) | copy-start | bytes 6148
  873.8 134.0 %reduce-scatter.6.cloned.1.call-start = ((), (), s32[]{:S(2)}) async-start(), calls=%async_computation.10 | async-start | bytes 393216 | tf_op jit(solution)/shard_map/reduce_scatter | solution.py:366
  874.1 48.8 %copy-start.92 = (f32[512,1]{0,1:T(1,128)}, f32[512,1]{0,1:T(1,128)S(1)}, u32[]{:S(2)}) copy-start(f32[512,1]{0,1:T(1,128)S(1)} %get-tuple-element.793) | copy-start | bytes 6148
  874.1 48.8 %copy-start.94 = (f32[512,1]{0,1:T(1,128)}, f32[512,1]{0,1:T(1,128)S(1)}, u32[]{:S(2)}) copy-start(f32[512,1]{0,1:T(1,128)S(1)} %get-tuple-element.794) | copy-start | bytes 6148
  874.1 48.8 %copy-start.96 = (f32[512,1]{0,1:T(1,128)}, f32[512,1]{0,1:T(1,128)S(1)}, u32[]{:S(2)}) copy-start(f32[512,1]{0,1:T(1,128)S(1)} %get-tuple-element.795) | copy-start | bytes 6148
  874.1 48.8 %copy-start.98 = (f32[512,1]{0,1:T(1,128)}, f32[512,1]{0,1:T(1,128)S(1)}, u32[]{:S(2)}) copy-start(f32[512,1]{0,1:T(1,128)S(1)} %get-tuple-element.796) | copy-start | bytes 6148
  874.1 48.8 %copy-start.100 = (f32[512,1]{0,1:T(1,128)}, f32[512,1]{0,1:T(1,128)S(1)}, u32[]{:S(2)}) copy-start(f32[512,1]{0,1:T(1,128)S(1)} %get-tuple-element.797) | copy-start | bytes 6148
  874.1 48.8 %copy-start.8 = (f32[512,1024]{1,0:T(8,128)S(1)}, f32[512,1024]{1,0:T(8,128)}, u32[]{:S(2)}) copy-start(f32[512,1024]{1,0:T(8,128)} %copy-done.7) | copy-start | bytes 6291460
  874.2 48.8 %copy-start.69 = (bf16[1024,32]{0,1:T(8,128)(2,1)S(1)}, bf16[1024,32]{0,1:T(8,128)(2,1)}, u32[]{:S(2)}) copy-start(bf16[1024,32]{0,1:T(8,128)(2,1)} %param.30) | copy-start | bytes 196612
  987.0 25.6 %reduce-scatter.8.cloned.1.call-start = ((), (), s32[]{:S(2)}) async-start(), calls=%async_computation.11 | async-start | bytes 393216 | tf_op jit(solution)/shard_map/reduce_scatter | solution.py:369
  996.7 240.6 %all-reduce.19.cloned.1.call-start = ((), (), s32[]{:S(2)}) async-start(), calls=%async_computation.14 | async-start | bytes 25165824 | tf_op jit(solution)/shard_map/psum | solution.py:406
  1003.8 288.4 %all-reduce.15.cloned.1.call-start = ((), (), s32[]{:S(2)}) async-start(), calls=%async_computation.12 | async-start | bytes 2097152 | tf_op jit(solution)/shard_map/psum | solution.py:396
  1016.6 352.5 %all-reduce.17.cloned.1.call-start = ((), (), s32[]{:S(2)}) async-start(), calls=%async_computation.13 | async-start | bytes 6553600 | tf_op jit(solution)/shard_map/psum | solution.py:401
  (101 other events, 557.7 us)
Sparse Core Ops, SparseCore 0:
  62.1 87.9 all-reduce.10
  282.1 142.7 reduce-scatter.3
  873.9 48.9 all-reduce.12
  987.1 11.0 reduce-scatter.5
  1000.9 11.6 reduce-scatter.7
  1015.8 221.4 all-reduce.18
  1240.2 51.9 all-reduce.14
  1297.7 71.3 all-reduce.16
where the time goes:
time: 1390 us; the launch traced here: 1380 us
  waiting for transfers between devices  629 us (45%)
  local copies, waits for them, and re-layouts  253 us (18%)
  blocking collectives  232 us (17%)
  matrix products  151 us (11%)
  other arithmetic  72.3 us (5%)
  loops' own time  16.1 us (1%)
  between operations  16.1 us (1%)
    psum x1, waiting for transfers between devices, per_device(): lax.psum(grad_gate.astype(jnp.bfloat16), 'dp').astype(jnp.float32)  209 us
    reduce_scatter x1, waiting for transfers between devices, per_device(): lax.psum_scatter(partial_out.astype(jnp.bfloat16), 'tensor', scatter_dime...  143 us
    all_to_all x1, blocking collectives, per_device(): lax.all_to_all(dispatched, 'expert', split_axis=0, concat_axis=1, tiled=T...  97.5 us
    all_to_all x1, blocking collectives, per_device(): lax.all_to_all(grad_slots, 'expert', split_axis=0, concat_axis=1, tiled=T...  95.2 us
    all_to_all x1, waiting for transfers between devices, per_device(): lax.all_to_all(rows_part.astype(jnp.bfloat16), 'expert', split_axis=1, co...  89.7 us
    gather x8, local copies, waits for them, and re-layouts, per_device(): second_part = second_part + padded_back[flat[:, pick]]  74.6 us
    psum x1, waiting for transfers between devices, per_device(): lax.psum((grad_query, grad_key, grad_value, grad_output, grad_router, gra...  56.3 us
    psum x1, waiting for transfers between devices, per_device(): attention = lax.psum(matmul(attended, w_output), 'tensor')  47.9 us
  transfers between devices with their start and end apart: 10, of which 8 were waited for; matrix products, arithmetic and copies ran while one was open for 10% of the time, Pallas kernels for 0%

commit v1 on v0

--- a/solution.py
+++ b/solution.py
@@ -1,8 +1,11 @@
+import functools
 import math
 
 import jax
 import jax.numpy as jnp
 from jax import lax
+from jax.experimental import pallas as pl
+from jax.experimental.pallas import tpu as pltpu
 from jax.sharding import PartitionSpec as P
 
 HEAD_SIZE = 64
@@ -82,7 +85,7 @@
     return scale * (weighted - unit * jnp.mean(weighted * unit, axis=-1, keepdims=True))
 
 
-def per_device(
+def general_device(
     block_input,
     first_gain,
     w_query,
@@ -423,7 +426,472 @@
     )
 
 
+BF = jnp.bfloat16
+F32 = jnp.float32
+MIB = 1 << 20
+
+
+def vmem_spec():
+    return pl.BlockSpec(memory_space=pltpu.VMEM)
+
+
+def smem_spec():
+    return pl.BlockSpec(memory_space=pltpu.SMEM)
+
+
+def allowed_pairs(scal_ref, rows):
+    side = scal_ref[0]
+    here = lax.broadcasted_iota(jnp.int32, (rows, 1), 0)
+    keys = lax.broadcasted_iota(jnp.int32, (1, 2 * rows), 1)
+    query_place = side * rows + here
+    key_place = jnp.where(keys < rows, side * rows + keys, (1 - side) * rows + keys - rows)
+    span = 2 * PIC
+
+    def piece(places):
+        window = places // span
+        within = places - window * span
+        start = jnp.where(window == 0, scal_ref[1], scal_ref[2])
+        inside = (within >= start) & (within < start + PIC)
+        return jnp.where(inside, window, -1)
+
+    query_piece = piece(query_place)
+    key_piece = piece(key_place)
+    return (key_place <= query_place) | ((key_piece == query_piece) & (query_piece >= 0))
+
+
+def attend_kernel(scal_ref, q_ref, k_ref, v_ref, wo_ref, att_ref, lse_ref, part_ref):
+    rows = q_ref.shape[0]
+    heads = q_ref.shape[1] // HEAD_SIZE
+    sharing = q_ref.shape[1] // k_ref.shape[1]
+    allowed = allowed_pairs(scal_ref, rows)
+    pieces = []
+    for head in range(heads):
+        at = head * HEAD_SIZE
+        kv = head // sharing * HEAD_SIZE
+        query = q_ref[:, at : at + HEAD_SIZE]
+        key = k_ref[:, kv : kv + HEAD_SIZE]
+        value = v_ref[:, kv : kv + HEAD_SIZE]
+        scores = jnp.where(allowed, matmul_nt(query, key) * (HEAD_SIZE**-0.5), masked_score)
+        peak = jnp.max(scores, axis=1, keepdims=True)
+        weights = jnp.exp(scores - peak)
+        total = jnp.sum(weights, axis=1, keepdims=True)
+        probs = (weights * (1.0 / total)).astype(BF)
+        pieces.append(matmul(probs, value))
+        lse_ref[:, head : head + 1] = peak + jnp.log(total)
+    attended = jnp.concatenate(pieces, axis=1).astype(BF)
+    att_ref[...] = attended
+    part_ref[...] = matmul(attended, wo_ref[...]).astype(BF)
+
+
+def attend(scal, query, key, value, w_output):
+    rows, wide = query.shape
+    return pl.pallas_call(
+        attend_kernel,
+        out_shape=(
+            jax.ShapeDtypeStruct((rows, wide), BF),
+            jax.ShapeDtypeStruct((rows, 128), F32),
+            jax.ShapeDtypeStruct((rows, w_output.shape[1]), BF),
+        ),
+        in_specs=[smem_spec()] + [vmem_spec()] * 4,
+        out_specs=(vmem_spec(),) * 3,
+        compiler_params=pltpu.CompilerParams(vmem_limit_bytes=48 * MIB),
+        name="attend",
+    )(scal, query, key, value, w_output)
+
+
+def turn(values, first):
+    wide = values.shape[1]
+    half = HEAD_SIZE // 2
+    return jnp.where(
+        first, -pltpu.roll(values, wide - half, 1), pltpu.roll(values, half, 1)
+    )
+
+
+def attend_back_kernel(
+    scal_ref, q_ref, k_ref, v_ref, lse_ref, att_ref, low_ref, wo_ref, cos_ref, sin_ref,
+    dq_ref, dk_ref, dv_ref, dwo_ref,
+):
+    rows, wide = q_ref.shape
+    heads = wide // HEAD_SIZE
+    sharing = q_ref.shape[1] // k_ref.shape[1]
+    scale = HEAD_SIZE**-0.5
+    low = low_ref[...]
+    dwo_ref[...] = matmul_tn(att_ref[...], low)
+    att_grad = matmul_nt(low, wo_ref[...]).astype(BF)
+    allowed = allowed_pairs(scal_ref, rows)
+    query_parts, key_parts, value_parts = [], [], []
+    for head in range(heads):
+        at = head * HEAD_SIZE
+        kv = head // sharing * HEAD_SIZE
+        query = q_ref[:, at : at + HEAD_SIZE]
+        key = k_ref[:, kv : kv + HEAD_SIZE]
+        value = v_ref[:, kv : kv + HEAD_SIZE]
+        grad = att_grad[:, at : at + HEAD_SIZE]
+        scores = jnp.where(allowed, matmul_nt(query, key) * scale, masked_score)
+        probs = jnp.exp(scores - lse_ref[:, head : head + 1])
+        prob_grad = matmul_nt(grad, value)
+        delta = jnp.sum(probs * prob_grad, axis=1, keepdims=True)
+        score_grad = (probs * (prob_grad - delta)).astype(BF)
+        query_parts.append(matmul(score_grad, key) * scale)
+        key_part = matmul_tn(score_grad, query) * scale
+        value_part = matmul_tn(probs.astype(BF), grad)
+        if head % sharing == 0:
+            key_parts.append(key_part)
+            value_parts.append(value_part)
+        else:
+            key_parts[-1] = key_parts[-1] + key_part
+            value_parts[-1] = value_parts[-1] + value_part
+    dk_ref[...] = jnp.concatenate(key_parts, axis=1).astype(BF)
+    dv_ref[...] = jnp.concatenate(value_parts, axis=1).astype(BF)
+    rotated = jnp.concatenate(query_parts, axis=1)
+    lane = lax.broadcasted_iota(jnp.int32, (1, wide), 1)
+    first = lane % HEAD_SIZE < HEAD_SIZE // 2
+    cosines = jnp.concatenate([cos_ref[...]] * (wide // 128), axis=1)
+    sines = jnp.concatenate([sin_ref[...]] * (wide // 128), axis=1)
+    dq_ref[...] = (rotated * cosines - turn(rotated, first) * sines).astype(BF)
+
+
+def attend_back(scal, query, key, value, lse, attended, low, w_output, cosines, sines):
+    rows, wide = query.shape
+    return pl.pallas_call(
+        attend_back_kernel,
+        out_shape=(
+            jax.ShapeDtypeStruct((rows, wide), BF),
+            jax.ShapeDtypeStruct(key.shape, BF),
+            jax.ShapeDtypeStruct(value.shape, BF),
+            jax.ShapeDtypeStruct(w_output.shape, F32),
+        ),
+        in_specs=[smem_spec()] + [vmem_spec()] * 9,
+        out_specs=(vmem_spec(),) * 4,
+        compiler_params=pltpu.CompilerParams(vmem_limit_bytes=56 * MIB),
+        name="attend_back",
+    )(scal, query, key, value, lse, attended, low, w_output, cosines, sines)
+
+
+CHUNK = 256
+GROUP = 4
+
+
+def expert_kernel(last, *refs):
+    if last:
+        (
+            scal_ref, n_ref, nt_ref, g_ref, chosen_ref, kept_ref, wr_ref, wg_ref, wu_ref, wd_ref, mix_in, back_in, gg_in,
+            dwg_ref, dwu_ref, dwd_ref, mix_ref, back_ref, route_ref,
+            gates, kept_gates, gate_grads, mix, back, wgs, wus, ghs, ght, dgs, dus,
+        ) = refs
+    else:
+        (
+            scal_ref, n_ref, g_ref, chosen_ref, kept_ref, wr_ref, wg_ref, wu_ref, wd_ref,
+            dwg_ref, dwu_ref, dwd_ref, mix_ref, back_ref, gg_ref, nt_ref,
+            gates, kept_gates, gate_grads, mix, back, wgs, wus, ghs, ght, dgs, dus,
+        ) = refs
+    step = pl.program_id(0)
+    tokens, width = n_ref.shape
+    experts_all = wr_ref.shape[1]
+    group, _, hid = wg_ref.shape
+    chunks = tokens // CHUNK
+    lane = lax.broadcasted_iota(jnp.int32, (1, experts_all), 1)
+
+    @pl.when(step == 0)
+    def _():
+        def start(at, carry):
+            rows = pl.ds(pl.multiple_of(at * CHUNK, CHUNK), CHUNK)
+            chosen = chosen_ref[rows, :] > 0.0
+            logits = jnp.where(chosen, matmul(n_ref[rows, :], wr_ref[...]), masked_score)
+            raised = jnp.exp(logits - jnp.max(logits, axis=1, keepdims=True))
+            raised = jnp.where(chosen, raised, 0.0)
+            gate = raised / jnp.sum(raised, axis=1, keepdims=True)
+            gates[rows, :] = gate
+            kept_gates[rows, :] = gate * kept_ref[rows, :]
+            if last:
+                mix[rows, :] = mix_in[rows, :].astype(F32)
+                back[rows, :] = back_in[rows, :].astype(F32)
+                gate_grads[rows, :] = gg_in[rows, :]
+            else:
+                mix[rows, :] = jnp.zeros((CHUNK, width), F32)
+                back[rows, :] = jnp.zeros((CHUNK, width), F32)
+                gate_grads[rows, :] = jnp.zeros((CHUNK, experts_all), F32)
+            return carry
+
+        lax.fori_loop(0, chunks, start, 0)
+        if not last:
+            for at in range(chunks):
+                nt_ref[:, at * CHUNK : (at + 1) * CHUNK] = n_ref[at * CHUNK : (at + 1) * CHUNK, :].T
+
+    for expert in range(group):
+        wgs[:, expert * hid : (expert + 1) * hid] = wg_ref[expert]
+        wus[:, expert * hid : (expert + 1) * hid] = wu_ref[expert]
+    column = scal_ref[1] * (experts_all // 2) + scal_ref[0] * (experts_all // 4) + step * group
+
+    def forward(at, carry):
+        rows = pl.ds(pl.multiple_of(at * CHUNK, CHUNK), CHUNK)
+        token = n_ref[rows, :]
+        down = wd_ref[...].reshape(group * hid, width)
+        gate_in = matmul(token, wgs[...])
+        up_in = matmul(token, wus[...])
+        pulled = matmul_nt(g_ref[rows, :], down)
+        sig = 0.5 * jnp.tanh(0.5 * gate_in) + 0.5
+        silu = gate_in * sig
+        hidden = silu * up_in
+        kept = kept_gates[rows, :]
+        weights = []
+        products = hidden * pulled
+        grads = gate_grads[rows, :]
+        for expert in range(group):
+            here = lane == column + expert
+            gate = jnp.sum(jnp.where(here, kept, 0.0), axis=1, keepdims=True)
+            weights.append(jnp.broadcast_to(gate, (CHUNK, hid)))
+            product = jnp.sum(products[:, expert * hid : (expert + 1) * hid], axis=1, keepdims=True)
+            grads = grads + jnp.where(here, product, 0.0)
+        gate_grads[rows, :] = grads
+        weight = jnp.concatenate(weights, axis=1)
+        gated = (hidden * weight).astype(BF)
+        pulled = pulled * weight
+        up_grad = (pulled * silu).astype(BF)
+        gate_grad = (pulled * up_in * (sig + silu * (1.0 - sig))).astype(BF)
+        ghs[rows, :] = gated
+        dgs[rows, :] = gate_grad
+        dus[rows, :] = up_grad
+        mix[rows, :] += matmul(gated, down)
+        back[rows, :] += matmul_nt(gate_grad, wgs[...]) + matmul_nt(up_grad, wus[...])
+        return carry
+
+    lax.fori_loop(0, chunks, forward, 0)
+    for at in range(chunks):
+        ght[:, at * CHUNK : (at + 1) * CHUNK] = ghs[at * CHUNK : (at + 1) * CHUNK, :].T
+
+    def weights_grad(at, carry):
+        rows = pl.ds(pl.multiple_of(at * CHUNK, CHUNK), CHUNK)
+        turned = nt_ref[rows, :]
+        gate_part = matmul(turned, dgs[...]).astype(BF)
+        up_part = matmul(turned, dus[...]).astype(BF)
+        for expert in range(group):
+            dwg_ref[expert, rows, :] = gate_part[:, expert * hid : (expert + 1) * hid]
+            dwu_ref[expert, rows, :] = up_part[:, expert * hid : (expert + 1) * hid]
+        return carry
+
+    lax.fori_loop(0, width // CHUNK, weights_grad, 0)
+    for at in range(group * hid // CHUNK):
+        part = matmul(ght[at * CHUNK : (at + 1) * CHUNK, :], g_ref[...]).astype(BF)
+        for inner in range(CHUNK // hid):
+            dwd_ref[at * (CHUNK // hid) + inner] = part[inner * hid : (inner + 1) * hid, :]
+
+    @pl.when(step == pl.num_programs(0) - 1)
+    def _():
+        if last:
+            route_ref[...] = jnp.zeros(route_ref.shape, F32)
+
+        def finish(at, carry):
+            rows = pl.ds(pl.multiple_of(at * CHUNK, CHUNK), CHUNK)
+            mix_ref[rows, :] = mix[rows, :].astype(BF)
+            if last:
+                grads = gate_grads[rows, :] * kept_gates[rows, :]
+                chosen_grad = grads - gates[rows, :] * jnp.sum(grads, axis=1, keepdims=True)
+                low = chosen_grad.astype(BF)
+                back_ref[rows, :] = (back[rows, :] + matmul_nt(low, wr_ref[...])).astype(BF)
+                route_ref[...] += matmul_tn(low, n_ref[rows, :])
+            else:
+                back_ref[rows, :] = back[rows, :].astype(BF)
+                gg_ref[rows, :] = gate_grads[rows, :]
+            return carry
+
+        lax.fori_loop(0, chunks, finish, 0)
+
+
+def experts(last, scal, normed, turned, upstream, chosen, kept, w_router, w_gate, w_up, w_down, mix, back, gate_grads):
+    tokens, width = normed.shape
+    count, _, hid = w_gate.shape
+    half = count // 2
+    steps = half // GROUP
+    experts_all = w_router.shape[1]
+    whole = lambda step, scal: (0, 0)
+    full = lambda array: pl.BlockSpec(array.shape, whole)
+    picked = lambda step, scal: (scal[0] * steps + step, 0, 0)
+    own = lambda step, scal: (step, 0, 0)
+    rows_block = pl.BlockSpec((tokens, width), whole)
+    narrow_block = pl.BlockSpec((tokens, experts_all), whole)
+    args = [normed] + ([turned] if last else []) + [upstream, chosen, kept, w_router]
+    specs = [full(array) for array in args]
+    args += [w_gate, w_up, w_down]
+    specs += [
+        pl.BlockSpec((GROUP, width, hid), picked),
+        pl.BlockSpec((GROUP, width, hid), picked),
+        pl.BlockSpec((GROUP, hid, width), picked),
+    ]
+    if last:
+        args += [mix, back, gate_grads]
+        specs += [rows_block, rows_block, narrow_block]
+    out_shape = [
+        jax.ShapeDtypeStruct((half, width, hid), BF),
+        jax.ShapeDtypeStruct((half, width, hid), BF),
+        jax.ShapeDtypeStruct((half, hid, width), BF),
+        jax.ShapeDtypeStruct((tokens, width), BF),
+        jax.ShapeDtypeStruct((tokens, width), BF),
+    ]
+    out_specs = [
+        pl.BlockSpec((GROUP, width, hid), own),
+        pl.BlockSpec((GROUP, width, hid), own),
+        pl.BlockSpec((GROUP, hid, width), own),
+        rows_block,
+        rows_block,
+    ]
+    if last:
+        out_shape += [jax.ShapeDtypeStruct((experts_all, width), F32)]
+        out_specs += [pl.BlockSpec((experts_all, width), whole)]
+    else:
+        out_shape += [
+            jax.ShapeDtypeStruct((tokens, experts_all), F32),
+            jax.ShapeDtypeStruct((width, tokens), BF),
+        ]
+        out_specs += [narrow_block, pl.BlockSpec((width, tokens), whole)]
+    return pl.pallas_call(
+        functools.partial(expert_kernel, last),
+        out_shape=out_shape,
+        grid_spec=pltpu.PrefetchScalarGridSpec(
+            num_scalar_prefetch=1,
+            grid=(steps,),
+            in_specs=specs,
+            out_specs=out_specs,
+            scratch_shapes=[
+                pltpu.VMEM((tokens, experts_all), F32),
+                pltpu.VMEM((tokens, experts_all), F32),
+                pltpu.VMEM((tokens, experts_all), F32),
+                pltpu.VMEM((tokens, width), F32),
+                pltpu.VMEM((tokens, width), F32),
+                pltpu.VMEM((width, GROUP * hid), BF),
+                pltpu.VMEM((width, GROUP * hid), BF),
+                pltpu.VMEM((tokens, GROUP * hid), BF),
+                pltpu.VMEM((GROUP * hid, tokens), BF),
+                pltpu.VMEM((tokens, GROUP * hid), BF),
+                pltpu.VMEM((tokens, GROUP * hid), BF),
+            ],
+        ),
+        compiler_params=pltpu.CompilerParams(
+            dimension_semantics=("arbitrary",), vmem_limit_bytes=60 * MIB
+        ),
+        cost_estimate=pl.CostEstimate(
+            flops=18 * tokens * width * half * hid,
+            bytes_accessed=12 * half * width * hid + 16 * tokens * width,
+            transcendentals=tokens * half * hid,
+        ),
+        name="experts_last" if last else "experts_first",
+    )(scal, *args)
+
+
+def swap(array, axis, bit):
+    size = lax.axis_size(axis)
+    return lax.ppermute(array, axis, [(at, at ^ bit) for at in range(size)])
+
+
+def fast_device(
+    block_input, first_gain, w_query, key_weight, value_weight, w_output, second_gain, w_router,
+    w_gate, w_up, w_down, expert_ids, slot_index, piece_start_offsets, upstream,
+):
+    rows, width = block_input.shape
+    local_heads = w_query.shape[1] // HEAD_SIZE
+    local_kv = key_weight.shape[1] // HEAD_SIZE
+    experts_all = w_router.shape[1]
+    side = lax.axis_index("expert")
+    core = lax.axis_index("dp") % 2
+    feature_start = lax.axis_index("tensor") * (width // 4)
+    scal = jnp.concatenate([side[None].astype(jnp.int32), piece_start_offsets[0]])
+
+    axis_row = jnp.arange(experts_all, dtype=jnp.int32)[None, None, :]
+    hits = (expert_ids[:, :, None] == axis_row)
+    chosen = jnp.sum(hits.astype(F32), axis=1)
+    kept = jnp.sum((hits & (slot_index >= 0)[:, :, None]).astype(F32), axis=1)
+    marks = jnp.concatenate([chosen, kept], axis=1).astype(BF)
+    marks = jnp.concatenate([marks, swap(marks, "expert", 1)], axis=0).astype(F32)
+    chosen, kept = marks[:, :experts_all], marks[:, experts_all:]
+    upstream_all = jnp.concatenate([upstream, swap(upstream, "expert", 1)], axis=0)
+
+    positions = side * rows + jnp.arange(rows, dtype=jnp.int32)
+    cosine_table, sine_table = rope_tables(positions)
+    cosines = jnp.tile(cosine_table, (1, 4))
+    sines = jnp.tile(sine_table, (1, 4))
+    inputs = block_input.astype(F32)
+    first_scale = norm_scale(inputs)
+    first_unit = inputs * first_scale
+    first_normed = (first_unit * first_gain).astype(BF)
+    query_rot = apply_rotary(
+        matmul(first_normed, w_query).reshape(rows, local_heads, HEAD_SIZE), cosine_table, sine_table
+    ).astype(BF).reshape(rows, local_heads * HEAD_SIZE)
+    key_rot = apply_rotary(
+        matmul(first_normed, key_weight).reshape(rows, local_kv, HEAD_SIZE), cosine_table, sine_table
+    ).astype(BF).reshape(rows, local_kv * HEAD_SIZE)
+    value_low = matmul(first_normed, value_weight).astype(BF)
+    both = jnp.concatenate([key_rot, value_low], axis=1)
+    both = jnp.concatenate([both, swap(both, "expert", 1)], axis=0)
+    keys, values = both[:, : local_kv * HEAD_SIZE], both[:, local_kv * HEAD_SIZE :]
+
+    attended, lse, part = attend(scal, query_rot, keys, values, w_output)
+    residual = inputs + lax.psum(part, "tensor").astype(F32)
+    second_scale = norm_scale(residual)
+    second_unit = residual * second_scale
+    second_normed = (second_unit * second_gain).astype(BF)
+    normed_all = jnp.concatenate([second_normed, swap(second_normed, "expert", 1)], axis=0)
+
+    away = jnp.stack([1 - core, side]).astype(jnp.int32)
+    home = jnp.stack([core, side]).astype(jnp.int32)
+    dwg0, dwu0, dwd0, mix, back, gate_grads, turned = experts(
+        False, away, normed_all, None, upstream_all, chosen, kept, w_router, w_gate, w_up, w_down, None, None, None
+    )
+    sent = [swap(item, "dp", 1) for item in (dwd0, dwg0, dwu0)]
+    dwg1, dwu1, dwd1, mix, back, route = experts(
+        True, home, normed_all, turned, upstream_all, chosen, kept, w_router, w_gate, w_up, w_down, mix, back, gate_grads
+    )
+    pairs = [
+        (mine.astype(F32) + other.astype(F32)).astype(BF) for mine, other in zip((dwd1, dwg1, dwu1), sent)
+    ]
+    crossed = [swap(item, "dp", 2) for item in pairs]
+    sums = [(mine.astype(F32) + other.astype(F32)).astype(BF) for mine, other in zip(pairs, crossed)]
+    others = [swap(item, "dp", 1) for item in sums]
+    expert_sums = [
+        jnp.where(core == 0, jnp.concatenate([mine, other], axis=0), jnp.concatenate([other, mine], axis=0)).astype(F32)
+        for mine, other in zip(sums, others)
+    ]
+
+    mixed = lax.psum_scatter(mix, "tensor", scatter_dimension=1, tiled=True)
+    mixed = mixed[:rows].astype(F32) + swap(mixed[rows:], "expert", 1).astype(F32)
+    block_output = (
+        lax.dynamic_slice_in_dim(residual, feature_start, width // 4, 1) + mixed
+    ).astype(BF)
+
+    own_back = (back[:rows].astype(F32) + swap(back[rows:], "expert", 1).astype(F32)).astype(BF)
+    second_grad = lax.psum(own_back, "tensor").astype(F32)
+    grad_second = jnp.sum(second_grad * second_unit, axis=0)
+    residual_grad = upstream.astype(F32) + norm_back(second_grad, second_unit, second_scale, second_gain)
+    residual_low = residual_grad.astype(BF)
+
+    query_grad, dk, dv, grad_output = attend_back(
+        scal, query_rot, keys, values, lse, attended, residual_low, w_output, cosines, sines
+    )
+    dboth = jnp.concatenate([dk, dv], axis=1)
+    dboth = dboth[:rows].astype(F32) + swap(dboth[rows:], "expert", 1).astype(F32)
+    key_back, value_back = dboth[:, : local_kv * HEAD_SIZE], dboth[:, local_kv * HEAD_SIZE :]
+    key_grad = unrotate(
+        key_back.reshape(rows, local_kv, HEAD_SIZE), cosine_table, sine_table
+    ).astype(BF).reshape(rows, local_kv * HEAD_SIZE)
+    value_grad = value_back.astype(BF)
+    grad_query = matmul_tn(first_normed, query_grad)
+    grad_key = matmul_tn(first_normed, key_grad)
+    grad_value = matmul_tn(first_normed, value_grad)
+    first_part = (
+        matmul_nt(query_grad, w_query) + matmul_nt(key_grad, key_weight) + matmul_nt(value_grad, value_weight)
+    )
+    first_grad = lax.psum(first_part.astype(BF), "tensor").astype(F32)
+    grad_first = jnp.sum(first_grad * first_unit, axis=0)
+    grad_input = (residual_grad + norm_back(first_grad, first_unit, first_scale, first_gain)).astype(BF)
+    dense = lax.psum((grad_query, grad_key, grad_value, grad_output, grad_first, grad_second), ("dp", "expert"))
+    grad_router = lax.psum(route, ("dp", "expert", "tensor")).T
+    return (
+        block_output, grad_input, dense[4], dense[0], dense[1], dense[2], dense[3], dense[5], grad_router,
+        expert_sums[1], expert_sums[2], expert_sums[0],
+    )
+
+
 def solution(mesh):
+    fast = mesh.shape["expert"] == 2 and mesh.shape["dp"] == 4 and mesh.shape["tensor"] == 4
     placed = (
         P(("dp", "expert"), None),
         P(),
@@ -442,7 +910,7 @@
         P(("dp", "expert"), None),
     )
     return jax.shard_map(
-        per_device,
+        fast_device if fast else general_device,
         mesh=mesh,
         in_specs=placed,
         out_specs=(

time: 1390 us -> 630 us (0.45)
  waiting for transfers between devices: 629 us -> 379 us
  local copies, waits for them, and re-layouts: 253 us -> 22.8 us
  blocking collectives: 232 us -> 14 us
  matrix products: 151 us -> 14.5 us
  Pallas kernels: 0 us -> 95.7 us
  loops' own time: 16.1 us -> 0 us
    all_to_all x2 -> x0, blocking collectives: 193 us -> none  [the longest x1 97.5 us: per_device(): lax.all_to_all(dispatched, 'expert', split_axis=0, concat_axis=1, tiled=T...]
    psum x5, waiting for transfers between devices: 393 us -> 203 us  [the longest x1 73.1 us: fast_device(): lax.psum((grad_query, grad_key, grad_value, grad_output, grad_first, grad...]
    ppermute x0 -> x16, waiting for transfers between devices: none -> 176 us  [swap(): return lax.ppermute(array, axis, [(at, at ^ bit) for at in range(size)])]
    reduce_scatter x3 -> x1, waiting for transfers between devices: 146 us -> 0.02 us  [fast_device(): mixed = lax.psum_scatter(mix, 'tensor', scatter_dimension=1, tiled=True)]
    gather x21 -> x0, local copies, waits for them, and re-layouts: 127 us -> none  [the longest x8 74.6 us: per_device(): second_part = second_part + padded_back[flat[:, pick]]]
    dot_general x27 -> x0, matrix products: 114 us -> none  [the longest x6 17.1 us: block_scores(): jnp.einsum('hqd,hkd->hqk', query_heads, key_block, preferred_element_type...]
    pallas_call x0 -> x4, Pallas kernels: none -> 95.7 us  [the longest x2 75.9 us: experts(): pl.pallas_call(functools.partial(expert_kernel, last), out_shape=out_shap...]
    all_to_all x2 -> x0, waiting for transfers between devices: 89.7 us -> none  [the longest x1 89.7 us: per_device(): lax.all_to_all(rows_part.astype(jnp.bfloat16), 'expert', split_axis=1, co...]
  transfers between devices with their start and end apart: 10 -> 22, of which waited for: 8 -> 12; matrix products, arithmetic and copies ran while one was open for 10% -> 11% of each run, Pallas kernels for 0% -> 0%
where the time goes in v1:
time: 630 us; the launch traced here: 622 us
  waiting for transfers between devices  379 us (60%)
  Pallas kernels  95.7 us (15%)
  other arithmetic  64.6 us (10%)
  local copies, waits for them, and re-layouts  22.8 us (4%)
  starting transfers between devices  16.1 us (3%)
  between operations  15.1 us (2%)
  matrix products  14.5 us (2%)
  blocking collectives  14 us (2%)
    ppermute x16, waiting for transfers between devices, swap(): return lax.ppermute(array, axis, [(at, at ^ bit) for at in range(size)])  176 us
    pallas_call x2, Pallas kernels, experts(): pl.pallas_call(functools.partial(expert_kernel, last), out_shape=out_shap...  75.9 us
    psum x1, waiting for transfers between devices, fast_device(): lax.psum((grad_query, grad_key, grad_value, grad_output, grad_first, grad...  73.1 us
    psum x1, waiting for transfers between devices, fast_device(): residual = inputs + lax.psum(part, 'tensor').astype(F32)  51.5 us
    psum x1, waiting for transfers between devices, fast_device(): second_grad = lax.psum(own_back, 'tensor').astype(F32)  49.2 us
    psum x1, waiting for transfers between devices, fast_device(): grad_router = lax.psum(route, ('dp', 'expert', 'tensor')).T  28.6 us
    convert_element_type x6, other arithmetic, fast_device(): (mine.astype(F32) + other.astype(F32)).astype(BF)  20.9 us
    convert_element_type x3, other arithmetic, fast_device(): jnp.where(core == 0, jnp.concatenate([mine, other], axis=0), jnp.concaten...  18.4 us
  transfers between devices with their start and end apart: 22, of which 12 were waited for; matrix products, arithmetic and copies ran while one was open for 11% of the time, Pallas kernels for 0%

profile of v1, /device:TPU:0, one launch (start us, length us, event | category | flops | bytes accessed | tf_op | source)
XLA Modules:
  0.0 621.6 jit_solution(11168124599749835758)
XLA Ops:
  16.5 5.6 collective-permute-done
  23.3 7.2 %attend.1 = (bf16[512,256]{1,0:T(8,128)(2,1)S(1)}, f32[512,128]{1,0:T(8,128)S(1)}, bf16[512,1024]{1,0:T(8,128)(2,1)}) custom-call(s32[3]{0:T(128)S(1)} %pad_add_fusion.scal_ref, bf16[512,256]{1,0:T(8,128)(2,1)S(1)} %copy.60.q_ref, bf16[1024,128]{1,0:T(8,128)(2,1)S(1)} %get-tuple-element.71.k_ref, bf16[1024,128]{1,0:T(8,128)(2,1)S(1)} %get-tuple-element.70.v_ref, ...), custom_call_target="tpu_custom_call" | custom-call | tf_op jit(solution)/shard_map/attend/pallas_call | solution.py:488
  33.8 51.5 %all-reduce.8.cloned.1.call-done = bf16[512,1024]{1,0:T(8,128)(2,1)} async-done(((bf16[512,1024]{1,0:T(8,128)(2,1)}), bf16[512,1024]{1,0:T(8,128)(2,1)}) %all-reduce.8.cloned.1.call-update) | async-done | bytes 1048592 | tf_op jit(solution)/shard_map/psum | solution.py:828
  94.9 21.7 %collective-permute-done.3 = bf16[512,64]{1,0:T(8,128)(2,1)S(1)} collective-permute-done((bf16[512,64]{1,0:T(8,128)(2,1)S(1)}, bf16[512,64]{1,0:T(8,128)(2,1)S(1)}, u32[]{:S(2)}, u32[]{:S(2)}) %collective-permute-start.3) | collective-permute-done | bytes 65568 | tf_op jit(solution)/shard_map/ppermute | solution.py:783
  123.2 37.1 %experts_first.1 = (bf16[8,1024,128]{2,1,0:T(8,128)(2,1)}, bf16[8,1024,128]{2,1,0:T(8,128)(2,1)}, bf16[8,128,1024]{2,1,0:T(8,128)(2,1)}, bf16[1024,1024]{1,0:T(8...) custom-call(s32[2]{0:T(128)} %get-tuple-element.79.refs_0_, ...), custom_call_target="tpu_custom_call" | custom-call | flops 19327352832 | bytes 29360128 | tf_op jit(solution)/shard_map/experts_first/pallas_call | solution.py:747
  160.3 38.7 %experts_last.1 = (bf16[8,1024,128]{2,1,0:T(8,128)(2,1)}, bf16[8,1024,128]{2,1,0:T(8,128)(2,1)}, bf16[8,128,1024]{2,1,0:T(8,128)(2,1)}, bf16[1024,1024]{1,0:T(8,...) custom-call(s32[2]{0:T(128)} %get-tuple-element.78.refs_0_, bf16[1024,1024]{1,0:T(8,128)(2,1)} %pad_maximum_fusion.refs_1_, ...), custom_call_target="tpu_custom_call" | custom-call | flops 19327352832 | bytes 29360128 | tf_op jit(solution)/shard_map/experts_last/pallas_call | solution.py:747
  202.1 22.8 %collective-permute-done.5 = bf16[512,1024]{1,0:T(8,128)(2,1)S(1)} collective-permute-done((bf16[512,1024]{1,0:T(8,128)(2,1)S(1)}, bf16[512,1024]{1,0:T(8,128)(2,1)S(1)}, u32[]{:S(2)}, u32[]{:S(2)}) %collective-permute-start.5) | collective-permute-done | bytes 1048608 | tf_op jit(solution)/shard_map/ppermute | solution.py:783
  228.3 49.2 %all-reduce.10.cloned.1.call-done = bf16[512,1024]{1,0:T(8,128)(2,1)} async-done(((bf16[512,1024]{1,0:T(8,128)(2,1)}), bf16[512,1024]{1,0:T(8,128)(2,1)}) %all-reduce.10.cloned.1.call-update) | async-done | bytes 1048592 | tf_op jit(solution)/shard_map/psum | solution.py:861
  282.2 12.6 %attend_back.1 = (bf16[512,256]{1,0:T(8,128)(2,1)}, bf16[1024,128]{1,0:T(8,128)(2,1)}, bf16[1024,128]{1,0:T(8,128)(2,1)}, f32[256,1024]{1,0:T(8,128)}) custom-call(s32[3]{0:T(128)} %copy-done.7, bf16[512,256]{1,0:T(8,128)(2,1)} %copy-done.1, bf16[1024,128]{1,0:T(8,128)(2,1)} %copy-done.3, bf16[1024,128]{1,0:T(8,128)(2,1)} %copy-done.2, ...), custom_call_target="tpu_custom_call" | custom-call | tf_op jit(solution)/shard_map/attend_back/pallas_call | solution.py:556
  301.1 4.1 collective-permute-done.6
  315.5 4.0 add_convert_fusion.1
  331.2 37.1 %collective-permute-done.14 = bf16[8,128,1024]{2,1,0:T(8,128)(2,1)} collective-permute-done((bf16[8,128,1024]{2,1,0:T(8,128)(2,1)}, bf16[8,128,1024]{2,1,0:T(8,128)(2,1)}, u32[]{:S(2)}, u32[]{:S(2)}) %collective-permute-start.14) | collective-permute-done | bytes 2097184 | tf_op jit(solution)/shard_map/ppermute | solution.py:783
  368.3 5.0 add_convert_fusion
  373.3 40.0 %collective-permute-done.11 = bf16[8,1024,128]{2,1,0:T(8,128)(2,1)} collective-permute-done((bf16[8,1024,128]{2,1,0:T(8,128)(2,1)}, bf16[8,1024,128]{2,1,0:T(8,128)(2,1)}, u32[]{:S(2)}, u32[]{:S(2)}) %collective-permute-start.11) | collective-permute-done | bytes 2097184 | tf_op jit(solution)/shard_map/ppermute | solution.py:783
  413.2 4.1 add_convert_fusion.2
  417.3 40.5 %collective-permute-done.8 = bf16[8,1024,128]{2,1,0:T(8,128)(2,1)} collective-permute-done((bf16[8,1024,128]{2,1,0:T(8,128)(2,1)}, bf16[8,1024,128]{2,1,0:T(8,128)(2,1)}, u32[]{:S(2)}, u32[]{:S(2)}) %collective-permute-start.8) | collective-permute-done | bytes 2097184 | tf_op jit(solution)/shard_map/ppermute | solution.py:783
  457.8 4.2 add_convert_fusion.4
  468.7 4.0 fusion.12
  472.7 14.0 %all-reduce = (f32[1024]{0:T(1024)}, f32[1024]{0:T(1024)}) all-reduce(f32[1024]{0:T(1024)S(1)} %get-tuple-element.54, f32[1024]{0:T(1024)S(1)} %copy-done.28), channel_id=1, replica_groups=mesh['dp'=4,'expert'=2,'tensor'=4] {'dp','expert'}, use_global_device_ids=true, to_apply=%region_11.12 | all-reduce | flops 2048 | bytes 16384 | tf_op jit(solution)/shard_map/psum | solution.py:885
  488.6 6.0 fusion.2
  494.6 6.0 fusion.1
  500.6 6.4 %fusion = f32[16,1024,128]{2,1,0:T(8,128)} fusion(bf16[8,1024,128]{2,1,0:T(8,128)(2,1)} %collective-permute-done.9, bf16[8,1024,128]{2,1,0:T(8,128)(2,1)} %add_convert_fusion.4, pred[]{:T(512)S(6)} %eq.23), kind=kLoop, calls=%fused_computation.1 | loop fusion | flops 8388608 | bytes 12582913 | tf_op jit(solution)/shard_map/convert_element_type | solution.py:850
  506.9 28.6 %all-reduce.14.cloned.1.call-done = f32[1024,32]{0,1:T(8,128)} async-done(((f32[1024,32]{0,1:T(8,128)}), f32[1024,32]{0,1:T(8,128)}) %all-reduce.14.cloned.1.call-update) | async-done | bytes 131088 | tf_op jit(solution)/shard_map/psum | solution.py:886
  535.6 73.1 %all-reduce.16.cloned.1.call-done = (f32[1024,256]{1,0:T(8,128)}, f32[1024,128]{1,0:T(8,128)}, f32[1024,128]{1,0:T(8,128)}, f32[256,1024]{1,0:T(8,128)}) async-done(((f32[1024,256]{1,0:T(8,128)}, f32[1024,128]{1,0:T(8,128)}, f32[1024,128]{1,0:T(8,128)}, f32[256,1024]{1,0:T(8,128)}), (f32[1024,256]{1,0:T(8,128)}, f32[1024,128]{1,0:T(8,128)}, f32[1024,128]{1,0:T(8,128)}, ...) | async-done | bytes 3145744 | tf_op jit(solution)/shard_map/psum | solution.py:885
  (170 shorter events, 82.9 us)
Async XLA Ops:
  7.2 78.1 %all-reduce.8.cloned.1.call-start = ((), (), s32[]{:S(2)}) async-start(), calls=%async_computation.1 | async-start | bytes 2097152 | tf_op jit(solution)/shard_map/psum | solution.py:828
  12.6 9.6 %collective-permute-start = (bf16[512,256]{1,0:T(8,128)(2,1)}, bf16[512,256]{1,0:T(8,128)(2,1)}, u32[]{:S(2)}, u32[]{:S(2)}) collective-permute-start(bf16[512,256]{1,0:T(8,128)(2,1)} %pad_maximum_fusion.3), channel_id=1, source_target_pairs={{0,4},{4,0},{1,5},{5,1},{2,6},{6,2},{3,7},{7,3},{8,12},{12,8},{9,1... | collective-permute-start | bytes 786440 | tf_op jit(solution)/shard_map/ppermute | solution.py:783
  23.2 63.9 %copy-start.2 = (bf16[1024,128]{1,0:T(8,128)(2,1)}, bf16[1024,128]{1,0:T(8,128)(2,1)S(1)}, u32[]{:S(2)}) copy-start(bf16[1024,128]{1,0:T(8,128)(2,1)S(1)} %get-tuple-element.70.v_ref) | copy-start | bytes 786436
  23.2 63.9 %copy-start.24 = (f32[1024]{0:T(1024)S(1)}, f32[1024]{0:T(1024)}, u32[]{:S(2)}) copy-start(f32[1024]{0:T(1024)} %param.21) | copy-start | bytes 12292
  31.9 245.6 %all-reduce.10.cloned.1.call-start = ((), (), s32[]{:S(2)}) async-start(), calls=%async_computation.3 | async-start | bytes 2097152 | tf_op jit(solution)/shard_map/psum | solution.py:861
  32.0 85.9 %collective-permute-start.2 = (bf16[512,1024]{1,0:T(8,128)(2,1)}, bf16[512,1024]{1,0:T(8,128)(2,1)}, u32[]{:S(2)}, u32[]{:S(2)}) collective-permute-start(bf16[512,1024]{1,0:T(8,128)(2,1)} %param.29), channel_id=1, source_target_pairs={{0,4},{4,0},{1,5},{5,1},{2,6},{6,2},{3,7},{7,3},{8,12},{12,8},{9,1... | collective-permute-start | bytes 3145736 | tf_op jit(solution)/shard_map/ppermute | solution.py:783
  88.6 31.6 %collective-permute-start.1 = (bf16[512,1024]{1,0:T(8,128)(2,1)}, bf16[512,1024]{1,0:T(8,128)(2,1)}, u32[]{:S(2)}, u32[]{:S(2)}) collective-permute-start(bf16[512,1024]{1,0:T(8,128)(2,1)} %multiply_convert_fusion), channel_id=1, source_target_pairs={{0,4},{4,0},{1,5},{5,1},{2,6},{6,2},{3,7},{7,3},{8,12},{12,8},{9,1... | collective-permute-start | bytes 3145736 | tf_op jit(solution)/shard_map/ppermute | solution.py:783
  90.6 26.1 %collective-permute-start.3 = (bf16[512,64]{1,0:T(8,128)(2,1)S(1)}, bf16[512,64]{1,0:T(8,128)(2,1)S(1)}, u32[]{:S(2)}, u32[]{:S(2)}) collective-permute-start(bf16[512,64]{1,0:T(8,128)(2,1)S(1)} %pad_maximum_fusion.5), channel_id=1, source_target_pairs={{0,4},{4,0},{1,5},{5,1},{2,6},{6,2},{3,7},{7,3},{8,12},{12,8},{9,1... | collective-permute-start | bytes 196616 | tf_op jit(solution)/shard_map/ppermute | solution.py:783
  200.5 24.3 %collective-permute-start.5 = (bf16[512,1024]{1,0:T(8,128)(2,1)S(1)}, bf16[512,1024]{1,0:T(8,128)(2,1)S(1)}, u32[]{:S(2)}, u32[]{:S(2)}) collective-permute-start(bf16[512,1024]{1,0:T(8,128)(2,1)S(1)} %slice.66), channel_id=1, source_target_pairs={{0,4},{4,0},{1,5},{5,1},{2,6},{6,2},{3,7},{7,3},{8,12},{12,8},{9,1... | collective-permute-start | bytes 3145736 | tf_op jit(solution)/shard_map/ppermute | solution.py:783
  226.3 237.2 %all-reduce.12.cloned.1.call-start = ((), (), s32[]{:S(2)}) async-start(), calls=%async_computation.4 | async-start | bytes 2097152 | tf_op jit(solution)/shard_map/psum | solution.py:882
  296.8 8.3 %collective-permute-start.6 = (bf16[512,256]{1,0:T(8,128)(2,1)S(1)}, bf16[512,256]{1,0:T(8,128)(2,1)S(1)}, u32[]{:S(2)}, u32[]{:S(2)}) collective-permute-start(bf16[512,256]{1,0:T(8,128)(2,1)S(1)} %slice.84), channel_id=1, source_target_pairs={{0,4},{4,0},{1,5},{5,1},{2,6},{6,2},{3,7},{7,3},{8,12},{12,8},{9,1... | collective-permute-start | bytes 786440 | tf_op jit(solution)/shard_map/ppermute | solution.py:783
  310.4 155.1 %reduce-scatter.2.cloned.1.call-start = ((), (), s32[]{:S(2)}) async-start(), calls=%async_computation.2 | async-start | bytes 2621440 | tf_op jit(solution)/shard_map/reduce_scatter | solution.py:854
  311.0 224.6 %all-reduce.14.cloned.1.call-start = ((), (), s32[]{:S(2)}) async-start(), calls=%async_computation.5 | async-start | bytes 262144 | tf_op jit(solution)/shard_map/psum | solution.py:886
  311.1 4.4 collective-permute-start.13
  311.1 9.9 %collective-permute-start.10 = (bf16[8,1024,128]{2,1,0:T(8,128)(2,1)}, bf16[8,1024,128]{2,1,0:T(8,128)(2,1)S(1)}, u32[]{:S(2)}, u32[]{:S(2)}) collective-permute-start(bf16[8,1024,128]{2,1,0:T(8,128)(2,1)} %get-tuple-element.49), channel_id=1, source_target_pairs={{0,8},{8,0},{16,24},{24,16},{1,9},{9,1},{17,25},{25,17},{2,10},{10... | collective-permute-start | bytes 6291464 | tf_op jit(solution)/shard_map/ppermute | solution.py:783
  311.6 11.8 %collective-permute-start.7 = (bf16[8,1024,128]{2,1,0:T(8,128)(2,1)}, bf16[8,1024,128]{2,1,0:T(8,128)(2,1)S(1)}, u32[]{:S(2)}, u32[]{:S(2)}) collective-permute-start(bf16[8,1024,128]{2,1,0:T(8,128)(2,1)} %get-tuple-element.47), channel_id=1, source_target_pairs={{0,8},{8,0},{16,24},{24,16},{1,9},{9,1},{17,25},{25,17},{2,10},{10... | collective-permute-start | bytes 6291464 | tf_op jit(solution)/shard_map/ppermute | solution.py:783
  319.5 48.8 %collective-permute-start.14 = (bf16[8,128,1024]{2,1,0:T(8,128)(2,1)}, bf16[8,128,1024]{2,1,0:T(8,128)(2,1)}, u32[]{:S(2)}, u32[]{:S(2)}) collective-permute-start(bf16[8,128,1024]{2,1,0:T(8,128)(2,1)} %add_convert_fusion.1), channel_id=1, source_target_pairs={{0,16},{8,24},{16,0},{24,8},{1,17},{9,25},{17,1},{25,9},{2,18},{10... | collective-permute-start | bytes 6291464 | tf_op jit(solution)/shard_map/ppermute | solution.py:783
  322.9 90.4 %collective-permute-start.11 = (bf16[8,1024,128]{2,1,0:T(8,128)(2,1)}, bf16[8,1024,128]{2,1,0:T(8,128)(2,1)}, u32[]{:S(2)}, u32[]{:S(2)}) collective-permute-start(bf16[8,1024,128]{2,1,0:T(8,128)(2,1)} %add_convert_fusion.3), channel_id=1, source_target_pairs={{0,16},{8,24},{16,0},{24,8},{1,17},{9,25},{17,1},{25,9},{2,18},{10... | collective-permute-start | bytes 6291464 | tf_op jit(solution)/shard_map/ppermute | solution.py:783
  325.3 132.5 %collective-permute-start.8 = (bf16[8,1024,128]{2,1,0:T(8,128)(2,1)}, bf16[8,1024,128]{2,1,0:T(8,128)(2,1)}, u32[]{:S(2)}, u32[]{:S(2)}) collective-permute-start(bf16[8,1024,128]{2,1,0:T(8,128)(2,1)} %add_convert_fusion.5), channel_id=1, source_target_pairs={{0,16},{8,24},{16,0},{24,8},{1,17},{9,25},{17,1},{25,9},{2,18},{10... | collective-permute-start | bytes 6291464 | tf_op jit(solution)/shard_map/ppermute | solution.py:783
  326.8 281.9 %all-reduce.16.cloned.1.call-start = ((), (), s32[]{:S(2)}) async-start(), calls=%async_computation.6 | async-start | bytes 6291456 | tf_op jit(solution)/shard_map/psum | solution.py:885
  373.3 115.3 %collective-permute-start.15 = (bf16[8,128,1024]{2,1,0:T(8,128)(2,1)}, bf16[8,128,1024]{2,1,0:T(8,128)(2,1)}, u32[]{:S(2)}, u32[]{:S(2)}) collective-permute-start(bf16[8,128,1024]{2,1,0:T(8,128)(2,1)} %add_convert_fusion), channel_id=1, source_target_pairs={{0,8},{8,0},{16,24},{24,16},{1,9},{9,1},{17,25},{25,17},{2,10},{10... | collective-permute-start | bytes 6291464 | tf_op jit(solution)/shard_map/ppermute | solution.py:783
  417.3 77.3 %collective-permute-start.12 = (bf16[8,1024,128]{2,1,0:T(8,128)(2,1)}, bf16[8,1024,128]{2,1,0:T(8,128)(2,1)}, u32[]{:S(2)}, u32[]{:S(2)}) collective-permute-start(bf16[8,1024,128]{2,1,0:T(8,128)(2,1)} %add_convert_fusion.2), channel_id=1, source_target_pairs={{0,8},{8,0},{16,24},{24,16},{1,9},{9,1},{17,25},{25,17},{2,10},{10... | collective-permute-start | bytes 6291464 | tf_op jit(solution)/shard_map/ppermute | solution.py:783
  462.0 38.6 %collective-permute-start.9 = (bf16[8,1024,128]{2,1,0:T(8,128)(2,1)}, bf16[8,1024,128]{2,1,0:T(8,128)(2,1)}, u32[]{:S(2)}, u32[]{:S(2)}) collective-permute-start(bf16[8,1024,128]{2,1,0:T(8,128)(2,1)} %add_convert_fusion.4), channel_id=1, source_target_pairs={{0,8},{8,0},{16,24},{24,16},{1,9},{9,1},{17,25},{25,17},{2,10},{10... | collective-permute-start | bytes 6291464 | tf_op jit(solution)/shard_map/ppermute | solution.py:783
  467.2 19.5 %collective-permute-start.4 = (bf16[512,256]{1,0:T(8,128)(2,1)}, bf16[512,256]{1,0:T(8,128)(2,1)S(1)}, u32[]{:S(2)}, u32[]{:S(2)}) collective-permute-start(bf16[512,256]{1,0:T(8,128)(2,1)} %slice.82), channel_id=1, source_target_pairs={{0,4},{4,0},{1,5},{5,1},{2,6},{6,2},{3,7},{7,3},{8,12},{12,8},{9,1... | collective-permute-start | bytes 786440 | tf_op jit(solution)/shard_map/ppermute | solution.py:783
  (30 other events, 266.4 us)
Sparse Core Ops, SparseCore 0:
  32.0 53.2 all-reduce.7
  226.4 51.0 all-reduce.9
  310.5 51.1 all-reduce.11
  364.0 43.2 reduce-scatter.1
  413.2 122.3 all-reduce.13
  539.6 69.0 all-reduce.15

commit v2 on v1

--- a/solution.py
+++ b/solution.py
@@ -778,6 +778,298 @@
     )(scal, *args)
 
 
+MESH = pl.DeviceIdType.MESH
+PART = 32
+
+
+def meet(partners):
+    barrier = pltpu.get_barrier_semaphore()
+    count = 0
+    for here, device in partners:
+        here = jnp.asarray(here)
+
+        @pl.when(here)
+        def _():
+            pl.semaphore_signal(barrier, inc=1, device_id=device, device_id_type=MESH)
+
+        count = count + here.astype(jnp.int32)
+    pl.semaphore_wait(barrier, count)
+
+
+def line_partners():
+    place = lax.axis_index("tensor")
+    last = lax.axis_size("tensor") - 1
+    return [(place > 0, {"tensor": place - 1}), (place < last, {"tensor": place + 1})]
+
+
+class Line:
+    def __init__(self, parts, term, from_left, from_right, to_right, to_left, sems):
+        self.place = lax.axis_index("tensor")
+        self.last = lax.axis_size("tensor") - 1
+        self.parts = parts
+        self.term = term
+        self.from_left, self.from_right = from_left, from_right
+        self.to_right, self.to_left = to_right, to_left
+        self.sems = sems
+
+    def copy(self, way, at):
+        near = jnp.where(self.place < self.last, self.place + 1, self.place - 1)
+        far = jnp.where(self.place > 0, self.place - 1, self.place + 1)
+        source, target, device = (
+            (self.to_right, self.from_left, near) if way == 0 else (self.to_left, self.from_right, far)
+        )
+        return pltpu.make_async_remote_copy(
+            src_ref=source.at[at],
+            dst_ref=target.at[at],
+            send_sem=self.sems.at[2 * way, at],
+            recv_sem=self.sems.at[2 * way + 1, at],
+            device_id={"tensor": device},
+            device_id_type=MESH,
+        )
+
+    def clear(self):
+        @pl.when(self.place == 0)
+        def _():
+            self.from_left[...] = jnp.zeros(self.from_left.shape, self.from_left.dtype)
+
+        @pl.when(self.place == self.last)
+        def _():
+            self.from_right[...] = jnp.zeros(self.from_right.shape, self.from_right.dtype)
+
+    def step(self, at):
+        for way in range(2):
+            part = at - (self.place if way == 0 else self.last - self.place)
+            has_source = self.place > 0 if way == 0 else self.place < self.last
+            has_target = self.place < self.last if way == 0 else self.place > 0
+            arrived = self.from_left if way == 0 else self.from_right
+            leaving = self.to_right if way == 0 else self.to_left
+            valid = (part >= 0) & (part < self.parts)
+
+            @pl.when(valid & has_source)
+            def _():
+                self.copy(way, part).wait_recv()
+
+            @pl.when(valid & has_target)
+            def _():
+                leaving[part] = (self.term(part) + arrived[part].astype(F32)).astype(BF)
+                self.copy(way, part).start()
+
+    def total(self, part):
+        return self.term(part) + self.from_left[part].astype(F32) + self.from_right[part].astype(F32)
+
+    def drain(self):
+        def wait(part, carry):
+            @pl.when(self.place < self.last)
+            def _():
+                self.copy(0, part).wait_send()
+
+            @pl.when(self.place > 0)
+            def _():
+                self.copy(1, part).wait_send()
+
+            return carry
+
+        lax.fori_loop(0, self.parts, wait, 0)
+
+
+def line_scratch(parts, width):
+    return [pltpu.VMEM((parts, PART, width), BF)] * 4 + [pltpu.SemaphoreType.DMA((4, parts))]
+
+
+def peer_copy(source, target, sems, at):
+    return pltpu.make_async_remote_copy(
+        src_ref=source,
+        dst_ref=target,
+        send_sem=sems.at[0, at],
+        recv_sem=sems.at[1, at],
+        device_id={"expert": 1 - lax.axis_index("expert")},
+        device_id_type=MESH,
+    )
+
+
+def scale_of(values):
+    return lax.rsqrt(jnp.mean(values * values, axis=-1, keepdims=True) + epsilon)
+
+
+def residual_kernel(
+    part_ref, x_ref, gain_ref, res_ref, n_ref, from_left, from_right, to_right, to_left, sems, peer_sems
+):
+    parts = part_ref.shape[0]
+    line = Line(parts, lambda at: part_ref[at].astype(F32), from_left, from_right, to_right, to_left, sems)
+    line.clear()
+    meet(line_partners() + [(True, {"expert": 1 - lax.axis_index("expert")})])
+
+    def body(at, carry):
+        line.step(at)
+        part = at - line.last
+
+        @pl.when(part >= 0)
+        def _():
+            residual = x_ref[part].astype(F32) + line.total(part)
+            res_ref[part] = residual
+            unit = residual * scale_of(residual)
+            n_ref[0, part] = (unit * gain_ref[...]).astype(BF)
+            peer_copy(n_ref.at[0, part], n_ref.at[1, part], peer_sems, part).start()
+
+        return carry
+
+    lax.fori_loop(0, parts + line.last, body, 0)
+    line.drain()
+
+    def wait(part, carry):
+        peer_copy(n_ref.at[0, part], n_ref.at[1, part], peer_sems, part).wait()
+        return carry
+
+    lax.fori_loop(0, parts, wait, 0)
+
+
+def residual_norm(part, block_input, gain):
+    rows, width = block_input.shape
+    parts = rows // PART
+    residual, normed = pl.pallas_call(
+        residual_kernel,
+        out_shape=(
+            jax.ShapeDtypeStruct((parts, PART, width), F32),
+            jax.ShapeDtypeStruct((2, parts, PART, width), BF),
+        ),
+        in_specs=[vmem_spec()] * 3,
+        out_specs=(vmem_spec(),) * 2,
+        scratch_shapes=line_scratch(parts, width) + [pltpu.SemaphoreType.DMA((2, parts))],
+        compiler_params=pltpu.CompilerParams(
+            collective_id=0, has_side_effects=True, vmem_limit_bytes=40 * MIB
+        ),
+        name="residual_norm",
+    )(part.reshape(parts, PART, width), block_input.reshape(parts, PART, width), gain[None])
+    return residual, normed.reshape(2 * rows, width)
+
+
+def residual_grad_kernel(
+    back_ref, route_ref, res_ref, up_ref, gain_ref, grad_ref, low_ref, second_ref, route_out,
+    from_left, from_right, to_right, to_left, sems, peer_sems, arrived, terms,
+):
+    parts = back_ref.shape[1]
+    line = Line(parts + 1, lambda at: terms[at], from_left, from_right, to_right, to_left, sems)
+    line.clear()
+    meet(line_partners() + [(True, {"expert": 1 - lax.axis_index("expert")})])
+
+    def send(part, carry):
+        peer_copy(back_ref.at[1, part], arrived.at[part], peer_sems, part).start()
+        return carry
+
+    lax.fori_loop(0, parts, send, 0)
+    terms[parts] = route_ref[...]
+    second_ref[...] = jnp.zeros(second_ref.shape, F32)
+
+    def body(at, carry):
+        @pl.when(at < parts)
+        def _():
+            peer_copy(back_ref.at[1, at], arrived.at[at], peer_sems, at).wait_recv()
+            terms[at] = back_ref[0, at].astype(F32) + arrived[at].astype(F32)
+
+        line.step(at)
+        part = at - line.last
+
+        @pl.when((part >= 0) & (part < parts))
+        def _():
+            grad = line.total(part)
+            residual = res_ref[part]
+            scale = scale_of(residual)
+            unit = residual * scale
+            second_ref[...] += jnp.sum(grad * unit, axis=0, keepdims=True)
+            result = up_ref[part].astype(F32) + norm_back(grad, unit, scale, gain_ref[...])
+            grad_ref[part] = result
+            low_ref[part] = result.astype(BF)
+
+        return carry
+
+    lax.fori_loop(0, parts + 1 + line.last, body, 0)
+    route_out[...] = line.total(parts)
+    line.drain()
+
+    def wait(part, carry):
+        peer_copy(back_ref.at[1, part], arrived.at[part], peer_sems, part).wait_send()
+        return carry
+
+    lax.fori_loop(0, parts, wait, 0)
+
+
+def residual_gradient(back, route, residual, upstream, gain):
+    rows, width = upstream.shape
+    parts = rows // PART
+    grad, low, second, route = pl.pallas_call(
+        residual_grad_kernel,
+        out_shape=(
+            jax.ShapeDtypeStruct((parts, PART, width), F32),
+            jax.ShapeDtypeStruct((parts, PART, width), BF),
+            jax.ShapeDtypeStruct((1, width), F32),
+            jax.ShapeDtypeStruct(route.shape, F32),
+        ),
+        in_specs=[vmem_spec()] * 5,
+        out_specs=(vmem_spec(),) * 4,
+        scratch_shapes=line_scratch(parts + 1, width)
+        + [
+            pltpu.SemaphoreType.DMA((2, parts)),
+            pltpu.VMEM((parts, PART, width), BF),
+            pltpu.VMEM((parts + 1, PART, width), F32),
+        ],
+        compiler_params=pltpu.CompilerParams(
+            collective_id=1, has_side_effects=True, vmem_limit_bytes=48 * MIB
+        ),
+        name="residual_grad",
+    )(
+        back.reshape(2, parts, PART, width), route, residual, upstream.reshape(parts, PART, width), gain[None]
+    )
+    return grad, low.reshape(rows, width), second[0], route
+
+
+def input_grad_kernel(
+    part_ref, x_ref, res_grad_ref, gain_ref, grad_ref, first_ref, from_left, from_right, to_right, to_left, sems
+):
+    parts = part_ref.shape[0]
+    line = Line(parts, lambda at: part_ref[at], from_left, from_right, to_right, to_left, sems)
+    line.clear()
+    meet(line_partners())
+    first_ref[...] = jnp.zeros(first_ref.shape, F32)
+
+    def body(at, carry):
+        line.step(at)
+        part = at - line.last
+
+        @pl.when(part >= 0)
+        def _():
+            grad = line.total(part)
+            values = x_ref[part].astype(F32)
+            scale = scale_of(values)
+            unit = values * scale
+            first_ref[...] += jnp.sum(grad * unit, axis=0, keepdims=True)
+            grad_ref[part] = (res_grad_ref[part] + norm_back(grad, unit, scale, gain_ref[...])).astype(BF)
+
+        return carry
+
+    lax.fori_loop(0, parts + line.last, body, 0)
+    line.drain()
+
+
+def input_gradient(first_part, block_input, residual_grad, gain):
+    rows, width = block_input.shape
+    parts = rows // PART
+    grad, first = pl.pallas_call(
+        input_grad_kernel,
+        out_shape=(
+            jax.ShapeDtypeStruct((parts, PART, width), BF),
+            jax.ShapeDtypeStruct((1, width), F32),
+        ),
+        in_specs=[vmem_spec()] * 4,
+        out_specs=(vmem_spec(),) * 2,
+        scratch_shapes=line_scratch(parts, width),
+        compiler_params=pltpu.CompilerParams(
+            collective_id=2, has_side_effects=True, vmem_limit_bytes=40 * MIB
+        ),
+        name="input_grad",
+    )(first_part.reshape(parts, PART, width), block_input.reshape(parts, PART, width), residual_grad, gain[None])
+    return grad.reshape(rows, width), first[0]
+
+
 def swap(array, axis, bit):
     size = lax.axis_size(axis)
     return lax.ppermute(array, axis, [(at, at ^ bit) for at in range(size)])
@@ -825,11 +1117,7 @@
     keys, values = both[:, : local_kv * HEAD_SIZE], both[:, local_kv * HEAD_SIZE :]
 
     attended, lse, part = attend(scal, query_rot, keys, values, w_output)
-    residual = inputs + lax.psum(part, "tensor").astype(F32)
-    second_scale = norm_scale(residual)
-    second_unit = residual * second_scale
-    second_normed = (second_unit * second_gain).astype(BF)
-    normed_all = jnp.concatenate([second_normed, swap(second_normed, "expert", 1)], axis=0)
+    residual, normed_all = residual_norm(part, block_input, second_gain)
 
     away = jnp.stack([1 - core, side]).astype(jnp.int32)
     home = jnp.stack([core, side]).astype(jnp.int32)
@@ -854,14 +1142,10 @@
     mixed = lax.psum_scatter(mix, "tensor", scatter_dimension=1, tiled=True)
     mixed = mixed[:rows].astype(F32) + swap(mixed[rows:], "expert", 1).astype(F32)
     block_output = (
-        lax.dynamic_slice_in_dim(residual, feature_start, width // 4, 1) + mixed
+        lax.dynamic_slice_in_dim(residual.reshape(rows, width), feature_start, width // 4, 1) + mixed
     ).astype(BF)
 
-    own_back = (back[:rows].astype(F32) + swap(back[rows:], "expert", 1).astype(F32)).astype(BF)
-    second_grad = lax.psum(own_back, "tensor").astype(F32)
-    grad_second = jnp.sum(second_grad * second_unit, axis=0)
-    residual_grad = upstream.astype(F32) + norm_back(second_grad, second_unit, second_scale, second_gain)
-    residual_low = residual_grad.astype(BF)
+    residual_grad, residual_low, grad_second, route = residual_gradient(back, route, residual, upstream, second_gain)
 
     query_grad, dk, dv, grad_output = attend_back(
         scal, query_rot, keys, values, lse, attended, residual_low, w_output, cosines, sines
@@ -879,13 +1163,15 @@
     first_part = (
         matmul_nt(query_grad, w_query) + matmul_nt(key_grad, key_weight) + matmul_nt(value_grad, value_weight)
     )
-    first_grad = lax.psum(first_part.astype(BF), "tensor").astype(F32)
-    grad_first = jnp.sum(first_grad * first_unit, axis=0)
-    grad_input = (residual_grad + norm_back(first_grad, first_unit, first_scale, first_gain)).astype(BF)
-    dense = lax.psum((grad_query, grad_key, grad_value, grad_output, grad_first, grad_second), ("dp", "expert"))
-    grad_router = lax.psum(route, ("dp", "expert", "tensor")).T
+    grad_input, grad_first = input_gradient(first_part, block_input, residual_grad, first_gain)
+    early = lax.psum((grad_output.astype(BF), route.astype(BF), grad_second.astype(BF)), ("dp", "expert"))
+    late = lax.psum(
+        (grad_query.astype(BF), grad_key.astype(BF), grad_value.astype(BF), grad_first.astype(BF)), ("dp", "expert")
+    )
+    early = [item.astype(F32) for item in early]
+    late = [item.astype(F32) for item in late]
     return (
-        block_output, grad_input, dense[4], dense[0], dense[1], dense[2], dense[3], dense[5], grad_router,
+        block_output, grad_input, late[3], late[0], late[1], late[2], early[0], early[2], early[1].T,
         expert_sums[1], expert_sums[2], expert_sums[0],
     )
 

time: 630 us -> 550 us (0.87)
  waiting for transfers between devices: 379 us -> 106 us
  Pallas kernels: 95.7 us -> 301 us
    pallas_call x0 -> x3, Pallas kernels: none -> 205 us  [the longest x1 86 us: residual_gradient(): pl.pallas_call(residual_grad_kernel, out_shape=(jax.ShapeDtypeStruct((par...]
    psum x5 -> x1, waiting for transfers between devices: 203 us -> 0.01 us  [fast_device(): lax.psum((grad_query.astype(BF), grad_key.astype(BF), grad_value.astype(B...]
    ppermute x16 -> x14, waiting for transfers between devices: 176 us -> 106 us  [swap(): return lax.ppermute(array, axis, [(at, at ^ bit) for at in range(size)])]
    ppermute x16 -> x14, starting transfers between devices: 15.6 us -> 11.2 us  [swap(): return lax.ppermute(array, axis, [(at, at ^ bit) for at in range(size)])]
  transfers between devices with their start and end apart: 22 -> 16, of which waited for: 12 -> 3; matrix products, arithmetic and copies ran while one was open for 11% -> 14% of each run, Pallas kernels for 0% -> 49%
where the time goes in v2:
time: 550 us; the launch traced here: 544 us
  Pallas kernels  301 us (55%)
  waiting for transfers between devices  106 us (19%)
  other arithmetic  63.4 us (12%)
  local copies, waits for them, and re-layouts  17.4 us (3%)
  between operations  16.4 us (3%)
  blocking collectives  13.9 us (3%)
  matrix products  13.8 us (3%)
  starting transfers between devices  11.2 us (2%)
    ppermute x14, waiting for transfers between devices, swap(): return lax.ppermute(array, axis, [(at, at ^ bit) for at in range(size)])  106 us
    pallas_call x1, Pallas kernels, residual_gradient(): pl.pallas_call(residual_grad_kernel, out_shape=(jax.ShapeDtypeStruct((par...  86 us
    pallas_call x2, Pallas kernels, experts(): pl.pallas_call(functools.partial(expert_kernel, last), out_shape=out_shap...  77.2 us
    pallas_call x1, Pallas kernels, residual_norm(): pl.pallas_call(residual_kernel, out_shape=(jax.ShapeDtypeStruct((parts, P...  61.4 us
    pallas_call x1, Pallas kernels, input_gradient(): pl.pallas_call(input_grad_kernel, out_shape=(jax.ShapeDtypeStruct((parts,...  57.9 us
    convert_element_type x6, other arithmetic, fast_device(): (mine.astype(F32) + other.astype(F32)).astype(BF)  24.6 us
    convert_element_type x3, other arithmetic, fast_device(): jnp.where(core == 0, jnp.concatenate([mine, other], axis=0), jnp.concaten...  18.1 us
    psum x1, blocking collectives, fast_device(): lax.psum((grad_query.astype(BF), grad_key.astype(BF), grad_value.astype(B...  13.9 us
  transfers between devices with their start and end apart: 16, of which 3 were waited for; matrix products, arithmetic and copies ran while one was open for 14% of the time, Pallas kernels for 49%

profile of v2, /device:TPU:0, one launch (start us, length us, event | category | flops | bytes accessed | tf_op | source)
XLA Modules:
  0.0 543.5 jit_solution(4720991606251561383)
XLA Ops:
  10.8 3.0 collective-permute-start.2
  30.2 6.3 %attend.1 = (bf16[512,256]{1,0:T(8,128)(2,1)S(1)}, f32[512,128]{1,0:T(8,128)S(1)}, bf16[512,1024]{1,0:T(8,128)(2,1)S(1)}) custom-call(s32[3]{0:T(128)S(1)} %pad_add_fusion.scal_ref, bf16[512,256]{1,0:T(8,128)(2,1)S(1)} %copy.60.q_ref, bf16[1024,128]{1,0:T(8,128)(2,1)S(1)} %get-tuple-element.82.k_ref, bf16[1024,128]{1,0:T(8,128)(2,1)S(1)} %get-tuple-element.81.v_ref, ...), custom_call_target="tpu_custom_call" | custom-call | tf_op jit(solution)/shard_map/attend/pallas_call | solution.py:488
  36.6 61.4 %residual_norm.1 = (f32[16,32,1024]{2,1,0:T(8,128)S(1)}, bf16[2,16,32,1024]{3,2,1,0:T(8,128)(2,1)S(1)}) custom-call(bf16[16,32,1024]{2,1,0:T(8,128)(2,1)S(1)} %bitcast.42, bf16[16,32,1024]{2,1,0:T(8,128)(2,1)S(1)} %bitcast.35, f32[1,1024]{1,0:T(1,128)S(1)} %bitcast.43), custom_call_target="tpu_custom_call" | custom-call | tf_op jit(solution)/shard_map/residual_norm/pallas_call | solution.py:929
  102.8 37.7 %experts_first.1 = (bf16[8,1024,128]{2,1,0:T(8,128)(2,1)}, bf16[8,1024,128]{2,1,0:T(8,128)(2,1)}, bf16[8,128,1024]{2,1,0:T(8,128)(2,1)}, bf16[1024,1024]{1,0:T(8...) custom-call(s32[2]{0:T(128)} %get-tuple-element.90.refs_0_, ...), custom_call_target="tpu_custom_call" | custom-call | flops 19327352832 | bytes 29360128 | tf_op jit(solution)/shard_map/experts_first/pallas_call | solution.py:747
  141.1 39.5 %experts_last.1 = (bf16[8,1024,128]{2,1,0:T(8,128)(2,1)}, bf16[8,1024,128]{2,1,0:T(8,128)(2,1)}, bf16[8,128,1024]{2,1,0:T(8,128)(2,1)}, bf16[1024,1024]{1,0:T(8,...) custom-call(s32[2]{0:T(128)} %get-tuple-element.89.refs_0_, bf16[1024,1024]{1,0:T(8,128)(2,1)} %bitcast.47, ...), custom_call_target="tpu_custom_call" | custom-call | flops 19327352832 | bytes 29360128 | tf_op jit(solution)/shard_map/experts_last/pallas_call | solution.py:747
  181.6 86.0 %residual_grad.1 = (f32[16,32,1024]{2,1,0:T(8,128)S(1)}, bf16[16,32,1024]{2,1,0:T(8,128)(2,1)S(1)}, f32[1,1024]{1,0:T(1,128)S(1)}, f32[32,1024]{1,0:T(8,128)S(1)}) custom-call(bf16[2,16,32,1024]{3,2,1,0:T(8,128)(2,1)} %bitcast.48, f32[32,1024]{1,0:T(8,128)S(1)} %copy-done.13, f32[16,32,1024]{2,1,0:T(8,128)} %copy-done.3, bf16[16,32,1024]{2,1,0:T(8,128)(2,1)S(1)} %bitcast.38, ...), custom_call_target="tpu_custom_call" | custom-call | tf_op jit(solution)/shard_map/residual_grad/pallas_call | solution.py:999
  269.9 12.6 %attend_back.1 = (bf16[512,256]{1,0:T(8,128)(2,1)}, bf16[1024,128]{1,0:T(8,128)(2,1)}, bf16[1024,128]{1,0:T(8,128)(2,1)}, f32[256,1024]{1,0:T(8,128)}) custom-call(s32[3]{0:T(128)} %copy-done.16, bf16[512,256]{1,0:T(8,128)(2,1)} %copy-done.4, bf16[1024,128]{1,0:T(8,128)(2,1)} %copy-done.6, bf16[1024,128]{1,0:T(8,128)(2,1)} %copy-done.5, ...), custom_call_target="tpu_custom_call" | custom-call | tf_op jit(solution)/shard_map/attend_back/pallas_call | solution.py:556
  284.7 2.2 collective-permute-start.4
  289.5 4.1 add_convert_fusion.1
  294.6 3.8 add_convert_fusion.3
  299.5 3.9 add_convert_fusion.5
  308.1 34.5 %collective-permute-done.12 = bf16[8,128,1024]{2,1,0:T(8,128)(2,1)} collective-permute-done((bf16[8,128,1024]{2,1,0:T(8,128)(2,1)}, bf16[8,128,1024]{2,1,0:T(8,128)(2,1)}, u32[]{:S(2)}, u32[]{:S(2)}) %collective-permute-start.12) | collective-permute-done | bytes 2097184 | tf_op jit(solution)/shard_map/ppermute | solution.py:1075
  342.6 4.6 add_convert_fusion
  347.1 40.4 %collective-permute-done.9 = bf16[8,1024,128]{2,1,0:T(8,128)(2,1)} collective-permute-done((bf16[8,1024,128]{2,1,0:T(8,128)(2,1)}, bf16[8,1024,128]{2,1,0:T(8,128)(2,1)}, u32[]{:S(2)}, u32[]{:S(2)}) %collective-permute-start.9) | collective-permute-done | bytes 2097184 | tf_op jit(solution)/shard_map/ppermute | solution.py:1075
  387.5 4.1 add_convert_fusion.2
  391.6 30.9 %collective-permute-done.6 = bf16[8,1024,128]{2,1,0:T(8,128)(2,1)} collective-permute-done((bf16[8,1024,128]{2,1,0:T(8,128)(2,1)}, bf16[8,1024,128]{2,1,0:T(8,128)(2,1)}, u32[]{:S(2)}, u32[]{:S(2)}) %collective-permute-start.6) | collective-permute-done | bytes 2097184 | tf_op jit(solution)/shard_map/ppermute | solution.py:1075
  422.5 4.1 add_convert_fusion.4
  431.2 3.0 add_add_fusion
  434.2 57.9 %input_grad.1 = (bf16[16,32,1024]{2,1,0:T(8,128)(2,1)S(1)}, f32[1,1024]{1,0:T(1,128)S(1)}) custom-call(f32[16,32,1024]{2,1,0:T(8,128)S(1)} %bitcast.37, bf16[16,32,1024]{2,1,0:T(8,128)(2,1)S(1)} %bitcast.36, f32[16,32,1024]{2,1,0:T(8,128)S(1)} %copy-done.8, f32[1,1024]{1,0:T(1,128)S(1)} %bitcast.45), custom_call_target="tpu_custom_call" | custom-call | tf_op jit(solution)/shard_map/input_grad/pallas_call | solution.py:1056
  492.2 13.9 %all-reduce = (bf16[1024]{0:T(1024)(128)(2,1)S(1)}, bf16[1024]{0:T(1024)(128)(2,1)S(1)}) all-reduce(bf16[1024]{0:T(1024)(128)(2,1)S(1)} %convert_reduce_fusion.3, bf16[1024]{0:T(1024)(128)(2,1)S(1)} %convert_reduce_fusion.2), channel_id=1, replica_groups=mesh['dp'=4,'expert'=2,'tensor'=4] {'dp','expert'}, use_global_device_ids=true, to_apply=%region_4.5 | all-reduce | flops 2048 | bytes 8192 | tf_op jit(solution)/shard_map/psum | solution.py:1168
  508.9 2.1 convert_element_type.185
  516.6 6.0 %fusion.2 = f32[16,128,1024]{2,1,0:T(8,128)} fusion(bf16[8,128,1024]{2,1,0:T(8,128)(2,1)} %collective-permute-done.13, bf16[8,128,1024]{2,1,0:T(8,128)(2,1)} %add_convert_fusion, pred[]{:T(512)S(6)} %eq.23), kind=kLoop, calls=%fused_computation.5 | loop fusion | flops 8388608 | bytes 12582913 | tf_op jit(solution)/shard_map/convert_element_type | solution.py:1138
  522.5 6.1 %fusion.1 = f32[16,1024,128]{2,1,0:T(8,128)} fusion(bf16[8,1024,128]{2,1,0:T(8,128)(2,1)} %collective-permute-done.10, bf16[8,1024,128]{2,1,0:T(8,128)(2,1)} %add_convert_fusion.2, pred[]{:T(512)S(6)} %eq.23), kind=kLoop, calls=%fused_computation.3 | loop fusion | flops 8388608 | bytes 12582913 | tf_op jit(solution)/shard_map/convert_element_type | solution.py:1138
  528.6 6.0 %fusion = f32[16,1024,128]{2,1,0:T(8,128)} fusion(bf16[8,1024,128]{2,1,0:T(8,128)(2,1)} %collective-permute-done.7, bf16[8,1024,128]{2,1,0:T(8,128)(2,1)} %add_convert_fusion.4, pred[]{:T(512)S(6)} %eq.23), kind=kLoop, calls=%fused_computation.1 | loop fusion | flops 8388608 | bytes 12582913 | tf_op jit(solution)/shard_map/convert_element_type | solution.py:1138
  (152 shorter events, 52.9 us)
Async XLA Ops:
  8.0 13.0 %copy-start = (bf16[1024,256]{1,0:T(8,128)(2,1)S(1)}, bf16[1024,256]{1,0:T(8,128)(2,1)}, u32[]{:S(2)}) copy-start(bf16[1024,256]{1,0:T(8,128)(2,1)} %param.17) | copy-start | bytes 1572868
  8.0 421.8 %reduce-scatter.2.cloned.1.call-start = ((), (), s32[]{:S(2)}) async-start(), calls=%async_computation.1 | async-start | bytes 2621440 | tf_op jit(solution)/shard_map/reduce_scatter | solution.py:1142
  8.8 8.3 %copy-start.1 = (bf16[512,1024]{1,0:T(8,128)(2,1)S(1)}, bf16[512,1024]{1,0:T(8,128)(2,1)}, u32[]{:S(2)}) copy-start(bf16[512,1024]{1,0:T(8,128)(2,1)} %param.15) | copy-start | bytes 3145732
  8.8 8.3 %copy-start.15 = (f32[1024]{0:T(1024)S(1)}, f32[1024]{0:T(1024)}, u32[]{:S(2)}) copy-start(f32[1024]{0:T(1024)} %param.16) | copy-start | bytes 12292
  8.8 8.3 %copy-start.25 = (bf16[1024,128]{1,0:T(8,128)(2,1)S(1)}, bf16[1024,128]{1,0:T(8,128)(2,1)}, u32[]{:S(2)}) copy-start(bf16[1024,128]{1,0:T(8,128)(2,1)} %param.18) | copy-start | bytes 786436
  10.8 16.1 %collective-permute-start.2 = (bf16[512,64]{1,0:T(8,128)(2,1)}, bf16[512,64]{1,0:T(8,128)(2,1)}, u32[]{:S(2)}, u32[]{:S(2)}) collective-permute-start(bf16[512,64]{1,0:T(8,128)(2,1)} %pad_maximum_fusion.4), channel_id=1, source_target_pairs={{0,4},{4,0},{1,5},{5,1},{2,6},{6,2},{3,7},{7,3},{8,12},{12,8},{9,1... | collective-permute-start | bytes 196616 | tf_op jit(solution)/shard_map/ppermute | solution.py:1075
  19.0 10.1 %collective-permute-start = (bf16[512,256]{1,0:T(8,128)(2,1)}, bf16[512,256]{1,0:T(8,128)(2,1)}, u32[]{:S(2)}, u32[]{:S(2)}) collective-permute-start(bf16[512,256]{1,0:T(8,128)(2,1)} %pad_maximum_fusion.2), channel_id=1, source_target_pairs={{0,4},{4,0},{1,5},{5,1},{2,6},{6,2},{3,7},{7,3},{8,12},{12,8},{9,1... | collective-permute-start | bytes 786440 | tf_op jit(solution)/shard_map/ppermute | solution.py:1075
  19.0 80.4 %collective-permute-start.1 = (bf16[512,1024]{1,0:T(8,128)(2,1)S(1)}, bf16[512,1024]{1,0:T(8,128)(2,1)}, u32[]{:S(2)}, u32[]{:S(2)}) collective-permute-start(bf16[512,1024]{1,0:T(8,128)(2,1)S(1)} %copy-done.2), channel_id=1, source_target_pairs={{0,4},{4,0},{1,5},{5,1},{2,6},{6,2},{3,7},{7,3},{8,12},{12,8},{9,1... | collective-permute-start | bytes 3145736 | tf_op jit(solution)/shard_map/ppermute | solution.py:1075
  30.2 71.3 %copy-start.5 = (bf16[1024,128]{1,0:T(8,128)(2,1)}, bf16[1024,128]{1,0:T(8,128)(2,1)S(1)}, u32[]{:S(2)}) copy-start(bf16[1024,128]{1,0:T(8,128)(2,1)S(1)} %get-tuple-element.81.v_ref) | copy-start | bytes 786436
  30.2 71.3 %copy-start.6 = (bf16[1024,128]{1,0:T(8,128)(2,1)}, bf16[1024,128]{1,0:T(8,128)(2,1)S(1)}, u32[]{:S(2)}) copy-start(bf16[1024,128]{1,0:T(8,128)(2,1)S(1)} %get-tuple-element.82.k_ref) | copy-start | bytes 786436
  36.6 64.9 %copy-start.11 = (bf16[512,256]{1,0:T(8,128)(2,1)}, bf16[512,256]{1,0:T(8,128)(2,1)S(1)}, u32[]{:S(2)}) copy-start(bf16[512,256]{1,0:T(8,128)(2,1)S(1)} %get-tuple-element.49.att_ref) | copy-start | bytes 786436
  36.6 64.9 %copy-start.12 = (f32[512,128]{1,0:T(8,128)}, f32[512,128]{1,0:T(8,128)S(1)}, u32[]{:S(2)}) copy-start(f32[512,128]{1,0:T(8,128)S(1)} %get-tuple-element.48.lse_ref) | copy-start | bytes 786436
  140.4 159.1 %collective-permute-start.5 = (bf16[8,1024,128]{2,1,0:T(8,128)(2,1)}, bf16[8,1024,128]{2,1,0:T(8,128)(2,1)}, u32[]{:S(2)}, u32[]{:S(2)}) collective-permute-start(bf16[8,1024,128]{2,1,0:T(8,128)(2,1)} %get-tuple-element.63), channel_id=1, source_target_pairs={{0,8},{8,0},{16,24},{24,16},{1,9},{9,1},{17,25},{25,17},{2,10},{10... | collective-permute-start | bytes 6291464 | tf_op jit(solution)/shard_map/ppermute | solution.py:1075
  140.5 154.1 %collective-permute-start.8 = (bf16[8,1024,128]{2,1,0:T(8,128)(2,1)}, bf16[8,1024,128]{2,1,0:T(8,128)(2,1)}, u32[]{:S(2)}, u32[]{:S(2)}) collective-permute-start(bf16[8,1024,128]{2,1,0:T(8,128)(2,1)} %get-tuple-element.65), channel_id=1, source_target_pairs={{0,8},{8,0},{16,24},{24,16},{1,9},{9,1},{17,25},{25,17},{2,10},{10... | collective-permute-start | bytes 6291464 | tf_op jit(solution)/shard_map/ppermute | solution.py:1075
  141.0 148.5 %collective-permute-start.11 = (bf16[8,128,1024]{2,1,0:T(8,128)(2,1)}, bf16[8,128,1024]{2,1,0:T(8,128)(2,1)}, u32[]{:S(2)}, u32[]{:S(2)}) collective-permute-start(bf16[8,128,1024]{2,1,0:T(8,128)(2,1)} %get-tuple-element.67), channel_id=1, source_target_pairs={{0,8},{8,0},{16,24},{24,16},{1,9},{9,1},{17,25},{25,17},{2,10},{10... | collective-permute-start | bytes 6291464 | tf_op jit(solution)/shard_map/ppermute | solution.py:1075
  180.7 326.6 %all-reduce.4.cloned.1.call-start = ((), (), s32[]{:S(2)}) async-start(), calls=%async_computation.2 | async-start | bytes 3276800 | tf_op jit(solution)/shard_map/psum | solution.py:1168
  284.7 21.8 %collective-permute-start.4 = (bf16[512,256]{1,0:T(8,128)(2,1)S(1)}, bf16[512,256]{1,0:T(8,128)(2,1)S(1)}, u32[]{:S(2)}, u32[]{:S(2)}) collective-permute-start(bf16[512,256]{1,0:T(8,128)(2,1)S(1)} %slice.76), channel_id=1, source_target_pairs={{0,4},{4,0},{1,5},{5,1},{2,6},{6,2},{3,7},{7,3},{8,12},{12,8},{9,1... | collective-permute-start | bytes 786440 | tf_op jit(solution)/shard_map/ppermute | solution.py:1075
  293.7 48.9 %collective-permute-start.12 = (bf16[8,128,1024]{2,1,0:T(8,128)(2,1)}, bf16[8,128,1024]{2,1,0:T(8,128)(2,1)}, u32[]{:S(2)}, u32[]{:S(2)}) collective-permute-start(bf16[8,128,1024]{2,1,0:T(8,128)(2,1)} %add_convert_fusion.1), channel_id=1, source_target_pairs={{0,16},{8,24},{16,0},{24,8},{1,17},{9,25},{17,1},{25,9},{2,18},{10... | collective-permute-start | bytes 6291464 | tf_op jit(solution)/shard_map/ppermute | solution.py:1075
  298.4 89.1 %collective-permute-start.9 = (bf16[8,1024,128]{2,1,0:T(8,128)(2,1)}, bf16[8,1024,128]{2,1,0:T(8,128)(2,1)}, u32[]{:S(2)}, u32[]{:S(2)}) collective-permute-start(bf16[8,1024,128]{2,1,0:T(8,128)(2,1)} %add_convert_fusion.3), channel_id=1, source_target_pairs={{0,16},{8,24},{16,0},{24,8},{1,17},{9,25},{17,1},{25,9},{2,18},{10... | collective-permute-start | bytes 6291464 | tf_op jit(solution)/shard_map/ppermute | solution.py:1075
  303.4 119.1 %collective-permute-start.6 = (bf16[8,1024,128]{2,1,0:T(8,128)(2,1)}, bf16[8,1024,128]{2,1,0:T(8,128)(2,1)}, u32[]{:S(2)}, u32[]{:S(2)}) collective-permute-start(bf16[8,1024,128]{2,1,0:T(8,128)(2,1)} %add_convert_fusion.5), channel_id=1, source_target_pairs={{0,16},{8,24},{16,0},{24,8},{1,17},{9,25},{17,1},{25,9},{2,18},{10... | collective-permute-start | bytes 6291464 | tf_op jit(solution)/shard_map/ppermute | solution.py:1075
  347.1 169.4 %collective-permute-start.13 = (bf16[8,128,1024]{2,1,0:T(8,128)(2,1)}, bf16[8,128,1024]{2,1,0:T(8,128)(2,1)}, u32[]{:S(2)}, u32[]{:S(2)}) collective-permute-start(bf16[8,128,1024]{2,1,0:T(8,128)(2,1)} %add_convert_fusion), channel_id=1, source_target_pairs={{0,8},{8,0},{16,24},{24,16},{1,9},{9,1},{17,25},{25,17},{2,10},{10... | collective-permute-start | bytes 6291464 | tf_op jit(solution)/shard_map/ppermute | solution.py:1075
  391.6 131.0 %collective-permute-start.10 = (bf16[8,1024,128]{2,1,0:T(8,128)(2,1)}, bf16[8,1024,128]{2,1,0:T(8,128)(2,1)}, u32[]{:S(2)}, u32[]{:S(2)}) collective-permute-start(bf16[8,1024,128]{2,1,0:T(8,128)(2,1)} %add_convert_fusion.2), channel_id=1, source_target_pairs={{0,8},{8,0},{16,24},{24,16},{1,9},{9,1},{17,25},{25,17},{2,10},{10... | collective-permute-start | bytes 6291464 | tf_op jit(solution)/shard_map/ppermute | solution.py:1075
  426.6 102.0 %collective-permute-start.7 = (bf16[8,1024,128]{2,1,0:T(8,128)(2,1)}, bf16[8,1024,128]{2,1,0:T(8,128)(2,1)}, u32[]{:S(2)}, u32[]{:S(2)}) collective-permute-start(bf16[8,1024,128]{2,1,0:T(8,128)(2,1)} %add_convert_fusion.4), channel_id=1, source_target_pairs={{0,8},{8,0},{16,24},{24,16},{1,9},{9,1},{17,25},{25,17},{2,10},{10... | collective-permute-start | bytes 6291464 | tf_op jit(solution)/shard_map/ppermute | solution.py:1075
  430.8 83.9 %collective-permute-start.3 = (bf16[512,256]{1,0:T(8,128)(2,1)S(1)}, bf16[512,256]{1,0:T(8,128)(2,1)S(1)}, u32[]{:S(2)}, u32[]{:S(2)}) collective-permute-start(bf16[512,256]{1,0:T(8,128)(2,1)S(1)} %slice.74), channel_id=1, source_target_pairs={{0,4},{4,0},{1,5},{5,1},{2,6},{6,2},{3,7},{7,3},{8,12},{12,8},{9,1... | collective-permute-start | bytes 786440 | tf_op jit(solution)/shard_map/ppermute | solution.py:1075
  (24 other events, 81.2 us)
Sparse Core Ops, SparseCore 0:
  180.8 54.4 reduce-scatter.1
Sparse Core Ops, SparseCore 1:
  428.1 59.9 all-reduce.3

commit v3 on v2

--- a/solution.py
+++ b/solution.py
@@ -568,32 +568,339 @@
     )(scal, query, key, value, lse, attended, low, w_output, cosines, sines)
 
 
-CHUNK = 256
+MESH = pl.DeviceIdType.MESH
+PART = 32
+LAG = 3
+LINK_COST = pl.CostEstimate(flops=4 * 10**10, bytes_accessed=10**7, transcendentals=0)
+
+
+def meet(partners):
+    barrier = pltpu.get_barrier_semaphore()
+    count = 0
+    for here, device in partners:
+        here = jnp.asarray(here)
+
+        @pl.when(here)
+        def _():
+            pl.semaphore_signal(barrier, inc=1, device_id=device, device_id_type=MESH)
+
+        count = count + here.astype(jnp.int32)
+    pl.semaphore_wait(barrier, count)
+
+
+def line_partners():
+    place = lax.axis_index("tensor")
+    last = lax.axis_size("tensor") - 1
+    return [(place > 0, {"tensor": place - 1}), (place < last, {"tensor": place + 1})]
+
+
+class Line:
+    def __init__(self, parts, term, from_left, from_right, to_right, to_left, sems):
+        self.place = lax.axis_index("tensor")
+        self.last = lax.axis_size("tensor") - 1
+        self.parts = parts
+        self.term = term
+        self.from_left, self.from_right = from_left, from_right
+        self.to_right, self.to_left = to_right, to_left
+        self.sems = sems
+
+    def copy(self, way, at):
+        near = jnp.where(self.place < self.last, self.place + 1, self.place - 1)
+        far = jnp.where(self.place > 0, self.place - 1, self.place + 1)
+        source, target, device = (
+            (self.to_right, self.from_left, near) if way == 0 else (self.to_left, self.from_right, far)
+        )
+        return pltpu.make_async_remote_copy(
+            src_ref=source.at[at],
+            dst_ref=target.at[at],
+            send_sem=self.sems.at[2 * way, at],
+            recv_sem=self.sems.at[2 * way + 1, at],
+            device_id={"tensor": device},
+            device_id_type=MESH,
+        )
+
+    def clear(self):
+        @pl.when(self.place == 0)
+        def _():
+            self.from_left[...] = jnp.zeros(self.from_left.shape, self.from_left.dtype)
+
+        @pl.when(self.place == self.last)
+        def _():
+            self.from_right[...] = jnp.zeros(self.from_right.shape, self.from_right.dtype)
+
+    def step(self, at):
+        for way in range(2):
+            part = at - LAG * (self.place if way == 0 else self.last - self.place)
+            has_source = self.place > 0 if way == 0 else self.place < self.last
+            has_target = self.place < self.last if way == 0 else self.place > 0
+            arrived = self.from_left if way == 0 else self.from_right
+            leaving = self.to_right if way == 0 else self.to_left
+            valid = (part >= 0) & (part < self.parts)
+
+            @pl.when(valid & has_source)
+            def _():
+                self.copy(way, part).wait_recv()
+
+            @pl.when(valid & has_target)
+            def _():
+                leaving[part] = (self.term(part) + arrived[part].astype(F32)).astype(BF)
+                self.copy(way, part).start()
+
+    def total(self, part):
+        return self.term(part) + self.from_left[part].astype(F32) + self.from_right[part].astype(F32)
+
+    def drain(self):
+        def wait(part, carry):
+            @pl.when(self.place < self.last)
+            def _():
+                self.copy(0, part).wait_send()
+
+            @pl.when(self.place > 0)
+            def _():
+                self.copy(1, part).wait_send()
+
+            return carry
+
+        lax.fori_loop(0, self.parts, wait, 0)
+
+
+def line_scratch(parts, width):
+    return [pltpu.VMEM((parts, PART, width), BF)] * 4 + [pltpu.SemaphoreType.DMA((4, parts))]
+
+
+def peer_copy(source, target, sems, at):
+    return pltpu.make_async_remote_copy(
+        src_ref=source,
+        dst_ref=target,
+        send_sem=sems.at[0, at],
+        recv_sem=sems.at[1, at],
+        device_id={"expert": 1 - lax.axis_index("expert")},
+        device_id_type=MESH,
+    )
+
+
+def scale_of(values):
+    return lax.rsqrt(jnp.mean(values * values, axis=-1, keepdims=True) + epsilon)
+
+
+def residual_kernel(
+    part_ref, x_ref, gain_ref, res_ref, n_ref, from_left, from_right, to_right, to_left, sems, peer_sems
+):
+    parts = part_ref.shape[0]
+    line = Line(parts, lambda at: part_ref[at].astype(F32), from_left, from_right, to_right, to_left, sems)
+    line.clear()
+    meet(line_partners() + [(True, {"expert": 1 - lax.axis_index("expert")})])
+
+    def body(at, carry):
+        line.step(at)
+        part = at - LAG * line.last
+
+        @pl.when(part >= 0)
+        def _():
+            residual = x_ref[part].astype(F32) + line.total(part)
+            res_ref[part] = residual
+            unit = residual * scale_of(residual)
+            n_ref[0, part] = (unit * gain_ref[...]).astype(BF)
+            peer_copy(n_ref.at[0, part], n_ref.at[1, part], peer_sems, part).start()
+
+        return carry
+
+    lax.fori_loop(0, parts + LAG * line.last, body, 0)
+    line.drain()
+
+    def wait(part, carry):
+        peer_copy(n_ref.at[0, part], n_ref.at[1, part], peer_sems, part).wait()
+        return carry
+
+    lax.fori_loop(0, parts, wait, 0)
+
+
+def residual_norm(part, block_input, gain):
+    rows, width = block_input.shape
+    parts = rows // PART
+    residual, normed = pl.pallas_call(
+        residual_kernel,
+        out_shape=(
+            jax.ShapeDtypeStruct((parts, PART, width), F32),
+            jax.ShapeDtypeStruct((2, parts, PART, width), BF),
+        ),
+        in_specs=[vmem_spec()] * 3,
+        out_specs=(vmem_spec(),) * 2,
+        scratch_shapes=line_scratch(parts, width) + [pltpu.SemaphoreType.DMA((2, parts))],
+        compiler_params=pltpu.CompilerParams(
+            collective_id=0, has_side_effects=True, vmem_limit_bytes=40 * MIB
+        ),
+        cost_estimate=LINK_COST,
+        name="residual_norm",
+    )(part.reshape(parts, PART, width), block_input.reshape(parts, PART, width), gain[None])
+    return residual, normed.reshape(2 * rows, width)
+
+
+def residual_grad_kernel(
+    back_ref, route_ref, res_ref, up_ref, gain_ref, grad_ref, low_ref, second_ref, route_out,
+    from_left, from_right, to_right, to_left, sems, peer_sems, arrived, terms,
+):
+    parts = back_ref.shape[1]
+    line = Line(parts + 1, lambda at: terms[at], from_left, from_right, to_right, to_left, sems)
+    line.clear()
+    meet(line_partners() + [(True, {"expert": 1 - lax.axis_index("expert")})])
+
+    def send(part, carry):
+        peer_copy(back_ref.at[1, part], arrived.at[part], peer_sems, part).start()
+        return carry
+
+    lax.fori_loop(0, parts, send, 0)
+    terms[parts] = route_ref[...]
+    second_ref[...] = jnp.zeros(second_ref.shape, F32)
+
+    def body(at, carry):
+        @pl.when(at < parts)
+        def _():
+            peer_copy(back_ref.at[1, at], arrived.at[at], peer_sems, at).wait_recv()
+            terms[at] = back_ref[0, at].astype(F32) + arrived[at].astype(F32)
+
+        line.step(at)
+        part = at - LAG * line.last
+
+        @pl.when((part >= 0) & (part < parts))
+        def _():
+            grad = line.total(part)
+            residual = res_ref[part]
+            scale = scale_of(residual)
+            unit = residual * scale
+            second_ref[...] += jnp.sum(grad * unit, axis=0, keepdims=True)
+            result = up_ref[part].astype(F32) + norm_back(grad, unit, scale, gain_ref[...])
+            grad_ref[part] = result
+            low_ref[part] = result.astype(BF)
+
+        return carry
+
+    lax.fori_loop(0, parts + 1 + LAG * line.last, body, 0)
+    route_out[...] = line.total(parts)
+    line.drain()
+
+    def wait(part, carry):
+        peer_copy(back_ref.at[1, part], arrived.at[part], peer_sems, part).wait_send()
+        return carry
+
+    lax.fori_loop(0, parts, wait, 0)
+
+
+def residual_gradient(back, route, residual, upstream, gain):
+    rows, width = upstream.shape
+    parts = rows // PART
+    grad, low, second, route = pl.pallas_call(
+        residual_grad_kernel,
+        out_shape=(
+            jax.ShapeDtypeStruct((parts, PART, width), F32),
+            jax.ShapeDtypeStruct((parts, PART, width), BF),
+            jax.ShapeDtypeStruct((1, width), F32),
+            jax.ShapeDtypeStruct(route.shape, F32),
+        ),
+        in_specs=[vmem_spec()] * 5,
+        out_specs=(vmem_spec(),) * 4,
+        scratch_shapes=line_scratch(parts + 1, width)
+        + [
+            pltpu.SemaphoreType.DMA((2, parts)),
+            pltpu.VMEM((parts, PART, width), BF),
+            pltpu.VMEM((parts + 1, PART, width), F32),
+        ],
+        compiler_params=pltpu.CompilerParams(
+            collective_id=1, has_side_effects=True, vmem_limit_bytes=48 * MIB
+        ),
+        cost_estimate=LINK_COST,
+        name="residual_grad",
+    )(
+        back.reshape(2, parts, PART, width), route, residual, upstream.reshape(parts, PART, width), gain[None]
+    )
+    return grad, low.reshape(rows, width), second[0], route
+
+
+def input_grad_kernel(
+    part_ref, x_ref, res_grad_ref, gain_ref, grad_ref, first_ref, from_left, from_right, to_right, to_left, sems
+):
+    parts = part_ref.shape[0]
+    line = Line(parts, lambda at: part_ref[at], from_left, from_right, to_right, to_left, sems)
+    line.clear()
+    meet(line_partners())
+    first_ref[...] = jnp.zeros(first_ref.shape, F32)
+
+    def body(at, carry):
+        line.step(at)
+        part = at - LAG * line.last
+
+        @pl.when(part >= 0)
+        def _():
+            grad = line.total(part)
+            values = x_ref[part].astype(F32)
+            scale = scale_of(values)
+            unit = values * scale
+            first_ref[...] += jnp.sum(grad * unit, axis=0, keepdims=True)
+            grad_ref[part] = (res_grad_ref[part] + norm_back(grad, unit, scale, gain_ref[...])).astype(BF)
+
+        return carry
+
+    lax.fori_loop(0, parts + LAG * line.last, body, 0)
+    line.drain()
+
+
+def input_gradient(first_part, block_input, residual_grad, gain):
+    rows, width = block_input.shape
+    parts = rows // PART
+    grad, first = pl.pallas_call(
+        input_grad_kernel,
+        out_shape=(
+            jax.ShapeDtypeStruct((parts, PART, width), BF),
+            jax.ShapeDtypeStruct((1, width), F32),
+        ),
+        in_specs=[vmem_spec()] * 4,
+        out_specs=(vmem_spec(),) * 2,
+        scratch_shapes=line_scratch(parts, width),
+        compiler_params=pltpu.CompilerParams(
+            collective_id=2, has_side_effects=True, vmem_limit_bytes=40 * MIB
+        ),
+        cost_estimate=LINK_COST,
+        name="input_grad",
+    )(first_part.reshape(parts, PART, width), block_input.reshape(parts, PART, width), residual_grad, gain[None])
+    return grad.reshape(rows, width), first[0]
+
+
+CHUNK = 512
 GROUP = 4
 
 
-def expert_kernel(last, *refs):
-    if last:
-        (
-            scal_ref, n_ref, nt_ref, g_ref, chosen_ref, kept_ref, wr_ref, wg_ref, wu_ref, wd_ref, mix_in, back_in, gg_in,
-            dwg_ref, dwu_ref, dwd_ref, mix_ref, back_ref, route_ref,
-            gates, kept_gates, gate_grads, mix, back, wgs, wus, ghs, ght, dgs, dus,
-        ) = refs
-    else:
-        (
-            scal_ref, n_ref, g_ref, chosen_ref, kept_ref, wr_ref, wg_ref, wu_ref, wd_ref,
-            dwg_ref, dwu_ref, dwd_ref, mix_ref, back_ref, gg_ref, nt_ref,
-            gates, kept_gates, gate_grads, mix, back, wgs, wus, ghs, ght, dgs, dus,
-        ) = refs
+def expert_kernel(
+    n_ref, g_ref, chosen_ref, kept_ref, wr_ref, wg_ref, wu_ref, wd_ref,
+    dwg_ref, dwu_ref, dwd_ref, mix_ref, back_ref, route_ref,
+    gates, kept_gates, gate_grads, mix, back, nt, wgs, wus, ght, dgs, dus,
+    out_g, out_u, out_d, in_g, in_u, in_d, sems,
+):
     step = pl.program_id(0)
+    steps = pl.num_programs(0) // 2
+    side = lax.axis_index("expert")
+    dp = lax.axis_index("dp")
+    core = lax.rem(dp, 2)
+    other = {"dp": dp + 1 - 2 * core}
     tokens, width = n_ref.shape
     experts_all = wr_ref.shape[1]
     group, _, hid = wg_ref.shape
     chunks = tokens // CHUNK
     lane = lax.broadcasted_iota(jnp.int32, (1, experts_all), 1)
 
+    def copies(slot):
+        return [
+            pltpu.make_async_remote_copy(
+                src_ref=source.at[slot], dst_ref=target.at[slot],
+                send_sem=sems.at[0, kind, slot], recv_sem=sems.at[1, kind, slot],
+                device_id=other, device_id_type=MESH,
+            )
+            for kind, (source, target) in enumerate(((out_g, in_g), (out_u, in_u), (out_d, in_d)))
+        ]
+
     @pl.when(step == 0)
     def _():
+        meet([(True, other)])
+
         def start(at, carry):
             rows = pl.ds(pl.multiple_of(at * CHUNK, CHUNK), CHUNK)
             chosen = chosen_ref[rows, :] > 0.0
@@ -603,28 +910,24 @@
             gate = raised / jnp.sum(raised, axis=1, keepdims=True)
             gates[rows, :] = gate
             kept_gates[rows, :] = gate * kept_ref[rows, :]
-            if last:
-                mix[rows, :] = mix_in[rows, :].astype(F32)
-                back[rows, :] = back_in[rows, :].astype(F32)
-                gate_grads[rows, :] = gg_in[rows, :]
-            else:
-                mix[rows, :] = jnp.zeros((CHUNK, width), F32)
-                back[rows, :] = jnp.zeros((CHUNK, width), F32)
-                gate_grads[rows, :] = jnp.zeros((CHUNK, experts_all), F32)
+            mix[rows, :] = jnp.zeros((CHUNK, width), F32)
+            back[rows, :] = jnp.zeros((CHUNK, width), F32)
+            gate_grads[rows, :] = jnp.zeros((CHUNK, experts_all), F32)
             return carry
 
         lax.fori_loop(0, chunks, start, 0)
-        if not last:
-            for at in range(chunks):
-                nt_ref[:, at * CHUNK : (at + 1) * CHUNK] = n_ref[at * CHUNK : (at + 1) * CHUNK, :].T
+        for at in range(chunks):
+            nt[:, at * CHUNK : (at + 1) * CHUNK] = n_ref[at * CHUNK : (at + 1) * CHUNK, :].T
 
     for expert in range(group):
         wgs[:, expert * hid : (expert + 1) * hid] = wg_ref[expert]
         wus[:, expert * hid : (expert + 1) * hid] = wu_ref[expert]
-    column = scal_ref[1] * (experts_all // 2) + scal_ref[0] * (experts_all // 4) + step * group
-
-    def forward(at, carry):
-        rows = pl.ds(pl.multiple_of(at * CHUNK, CHUNK), CHUNK)
+    first = step < steps
+    block = jnp.where(first, (1 - core) * steps + step, core * steps + step - steps)
+    column = side * (experts_all // 2) + block * group
+
+    for at in range(chunks):
+        rows = slice(at * CHUNK, (at + 1) * CHUNK)
         token = n_ref[rows, :]
         down = wd_ref[...].reshape(group * hid, width)
         gate_in = matmul(token, wgs[...])
@@ -649,425 +952,175 @@
         pulled = pulled * weight
         up_grad = (pulled * silu).astype(BF)
         gate_grad = (pulled * up_in * (sig + silu * (1.0 - sig))).astype(BF)
-        ghs[rows, :] = gated
+        ght[:, rows] = gated.T
         dgs[rows, :] = gate_grad
         dus[rows, :] = up_grad
         mix[rows, :] += matmul(gated, down)
         back[rows, :] += matmul_nt(gate_grad, wgs[...]) + matmul_nt(up_grad, wus[...])
-        return carry
-
-    lax.fori_loop(0, chunks, forward, 0)
-    for at in range(chunks):
-        ght[:, at * CHUNK : (at + 1) * CHUNK] = ghs[at * CHUNK : (at + 1) * CHUNK, :].T
-
-    def weights_grad(at, carry):
-        rows = pl.ds(pl.multiple_of(at * CHUNK, CHUNK), CHUNK)
-        turned = nt_ref[rows, :]
-        gate_part = matmul(turned, dgs[...]).astype(BF)
-        up_part = matmul(turned, dus[...]).astype(BF)
+
+    def weight_grads(store_rows, store_down):
+        for at in range(width // CHUNK):
+            rows = slice(at * CHUNK, (at + 1) * CHUNK)
+            turned = nt[rows, :]
+            gate_part = matmul(turned, dgs[...])
+            up_part = matmul(turned, dus[...])
+            for expert in range(group):
+                inner = slice(expert * hid, (expert + 1) * hid)
+                store_rows(expert, rows, gate_part[:, inner], up_part[:, inner])
+        down_part = matmul(ght[...], g_ref[...])
         for expert in range(group):
-            dwg_ref[expert, rows, :] = gate_part[:, expert * hid : (expert + 1) * hid]
-            dwu_ref[expert, rows, :] = up_part[:, expert * hid : (expert + 1) * hid]
-        return carry
-
-    lax.fori_loop(0, width // CHUNK, weights_grad, 0)
-    for at in range(group * hid // CHUNK):
-        part = matmul(ght[at * CHUNK : (at + 1) * CHUNK, :], g_ref[...]).astype(BF)
-        for inner in range(CHUNK // hid):
-            dwd_ref[at * (CHUNK // hid) + inner] = part[inner * hid : (inner + 1) * hid, :]
-
-    @pl.when(step == pl.num_programs(0) - 1)
+            store_down(expert, down_part[expert * hid : (expert + 1) * hid, :])
+
+    @pl.when(first)
     def _():
-        if last:
-            route_ref[...] = jnp.zeros(route_ref.shape, F32)
+        def store_rows(expert, rows, gate_part, up_part):
+            out_g[step, expert, rows, :] = gate_part.astype(BF)
+            out_u[step, expert, rows, :] = up_part.astype(BF)
+
+        def store_down(expert, part):
+            out_d[step, expert] = part.astype(BF)
+
+        weight_grads(store_rows, store_down)
+        for copy in copies(step):
+            copy.start()
+
+    @pl.when(step >= steps)
+    def _():
+        slot = step - steps
+        for copy in copies(slot):
+            copy.wait_recv()
+
+        def store_rows(expert, rows, gate_part, up_part):
+            dwg_ref[expert, rows, :] = (gate_part + in_g[slot, expert, rows, :].astype(F32)).astype(BF)
+            dwu_ref[expert, rows, :] = (up_part + in_u[slot, expert, rows, :].astype(F32)).astype(BF)
+
+        def store_down(expert, part):
+            dwd_ref[expert] = (part + in_d[slot, expert].astype(F32)).astype(BF)
+
+        weight_grads(store_rows, store_down)
+        for copy in copies(slot):
+            copy.wait_send()
+
+    @pl.when(step == 2 * steps - 1)
+    def _():
+        route_ref[...] = jnp.zeros(route_ref.shape, F32)
 
         def finish(at, carry):
             rows = pl.ds(pl.multiple_of(at * CHUNK, CHUNK), CHUNK)
             mix_ref[rows, :] = mix[rows, :].astype(BF)
-            if last:
-                grads = gate_grads[rows, :] * kept_gates[rows, :]
-                chosen_grad = grads - gates[rows, :] * jnp.sum(grads, axis=1, keepdims=True)
-                low = chosen_grad.astype(BF)
-                back_ref[rows, :] = (back[rows, :] + matmul_nt(low, wr_ref[...])).astype(BF)
-                route_ref[...] += matmul_tn(low, n_ref[rows, :])
-            else:
-                back_ref[rows, :] = back[rows, :].astype(BF)
-                gg_ref[rows, :] = gate_grads[rows, :]
+            grads = gate_grads[rows, :] * kept_gates[rows, :]
+            chosen_grad = grads - gates[rows, :] * jnp.sum(grads, axis=1, keepdims=True)
+            low = chosen_grad.astype(BF)
+            back_ref[rows, :] = (back[rows, :] + matmul_nt(low, wr_ref[...])).astype(BF)
+            route_ref[...] += matmul_tn(low, n_ref[rows, :])
             return carry
 
         lax.fori_loop(0, chunks, finish, 0)
 
 
-def experts(last, scal, normed, turned, upstream, chosen, kept, w_router, w_gate, w_up, w_down, mix, back, gate_grads):
+def experts(normed, upstream, chosen, kept, w_router, w_gate, w_up, w_down):
     tokens, width = normed.shape
     count, _, hid = w_gate.shape
     half = count // 2
     steps = half // GROUP
     experts_all = w_router.shape[1]
-    whole = lambda step, scal: (0, 0)
-    full = lambda array: pl.BlockSpec(array.shape, whole)
-    picked = lambda step, scal: (scal[0] * steps + step, 0, 0)
-    own = lambda step, scal: (step, 0, 0)
-    rows_block = pl.BlockSpec((tokens, width), whole)
-    narrow_block = pl.BlockSpec((tokens, experts_all), whole)
-    args = [normed] + ([turned] if last else []) + [upstream, chosen, kept, w_router]
-    specs = [full(array) for array in args]
-    args += [w_gate, w_up, w_down]
-    specs += [
-        pl.BlockSpec((GROUP, width, hid), picked),
-        pl.BlockSpec((GROUP, width, hid), picked),
-        pl.BlockSpec((GROUP, hid, width), picked),
+    once = pl.Buffered(1)
+    whole = lambda step: (0, 0)
+
+    def picked(step):
+        core = lax.rem(lax.axis_index("dp"), 2)
+        return (jnp.where(step < steps, (1 - core) * steps + step, core * steps + step - steps), 0, 0)
+
+    own = lambda step: (jnp.maximum(step - steps, 0), 0, 0)
+    args = [normed, upstream, chosen, kept, w_router]
+    specs = [pl.BlockSpec(array.shape, whole, pipeline_mode=once) for array in args]
+    up_block, down_block = (GROUP, width, hid), (GROUP, hid, width)
+    specs += [pl.BlockSpec(up_block, picked), pl.BlockSpec(up_block, picked), pl.BlockSpec(down_block, picked)]
+    gate_scratch = pltpu.VMEM((tokens, experts_all), F32)
+    rows_scratch = pltpu.VMEM((tokens, width), F32)
+    swap_scratch = [
+        pltpu.VMEM((steps,) + up_block, BF),
+        pltpu.VMEM((steps,) + up_block, BF),
+        pltpu.VMEM((steps,) + down_block, BF),
     ]
-    if last:
-        args += [mix, back, gate_grads]
-        specs += [rows_block, rows_block, narrow_block]
-    out_shape = [
-        jax.ShapeDtypeStruct((half, width, hid), BF),
-        jax.ShapeDtypeStruct((half, width, hid), BF),
-        jax.ShapeDtypeStruct((half, hid, width), BF),
-        jax.ShapeDtypeStruct((tokens, width), BF),
-        jax.ShapeDtypeStruct((tokens, width), BF),
-    ]
-    out_specs = [
-        pl.BlockSpec((GROUP, width, hid), own),
-        pl.BlockSpec((GROUP, width, hid), own),
-        pl.BlockSpec((GROUP, hid, width), own),
-        rows_block,
-        rows_block,
-    ]
-    if last:
-        out_shape += [jax.ShapeDtypeStruct((experts_all, width), F32)]
-        out_specs += [pl.BlockSpec((experts_all, width), whole)]
-    else:
-        out_shape += [
-            jax.ShapeDtypeStruct((tokens, experts_all), F32),
-            jax.ShapeDtypeStruct((width, tokens), BF),
+    return pl.pallas_call(
+        expert_kernel,
+        out_shape=[
+            jax.ShapeDtypeStruct((half, width, hid), BF),
+            jax.ShapeDtypeStruct((half, width, hid), BF),
+            jax.ShapeDtypeStruct((half, hid, width), BF),
+            jax.ShapeDtypeStruct((tokens, width), BF),
+            jax.ShapeDtypeStruct((tokens, width), BF),
+            jax.ShapeDtypeStruct((experts_all, width), F32),
+        ],
+        grid=(2 * steps,),
+        in_specs=specs,
+        out_specs=[
+            pl.BlockSpec(up_block, own),
+            pl.BlockSpec(up_block, own),
+            pl.BlockSpec(down_block, own),
+            pl.BlockSpec((tokens, width), whole, pipeline_mode=once),
+            pl.BlockSpec((tokens, width), whole, pipeline_mode=once),
+            pl.BlockSpec((experts_all, width), whole, pipeline_mode=once),
+        ],
+        scratch_shapes=[
+            gate_scratch, gate_scratch, gate_scratch, rows_scratch, rows_scratch,
+            pltpu.VMEM((width, tokens), BF),
+            pltpu.VMEM((width, GROUP * hid), BF),
+            pltpu.VMEM((width, GROUP * hid), BF),
+            pltpu.VMEM((GROUP * hid, tokens), BF),
+            pltpu.VMEM((tokens, GROUP * hid), BF),
+            pltpu.VMEM((tokens, GROUP * hid), BF),
         ]
-        out_specs += [narrow_block, pl.BlockSpec((width, tokens), whole)]
+        + swap_scratch
+        + swap_scratch
+        + [pltpu.SemaphoreType.DMA((2, 3, steps))],
+        compiler_params=pltpu.CompilerParams(
+            dimension_semantics=("arbitrary",), collective_id=3, has_side_effects=True, vmem_limit_bytes=60 * MIB
+        ),
+        cost_estimate=pl.CostEstimate(
+            flops=18 * tokens * width * count * hid,
+            bytes_accessed=12 * count * width * hid,
+            transcendentals=tokens * count * hid,
+        ),
+        name="experts",
+    )(*args, w_gate, w_up, w_down)
+
+
+def combine_kernel(core_ref, mine_ref, crossed_ref, other_ref, other_crossed_ref, out_ref):
+    here = pl.program_id(0) == 0
+
+    @pl.when(here)
+    def _():
+        out_ref[...] = mine_ref[...].astype(F32) + crossed_ref[...].astype(F32)
+
+    @pl.when(jnp.logical_not(here))
+    def _():
+        out_ref[...] = other_ref[...].astype(F32) + other_crossed_ref[...].astype(F32)
+
+
+def combine(core, mine, crossed, other, other_crossed):
+    half, high, wide = mine.shape
+    step = 2
+    count = half // step
+    block = (step, high, wide)
+    first = pl.BlockSpec(block, lambda part, at, core: (jnp.where(part == 0, at, count - 1), 0, 0))
+    second = pl.BlockSpec(block, lambda part, at, core: (jnp.where(part == 0, 0, at), 0, 0))
     return pl.pallas_call(
-        functools.partial(expert_kernel, last),
-        out_shape=out_shape,
+        combine_kernel,
+        out_shape=jax.ShapeDtypeStruct((2 * half, high, wide), F32),
         grid_spec=pltpu.PrefetchScalarGridSpec(
             num_scalar_prefetch=1,
-            grid=(steps,),
-            in_specs=specs,
-            out_specs=out_specs,
-            scratch_shapes=[
-                pltpu.VMEM((tokens, experts_all), F32),
-                pltpu.VMEM((tokens, experts_all), F32),
-                pltpu.VMEM((tokens, experts_all), F32),
-                pltpu.VMEM((tokens, width), F32),
-                pltpu.VMEM((tokens, width), F32),
-                pltpu.VMEM((width, GROUP * hid), BF),
-                pltpu.VMEM((width, GROUP * hid), BF),
-                pltpu.VMEM((tokens, GROUP * hid), BF),
-                pltpu.VMEM((GROUP * hid, tokens), BF),
-                pltpu.VMEM((tokens, GROUP * hid), BF),
-                pltpu.VMEM((tokens, GROUP * hid), BF),
-            ],
+            grid=(2, count),
+            in_specs=[first, first, second, second],
+            out_specs=pl.BlockSpec(
+                block, lambda part, at, core: (jnp.where(part == 0, core[0], 1 - core[0]) * count + at, 0, 0)
+            ),
         ),
-        compiler_params=pltpu.CompilerParams(
-            dimension_semantics=("arbitrary",), vmem_limit_bytes=60 * MIB
-        ),
-        cost_estimate=pl.CostEstimate(
-            flops=18 * tokens * width * half * hid,
-            bytes_accessed=12 * half * width * hid + 16 * tokens * width,
-            transcendentals=tokens * half * hid,
-        ),
-        name="experts_last" if last else "experts_first",
-    )(scal, *args)
-
-
-MESH = pl.DeviceIdType.MESH
-PART = 32
-
-
-def meet(partners):
-    barrier = pltpu.get_barrier_semaphore()
-    count = 0
-    for here, device in partners:
-        here = jnp.asarray(here)
-
-        @pl.when(here)
-        def _():
-            pl.semaphore_signal(barrier, inc=1, device_id=device, device_id_type=MESH)
-
-        count = count + here.astype(jnp.int32)
-    pl.semaphore_wait(barrier, count)
-
-
-def line_partners():
-    place = lax.axis_index("tensor")
-    last = lax.axis_size("tensor") - 1
-    return [(place > 0, {"tensor": place - 1}), (place < last, {"tensor": place + 1})]
-
-
-class Line:
-    def __init__(self, parts, term, from_left, from_right, to_right, to_left, sems):
-        self.place = lax.axis_index("tensor")
-        self.last = lax.axis_size("tensor") - 1
-        self.parts = parts
-        self.term = term
-        self.from_left, self.from_right = from_left, from_right
-        self.to_right, self.to_left = to_right, to_left
-        self.sems = sems
-
-    def copy(self, way, at):
-        near = jnp.where(self.place < self.last, self.place + 1, self.place - 1)
-        far = jnp.where(self.place > 0, self.place - 1, self.place + 1)
-        source, target, device = (
-            (self.to_right, self.from_left, near) if way == 0 else (self.to_left, self.from_right, far)
-        )
-        return pltpu.make_async_remote_copy(
-            src_ref=source.at[at],
-            dst_ref=target.at[at],
-            send_sem=self.sems.at[2 * way, at],
-            recv_sem=self.sems.at[2 * way + 1, at],
-            device_id={"tensor": device},
-            device_id_type=MESH,
-        )
-
-    def clear(self):
-        @pl.when(self.place == 0)
-        def _():
-            self.from_left[...] = jnp.zeros(self.from_left.shape, self.from_left.dtype)
-
-        @pl.when(self.place == self.last)
-        def _():
-            self.from_right[...] = jnp.zeros(self.from_right.shape, self.from_right.dtype)
-
-    def step(self, at):
-        for way in range(2):
-            part = at - (self.place if way == 0 else self.last - self.place)
-            has_source = self.place > 0 if way == 0 else self.place < self.last
-            has_target = self.place < self.last if way == 0 else self.place > 0
-            arrived = self.from_left if way == 0 else self.from_right
-            leaving = self.to_right if way == 0 else self.to_left
-            valid = (part >= 0) & (part < self.parts)
-
-            @pl.when(valid & has_source)
-            def _():
-                self.copy(way, part).wait_recv()
-
-            @pl.when(valid & has_target)
-            def _():
-                leaving[part] = (self.term(part) + arrived[part].astype(F32)).astype(BF)
-                self.copy(way, part).start()
-
-    def total(self, part):
-        return self.term(part) + self.from_left[part].astype(F32) + self.from_right[part].astype(F32)
-
-    def drain(self):
-        def wait(part, carry):
-            @pl.when(self.place < self.last)
-            def _():
-                self.copy(0, part).wait_send()
-
-            @pl.when(self.place > 0)
-            def _():
-                self.copy(1, part).wait_send()
-
-            return carry
-
-        lax.fori_loop(0, self.parts, wait, 0)
-
-
-def line_scratch(parts, width):
-    return [pltpu.VMEM((parts, PART, width), BF)] * 4 + [pltpu.SemaphoreType.DMA((4, parts))]
-
-
-def peer_copy(source, target, sems, at):
-    return pltpu.make_async_remote_copy(
-        src_ref=source,
-        dst_ref=target,
-        send_sem=sems.at[0, at],
-        recv_sem=sems.at[1, at],
-        device_id={"expert": 1 - lax.axis_index("expert")},
-        device_id_type=MESH,
-    )
-
-
-def scale_of(values):
-    return lax.rsqrt(jnp.mean(values * values, axis=-1, keepdims=True) + epsilon)
-
-
-def residual_kernel(
-    part_ref, x_ref, gain_ref, res_ref, n_ref, from_left, from_right, to_right, to_left, sems, peer_sems
-):
-    parts = part_ref.shape[0]
-    line = Line(parts, lambda at: part_ref[at].astype(F32), from_left, from_right, to_right, to_left, sems)
-    line.clear()
-    meet(line_partners() + [(True, {"expert": 1 - lax.axis_index("expert")})])
-
-    def body(at, carry):
-        line.step(at)
-        part = at - line.last
-
-        @pl.when(part >= 0)
-        def _():
-            residual = x_ref[part].astype(F32) + line.total(part)
-            res_ref[part] = residual
-            unit = residual * scale_of(residual)
-            n_ref[0, part] = (unit * gain_ref[...]).astype(BF)
-            peer_copy(n_ref.at[0, part], n_ref.at[1, part], peer_sems, part).start()
-
-        return carry
-
-    lax.fori_loop(0, parts + line.last, body, 0)
-    line.drain()
-
-    def wait(part, carry):
-        peer_copy(n_ref.at[0, part], n_ref.at[1, part], peer_sems, part).wait()
-        return carry
-
-    lax.fori_loop(0, parts, wait, 0)
-
-
-def residual_norm(part, block_input, gain):
-    rows, width = block_input.shape
-    parts = rows // PART
-    residual, normed = pl.pallas_call(
-        residual_kernel,
-        out_shape=(
-            jax.ShapeDtypeStruct((parts, PART, width), F32),
-            jax.ShapeDtypeStruct((2, parts, PART, width), BF),
-        ),
-        in_specs=[vmem_spec()] * 3,
-        out_specs=(vmem_spec(),) * 2,
-        scratch_shapes=line_scratch(parts, width) + [pltpu.SemaphoreType.DMA((2, parts))],
-        compiler_params=pltpu.CompilerParams(
-            collective_id=0, has_side_effects=True, vmem_limit_bytes=40 * MIB
-        ),
-        name="residual_norm",
-    )(part.reshape(parts, PART, width), block_input.reshape(parts, PART, width), gain[None])
-    return residual, normed.reshape(2 * rows, width)
-
-
-def residual_grad_kernel(
-    back_ref, route_ref, res_ref, up_ref, gain_ref, grad_ref, low_ref, second_ref, route_out,
-    from_left, from_right, to_right, to_left, sems, peer_sems, arrived, terms,
-):
-    parts = back_ref.shape[1]
-    line = Line(parts + 1, lambda at: terms[at], from_left, from_right, to_right, to_left, sems)
-    line.clear()
-    meet(line_partners() + [(True, {"expert": 1 - lax.axis_index("expert")})])
-
-    def send(part, carry):
-        peer_copy(back_ref.at[1, part], arrived.at[part], peer_sems, part).start()
-        return carry
-
-    lax.fori_loop(0, parts, send, 0)
-    terms[parts] = route_ref[...]
-    second_ref[...] = jnp.zeros(second_ref.shape, F32)
-
-    def body(at, carry):
-        @pl.when(at < parts)
-        def _():
-            peer_copy(back_ref.at[1, at], arrived.at[at], peer_sems, at).wait_recv()
-            terms[at] = back_ref[0, at].astype(F32) + arrived[at].astype(F32)
-
-        line.step(at)
-        part = at - line.last
-
-        @pl.when((part >= 0) & (part < parts))
-        def _():
-            grad = line.total(part)
-            residual = res_ref[part]
-            scale = scale_of(residual)
-            unit = residual * scale
-            second_ref[...] += jnp.sum(grad * unit, axis=0, keepdims=True)
-            result = up_ref[part].astype(F32) + norm_back(grad, unit, scale, gain_ref[...])
-            grad_ref[part] = result
-            low_ref[part] = result.astype(BF)
-
-        return carry
-
-    lax.fori_loop(0, parts + 1 + line.last, body, 0)
-    route_out[...] = line.total(parts)
-    line.drain()
-
-    def wait(part, carry):
-        peer_copy(back_ref.at[1, part], arrived.at[part], peer_sems, part).wait_send()
-        return carry
-
-    lax.fori_loop(0, parts, wait, 0)
-
-
-def residual_gradient(back, route, residual, upstream, gain):
-    rows, width = upstream.shape
-    parts = rows // PART
-    grad, low, second, route = pl.pallas_call(
-        residual_grad_kernel,
-        out_shape=(
-            jax.ShapeDtypeStruct((parts, PART, width), F32),
-            jax.ShapeDtypeStruct((parts, PART, width), BF),
-            jax.ShapeDtypeStruct((1, width), F32),
-            jax.ShapeDtypeStruct(route.shape, F32),
-        ),
-        in_specs=[vmem_spec()] * 5,
-        out_specs=(vmem_spec(),) * 4,
-        scratch_shapes=line_scratch(parts + 1, width)
-        + [
-            pltpu.SemaphoreType.DMA((2, parts)),
-            pltpu.VMEM((parts, PART, width), BF),
-            pltpu.VMEM((parts + 1, PART, width), F32),
-        ],
-        compiler_params=pltpu.CompilerParams(
-            collective_id=1, has_side_effects=True, vmem_limit_bytes=48 * MIB
-        ),
-        name="residual_grad",
-    )(
-        back.reshape(2, parts, PART, width), route, residual, upstream.reshape(parts, PART, width), gain[None]
-    )
-    return grad, low.reshape(rows, width), second[0], route
-
-
-def input_grad_kernel(
-    part_ref, x_ref, res_grad_ref, gain_ref, grad_ref, first_ref, from_left, from_right, to_right, to_left, sems
-):
-    parts = part_ref.shape[0]
-    line = Line(parts, lambda at: part_ref[at], from_left, from_right, to_right, to_left, sems)
-    line.clear()
-    meet(line_partners())
-    first_ref[...] = jnp.zeros(first_ref.shape, F32)
-
-    def body(at, carry):
-        line.step(at)
-        part = at - line.last
-
-        @pl.when(part >= 0)
-        def _():
-            grad = line.total(part)
-            values = x_ref[part].astype(F32)
-            scale = scale_of(values)
-            unit = values * scale
-            first_ref[...] += jnp.sum(grad * unit, axis=0, keepdims=True)
-            grad_ref[part] = (res_grad_ref[part] + norm_back(grad, unit, scale, gain_ref[...])).astype(BF)
-
-        return carry
-
-    lax.fori_loop(0, parts + line.last, body, 0)
-    line.drain()
-
-
-def input_gradient(first_part, block_input, residual_grad, gain):
-    rows, width = block_input.shape
-    parts = rows // PART
-    grad, first = pl.pallas_call(
-        input_grad_kernel,
-        out_shape=(
-            jax.ShapeDtypeStruct((parts, PART, width), BF),
-            jax.ShapeDtypeStruct((1, width), F32),
-        ),
-        in_specs=[vmem_spec()] * 4,
-        out_specs=(vmem_spec(),) * 2,
-        scratch_shapes=line_scratch(parts, width),
-        compiler_params=pltpu.CompilerParams(
-            collective_id=2, has_side_effects=True, vmem_limit_bytes=40 * MIB
-        ),
-        name="input_grad",
-    )(first_part.reshape(parts, PART, width), block_input.reshape(parts, PART, width), residual_grad, gain[None])
-    return grad.reshape(rows, width), first[0]
+        compiler_params=pltpu.CompilerParams(vmem_limit_bytes=32 * MIB),
+        cost_estimate=pl.CostEstimate(flops=4 * half * high * wide, bytes_accessed=16 * half * high * wide, transcendentals=0),
+        name="combine",
+    )(core, mine, crossed, other, other_crossed)
 
 
 def swap(array, axis, bit):
@@ -1119,31 +1172,12 @@
     attended, lse, part = attend(scal, query_rot, keys, values, w_output)
     residual, normed_all = residual_norm(part, block_input, second_gain)
 
-    away = jnp.stack([1 - core, side]).astype(jnp.int32)
-    home = jnp.stack([core, side]).astype(jnp.int32)
-    dwg0, dwu0, dwd0, mix, back, gate_grads, turned = experts(
-        False, away, normed_all, None, upstream_all, chosen, kept, w_router, w_gate, w_up, w_down, None, None, None
-    )
-    sent = [swap(item, "dp", 1) for item in (dwd0, dwg0, dwu0)]
-    dwg1, dwu1, dwd1, mix, back, route = experts(
-        True, home, normed_all, turned, upstream_all, chosen, kept, w_router, w_gate, w_up, w_down, mix, back, gate_grads
-    )
-    pairs = [
-        (mine.astype(F32) + other.astype(F32)).astype(BF) for mine, other in zip((dwd1, dwg1, dwu1), sent)
-    ]
+    dwg, dwu, dwd, mix, back, route = experts(
+        normed_all, upstream_all, chosen, kept, w_router, w_gate, w_up, w_down
+    )
+    pairs = (dwd, dwg, dwu)
     crossed = [swap(item, "dp", 2) for item in pairs]
-    sums = [(mine.astype(F32) + other.astype(F32)).astype(BF) for mine, other in zip(pairs, crossed)]
-    others = [swap(item, "dp", 1) for item in sums]
-    expert_sums = [
-        jnp.where(core == 0, jnp.concatenate([mine, other], axis=0), jnp.concatenate([other, mine], axis=0)).astype(F32)
-        for mine, other in zip(sums, others)
-    ]
-
-    mixed = lax.psum_scatter(mix, "tensor", scatter_dimension=1, tiled=True)
-    mixed = mixed[:rows].astype(F32) + swap(mixed[rows:], "expert", 1).astype(F32)
-    block_output = (
-        lax.dynamic_slice_in_dim(residual.reshape(rows, width), feature_start, width // 4, 1) + mixed
-    ).astype(BF)
+    pairs_other = [swap(item, "dp", 1) for item in pairs]
 
     residual_grad, residual_low, grad_second, route = residual_gradient(back, route, residual, upstream, second_gain)
 
@@ -1164,6 +1198,18 @@
         matmul_nt(query_grad, w_query) + matmul_nt(key_grad, key_weight) + matmul_nt(value_grad, value_weight)
     )
     grad_input, grad_first = input_gradient(first_part, block_input, residual_grad, first_gain)
+    mix, grad_input = lax.optimization_barrier((mix, grad_input))
+    mixed = lax.psum_scatter(mix, "tensor", scatter_dimension=1, tiled=True)
+    mixed = mixed[:rows].astype(F32) + swap(mixed[rows:], "expert", 1).astype(F32)
+    block_output = (
+        lax.dynamic_slice_in_dim(residual.reshape(rows, width), feature_start, width // 4, 1) + mixed
+    ).astype(BF)
+
+    core_row = core[None].astype(jnp.int32)
+    expert_sums = [
+        combine(core_row, mine, other, away, swap(other, "dp", 1))
+        for mine, other, away in zip(pairs, crossed, pairs_other)
+    ]
     early = lax.psum((grad_output.astype(BF), route.astype(BF), grad_second.astype(BF)), ("dp", "expert"))
     late = lax.psum(
         (grad_query.astype(BF), grad_key.astype(BF), grad_value.astype(BF), grad_first.astype(BF)), ("dp", "expert")

time: 550 us -> 495 us (0.900)
  Pallas kernels: 301 us -> 212 us
  waiting for transfers between devices: 106 us -> 171 us
  other arithmetic: 63.4 us -> 25.2 us
  blocking collectives: 13.9 us -> 20.3 us
    pallas_call x1, Pallas kernels: 86 us -> 43.1 us  [residual_gradient(): pl.pallas_call(residual_grad_kernel, out_shape=(jax.ShapeDtypeStruct((par...]
    convert_element_type x9 -> x0, other arithmetic: 42.6 us -> none  [the longest x6 24.6 us: fast_device(): (mine.astype(F32) + other.astype(F32)).astype(BF)]
    psum x1, waiting for transfers between devices: 0.01 us -> 37.1 us  [fast_device(): lax.psum((grad_query.astype(BF), grad_key.astype(BF), grad_value.astype(B...]
    ppermute x14, waiting for transfers between devices: 106 us -> 134 us  [swap(): return lax.ppermute(array, axis, [(at, at ^ bit) for at in range(size)])]
    pallas_call x1, Pallas kernels: 57.9 us -> 31.9 us  [input_gradient(): pl.pallas_call(input_grad_kernel, out_shape=(jax.ShapeDtypeStruct((parts,...]
    pallas_call x1, Pallas kernels: 61.4 us -> 36.7 us  [residual_norm(): pl.pallas_call(residual_kernel, out_shape=(jax.ShapeDtypeStruct((parts, P...]
    psum x1, blocking collectives: 13.9 us -> 20.3 us  [fast_device(): lax.psum((grad_query.astype(BF), grad_key.astype(BF), grad_value.astype(B...]
    pallas_call x2 -> x4, Pallas kernels: 77.2 us -> 81 us  [the longest x1 55.4 us: experts(): pl.pallas_call(expert_kernel, out_shape=[jax.ShapeDtypeStruct((half, widt...]
  transfers between devices with their start and end apart: 16 -> 16, of which waited for: 3 -> 6; matrix products, arithmetic and copies ran while one was open for 14% -> 7% of each run, Pallas kernels for 49% -> 14%
where the time goes in v3:
time: 495 us; the launch traced here: 486 us
  Pallas kernels  212 us (43%)
  waiting for transfers between devices  171 us (35%)
  other arithmetic  25.2 us (5%)
  blocking collectives  20.3 us (4%)
  between operations  16.6 us (3%)
  local copies, waits for them, and re-layouts  15.1 us (3%)
  matrix products  13.2 us (3%)
  starting transfers between devices  12.9 us (3%)
    ppermute x14, waiting for transfers between devices, swap(): return lax.ppermute(array, axis, [(at, at ^ bit) for at in range(size)])  134 us
    pallas_call x1, Pallas kernels, experts(): pl.pallas_call(expert_kernel, out_shape=[jax.ShapeDtypeStruct((half, widt...  55.4 us
    pallas_call x1, Pallas kernels, residual_gradient(): pl.pallas_call(residual_grad_kernel, out_shape=(jax.ShapeDtypeStruct((par...  43.1 us
    psum x1, waiting for transfers between devices, fast_device(): lax.psum((grad_query.astype(BF), grad_key.astype(BF), grad_value.astype(B...  37.1 us
    pallas_call x1, Pallas kernels, residual_norm(): pl.pallas_call(residual_kernel, out_shape=(jax.ShapeDtypeStruct((parts, P...  36.7 us
    pallas_call x1, Pallas kernels, input_gradient(): pl.pallas_call(input_grad_kernel, out_shape=(jax.ShapeDtypeStruct((parts,...  31.9 us
    pallas_call x3, Pallas kernels, combine(): pl.pallas_call(combine_kernel, out_shape=jax.ShapeDtypeStruct((2 * half,...  25.6 us
    psum x1, blocking collectives, fast_device(): lax.psum((grad_query.astype(BF), grad_key.astype(BF), grad_value.astype(B...  20.3 us
  transfers between devices with their start and end apart: 16, of which 6 were waited for; matrix products, arithmetic and copies ran while one was open for 7% of the time, Pallas kernels for 14%

profile of v3, /device:TPU:0, one launch (start us, length us, event | category | flops | bytes accessed | tf_op | source)
XLA Modules:
  0.0 486.1 jit_solution(5024690782080558930)
XLA Ops:
  10.8 3.0 collective-permute-start.2
  15.3 1.8 convolution_convert_fusion.3
  19.1 2.0 collective-permute-start.1
  29.7 6.3 %attend.1 = (bf16[512,256]{1,0:T(8,128)(2,1)S(1)}, f32[512,128]{1,0:T(8,128)S(1)}, bf16[512,1024]{1,0:T(8,128)(2,1)S(1)}) custom-call(s32[3]{0:T(128)S(1)} %pad_add_fusion.scal_ref, bf16[512,256]{1,0:T(8,128)(2,1)S(1)} %copy.57.q_ref, bf16[1024,128]{1,0:T(8,128)(2,1)S(1)} %get-tuple-element.72.k_ref, bf16[1024,128]{1,0:T(8,128)(2,1)S(1)} %get-tuple-element.71.v_ref, ...), custom_call_target="tpu_custom_call" | custom-call | tf_op jit(solution)/shard_map/attend/pallas_call | solution.py:488
  36.1 36.7 %residual_norm.1 = (f32[16,32,1024]{2,1,0:T(8,128)S(1)}, bf16[2,16,32,1024]{3,2,1,0:T(8,128)(2,1)S(1)}) custom-call(bf16[16,32,1024]{2,1,0:T(8,128)(2,1)S(1)} %bitcast.41, bf16[16,32,1024]{2,1,0:T(8,128)(2,1)S(1)} %bitcast.35, f32[1,1024]{1,0:T(1,128)S(1)} %bitcast.42), custom_call_target="tpu_custom_call" | custom-call | flops 40000000000 | bytes 10000000 | tf_op jit(solution)/shard_map/residual_norm/pallas_call | solution.py:721
  72.9 3.5 pad_maximum_fusion.g_ref
  76.4 55.4 %experts.1 = (bf16[8,1024,128]{2,1,0:T(8,128)(2,1)}, bf16[8,1024,128]{2,1,0:T(8,128)(2,1)}, bf16[8,128,1024]{2,1,0:T(8,128)(2,1)}, bf16[1024,1024]{1,0:T(8,128)(...) custom-call(bf16[1024,1024]{1,0:T(8,128)(2,1)} %bitcast.45, bf16[1024,1024]{1,0:T(8,128)(2,1)} %pad_maximum_fusion.g_ref, ...), custom_call_target="tpu_custom_call" | custom-call | flops 38654705664 | bytes 25165824 | tf_op jit(solution)/shard_map/experts/pallas_call | solution.py:1046
  132.7 43.1 %residual_grad.1 = (f32[16,32,1024]{2,1,0:T(8,128)S(1)}, bf16[16,32,1024]{2,1,0:T(8,128)(2,1)S(1)}, f32[1,1024]{1,0:T(1,128)S(1)}, f32[32,1024]{1,0:T(8,128)S(1)}) custom-call(bf16[2,16,32,1024]{3,2,1,0:T(8,128)(2,1)} %bitcast.56, f32[32,1024]{1,0:T(8,128)S(1)} %copy-done.25, f32[16,32,1024]{2,1,0:T(8,128)} %copy-done.18, ...), custom_call_target="tpu_custom_call" | custom-call | flops 40000000000 | bytes 10000000 | tf_op jit(solution)/shard_map/residual_grad/pallas_call | solution.py:792
  178.1 12.6 %attend_back.1 = (bf16[512,256]{1,0:T(8,128)(2,1)}, bf16[1024,128]{1,0:T(8,128)(2,1)}, bf16[1024,128]{1,0:T(8,128)(2,1)}, f32[256,1024]{1,0:T(8,128)}) custom-call(s32[3]{0:T(128)} %copy-done.19, bf16[512,256]{1,0:T(8,128)(2,1)} %copy-done.1, bf16[1024,128]{1,0:T(8,128)(2,1)} %copy-done.3, bf16[1024,128]{1,0:T(8,128)(2,1)} %copy-done.2, ...), custom_call_target="tpu_custom_call" | custom-call | tf_op jit(solution)/shard_map/attend_back/pallas_call | solution.py:556
  194.4 2.8 fusion.14
  197.2 2.9 collective-permute-done.3
  203.6 31.9 %input_grad.1 = (bf16[16,32,1024]{2,1,0:T(8,128)(2,1)S(1)}, f32[1,1024]{1,0:T(1,128)S(1)}) custom-call(f32[16,32,1024]{2,1,0:T(8,128)S(1)} %bitcast.34, bf16[16,32,1024]{2,1,0:T(8,128)(2,1)S(1)} %bitcast.36, f32[16,32,1024]{2,1,0:T(8,128)S(1)} %copy-done.24, f32[1,1024]{1,0:T(1,128)S(1)} %bitcast.44), custom_call_target="tpu_custom_call" | custom-call | flops 40000000000 | bytes 10000000 | tf_op jit(solution)/shard_map/input_grad/pallas_call | solution.py:850
  240.2 45.3 %collective-permute-done.5.crossed_ref = bf16[8,1024,128]{2,1,0:T(8,128)(2,1)} collective-permute-done((bf16[8,1024,128]{2,1,0:T(8,128)(2,1)}, bf16[8,1024,128]{2,1,0:T(8,128)(2,1)}, u32[]{:S(2)}, u32[]{:S(2)}) %collective-permute-start.5) | collective-permute-done | bytes 2097184 | tf_op jit(solution)/shard_map/ppermute | solution.py:1128
  286.1 44.4 %collective-permute-done.8.crossed_ref = bf16[8,1024,128]{2,1,0:T(8,128)(2,1)} collective-permute-done((bf16[8,1024,128]{2,1,0:T(8,128)(2,1)}, bf16[8,1024,128]{2,1,0:T(8,128)(2,1)}, u32[]{:S(2)}, u32[]{:S(2)}) %collective-permute-start.8) | collective-permute-done | bytes 2097184 | tf_op jit(solution)/shard_map/ppermute | solution.py:1128
  332.3 39.5 %collective-permute-done.11.crossed_ref = bf16[8,128,1024]{2,1,0:T(8,128)(2,1)} collective-permute-done((bf16[8,128,1024]{2,1,0:T(8,128)(2,1)S(1)}, bf16[8,128,1024]{2,1,0:T(8,128)(2,1)}, u32[]{:S(2)}, u32[]{:S(2)}) %collective-permute-start.11) | collective-permute-done | bytes 2097184 | tf_op jit(solution)/shard_map/ppermute | solution.py:1128
  371.8 2.1 convert_element_type.127
  374.5 2.7 convolution_convert_fusion
  382.6 20.3 %all-reduce = (bf16[1024]{0:T(1024)(128)(2,1)S(1)}, bf16[1024]{0:T(1024)(128)(2,1)S(1)}) all-reduce(bf16[1024]{0:T(1024)(128)(2,1)S(1)} %convert_reduce_fusion.3, bf16[1024]{0:T(1024)(128)(2,1)S(1)} %convert_reduce_fusion.2), channel_id=1, replica_groups=mesh['dp'=4,'expert'=2,'tensor'=4] {'dp','expert'}, use_global_device_ids=true, to_apply=%region_4.5 | all-reduce | flops 2048 | bytes 8192 | tf_op jit(solution)/shard_map/psum | solution.py:1214
  404.1 37.1 %all-reduce.4.cloned.1.call-done = (bf16[1024,256]{1,0:T(8,128)(2,1)}, bf16[1024,128]{1,0:T(8,128)(2,1)}, bf16[1024,128]{1,0:T(8,128)(2,1)}, bf16[256,1024]{1,0:T(8,128)(2,1)}, bf16[1024,32]{0,1:T(8,128)(2,1)}) async-done(((bf16[1024,256]{1,0:T(8,128)(2,1)}, bf16[1024,128]{1,0:T(8,128)(2,1)}, bf16[1024,128]{1,0:T(8,128)(2,1)}, bf16[256,1024]{1,0:T(8,128)(2,1)}, bf16[1024,32]{0,1:T(8,128)(2,1)}), ...) | async-done | bytes 1638416 | tf_op jit(solution)/shard_map/psum | solution.py:1214
  442.8 2.2 convert_element_type.122
  449.7 7.9 %combine.3 = f32[16,1024,128]{2,1,0:T(8,128)} custom-call(s32[1]{0:T(128)} %bitcast.22.core_ref, bf16[8,1024,128]{2,1,0:T(8,128)(2,1)S(1)} %copy-done.6, bf16[8,1024,128]{2,1,0:T(8,128)(2,1)} %collective-permute-done.5.crossed_ref, bf16[8,1024,128]{2,1,0:T(8,128)(2,1)S(1)} %copy-done.8, bf16[8,1024,128]{2,1,0:T(8,128)(2,1)} %collective-permute-done.7.other_crossed_ref), custom_call_target="tpu_custom_call" | custom-call | flops 4194304 | bytes 16777216 | tf_op jit(solution)/shard_map/combine/pallas_call | solution.py:1109
  457.6 8.8 %combine.4 = f32[16,1024,128]{2,1,0:T(8,128)} custom-call(s32[1]{0:T(128)} %bitcast.22.core_ref, bf16[8,1024,128]{2,1,0:T(8,128)(2,1)S(1)} %copy-done.5, bf16[8,1024,128]{2,1,0:T(8,128)(2,1)} %collective-permute-done.8.crossed_ref, bf16[8,1024,128]{2,1,0:T(8,128)(2,1)} %collective-permute-done.9.other_ref, ...), custom_call_target="tpu_custom_call" | custom-call | flops 4194304 | bytes 16777216 | tf_op jit(solution)/shard_map/combine/pallas_call | solution.py:1109
  466.4 8.9 %combine.5 = f32[16,128,1024]{2,1,0:T(8,128)} custom-call(s32[1]{0:T(128)} %bitcast.22.core_ref, bf16[8,128,1024]{2,1,0:T(8,128)(2,1)S(1)} %copy-done.4, bf16[8,128,1024]{2,1,0:T(8,128)(2,1)} %collective-permute-done.11.crossed_ref, bf16[8,128,1024]{2,1,0:T(8,128)(2,1)} %collective-permute-done.12.other_ref, ...), custom_call_target="tpu_custom_call" | custom-call | flops 4194304 | bytes 16777216 | tf_op jit(solution)/shard_map/combine/pallas_call | solution.py:1109
  475.4 1.9 add_convert_fusion
  (161 shorter events, 46.3 us)
Async XLA Ops:
  8.0 15.7 %copy-start = (bf16[1024,256]{1,0:T(8,128)(2,1)S(1)}, bf16[1024,256]{1,0:T(8,128)(2,1)}, u32[]{:S(2)}) copy-start(bf16[1024,256]{1,0:T(8,128)(2,1)} %param.17) | copy-start | bytes 1572868
  8.0 372.0 %reduce-scatter.2.cloned.1.call-start = ((), (), s32[]{:S(2)}) async-start(), calls=%async_computation.1 | async-start | bytes 2621440 | tf_op jit(solution)/shard_map/reduce_scatter | solution.py:1202
  10.8 13.8 %collective-permute-start.2 = (bf16[512,64]{1,0:T(8,128)(2,1)}, bf16[512,64]{1,0:T(8,128)(2,1)}, u32[]{:S(2)}, u32[]{:S(2)}) collective-permute-start(bf16[512,64]{1,0:T(8,128)(2,1)} %pad_maximum_fusion.5), channel_id=1, source_target_pairs={{0,4},{4,0},{1,5},{5,1},{2,6},{6,2},{3,7},{7,3},{8,12},{12,8},{9,1... | collective-permute-start | bytes 196616 | tf_op jit(solution)/shard_map/ppermute | solution.py:1128
  19.1 9.5 %collective-permute-start = (bf16[512,256]{1,0:T(8,128)(2,1)}, bf16[512,256]{1,0:T(8,128)(2,1)}, u32[]{:S(2)}, u32[]{:S(2)}) collective-permute-start(bf16[512,256]{1,0:T(8,128)(2,1)} %pad_maximum_fusion.3), channel_id=1, source_target_pairs={{0,4},{4,0},{1,5},{5,1},{2,6},{6,2},{3,7},{7,3},{8,12},{12,8},{9,1... | collective-permute-start | bytes 786440 | tf_op jit(solution)/shard_map/ppermute | solution.py:1128
  19.1 53.8 %collective-permute-start.1 = (bf16[512,1024]{1,0:T(8,128)(2,1)S(1)}, bf16[512,1024]{1,0:T(8,128)(2,1)}, u32[]{:S(2)}, u32[]{:S(2)}) collective-permute-start(bf16[512,1024]{1,0:T(8,128)(2,1)S(1)} %copy-done.15), channel_id=1, source_target_pairs={{0,4},{4,0},{1,5},{5,1},{2,6},{6,2},{3,7},{7,3},{8,12},{12,8},{9,1... | collective-permute-start | bytes 3145736 | tf_op jit(solution)/shard_map/ppermute | solution.py:1128
  26.9 9.2 %copy-start.20 = (f32[1024]{0:T(1024)S(1)}, f32[1024]{0:T(1024)}, u32[]{:S(2)}) copy-start(f32[1024]{0:T(1024)} %param.21) | copy-start | bytes 12292
  29.6 43.2 %copy-start.2 = (bf16[1024,128]{1,0:T(8,128)(2,1)}, bf16[1024,128]{1,0:T(8,128)(2,1)S(1)}, u32[]{:S(2)}) copy-start(bf16[1024,128]{1,0:T(8,128)(2,1)S(1)} %get-tuple-element.71.v_ref) | copy-start | bytes 786436
  29.7 43.2 %copy-start.3 = (bf16[1024,128]{1,0:T(8,128)(2,1)}, bf16[1024,128]{1,0:T(8,128)(2,1)S(1)}, u32[]{:S(2)}) copy-start(bf16[1024,128]{1,0:T(8,128)(2,1)S(1)} %get-tuple-element.72.k_ref) | copy-start | bytes 786436
  36.0 36.8 %copy-start.16 = (bf16[512,256]{1,0:T(8,128)(2,1)}, bf16[512,256]{1,0:T(8,128)(2,1)S(1)}, u32[]{:S(2)}) copy-start(bf16[512,256]{1,0:T(8,128)(2,1)S(1)} %get-tuple-element.40.att_ref) | copy-start | bytes 786436
  36.1 36.8 %copy-start.17 = (f32[512,128]{1,0:T(8,128)}, f32[512,128]{1,0:T(8,128)S(1)}, u32[]{:S(2)}) copy-start(f32[512,128]{1,0:T(8,128)S(1)} %get-tuple-element.39.lse_ref) | copy-start | bytes 786436
  192.8 7.3 %collective-permute-start.3 = (bf16[512,256]{1,0:T(8,128)(2,1)S(1)}, bf16[512,256]{1,0:T(8,128)(2,1)S(1)}, u32[]{:S(2)}, u32[]{:S(2)}) collective-permute-start(bf16[512,256]{1,0:T(8,128)(2,1)S(1)} %slice.74), channel_id=1, source_target_pairs={{0,4},{4,0},{1,5},{5,1},{2,6},{6,2},{3,7},{7,3},{8,12},{12,8},{9,1... | collective-permute-start | bytes 786440 | tf_op jit(solution)/shard_map/ppermute | solution.py:1128
  236.5 138.0 %copy-start.39 = (f32[512]{0:T(512)S(1)}, f32[512]{0:T(512)}, u32[]{:S(2)}) copy-start(f32[512]{0:T(512)} %copy-done.38) | copy-start | bytes 6148
  236.5 204.7 %all-reduce.4.cloned.1.call-start = ((), (), s32[]{:S(2)}) async-start(), calls=%async_computation.2 | async-start | bytes 3276800 | tf_op jit(solution)/shard_map/psum | solution.py:1214
  236.6 49.0 %collective-permute-start.5 = (bf16[8,1024,128]{2,1,0:T(8,128)(2,1)}, bf16[8,1024,128]{2,1,0:T(8,128)(2,1)}, u32[]{:S(2)}, u32[]{:S(2)}) collective-permute-start(bf16[8,1024,128]{2,1,0:T(8,128)(2,1)} %get-tuple-element.55.mine_ref), channel_id=1, source_target_pairs={{0,16},{8,24},{16,0},{24,8},{1,17},{9,25},{17,1},{25,9},{2,18},{10... | collective-permute-start | bytes 6291464 | tf_op jit(solution)/shard_map/ppermute | solution.py:1128
  238.2 92.3 %collective-permute-start.8 = (bf16[8,1024,128]{2,1,0:T(8,128)(2,1)}, bf16[8,1024,128]{2,1,0:T(8,128)(2,1)}, u32[]{:S(2)}, u32[]{:S(2)}) collective-permute-start(bf16[8,1024,128]{2,1,0:T(8,128)(2,1)} %get-tuple-element.56.mine_ref), channel_id=1, source_target_pairs={{0,16},{8,24},{16,0},{24,8},{1,17},{9,25},{17,1},{25,9},{2,18},{10... | collective-permute-start | bytes 6291464 | tf_op jit(solution)/shard_map/ppermute | solution.py:1128
  238.7 91.8 %collective-permute-start.6 = (bf16[8,1024,128]{2,1,0:T(8,128)(2,1)}, bf16[8,1024,128]{2,1,0:T(8,128)(2,1)S(1)}, u32[]{:S(2)}, u32[]{:S(2)}) collective-permute-start(bf16[8,1024,128]{2,1,0:T(8,128)(2,1)} %get-tuple-element.55.mine_ref), channel_id=1, source_target_pairs={{0,8},{8,0},{16,24},{24,16},{1,9},{9,1},{17,25},{25,17},{2,10},{10... | collective-permute-start | bytes 6291464 | tf_op jit(solution)/shard_map/ppermute | solution.py:1128
  238.7 133.1 %collective-permute-start.11 = (bf16[8,128,1024]{2,1,0:T(8,128)(2,1)S(1)}, bf16[8,128,1024]{2,1,0:T(8,128)(2,1)}, u32[]{:S(2)}, u32[]{:S(2)}) collective-permute-start(bf16[8,128,1024]{2,1,0:T(8,128)(2,1)S(1)} %copy-done.4), channel_id=1, source_target_pairs={{0,16},{8,24},{16,0},{24,8},{1,17},{9,25},{17,1},{25,9},{2,18},{10... | collective-permute-start | bytes 6291464 | tf_op jit(solution)/shard_map/ppermute | solution.py:1128
  285.6 95.5 %collective-permute-start.7 = (bf16[8,1024,128]{2,1,0:T(8,128)(2,1)}, bf16[8,1024,128]{2,1,0:T(8,128)(2,1)}, u32[]{:S(2)}, u32[]{:S(2)}) collective-permute-start(bf16[8,1024,128]{2,1,0:T(8,128)(2,1)} %collective-permute-done.5.crossed_ref), channel_id=1, source_target_pairs={{0,8},{8,0},{16,24},{24,16},{1,9},{9,1},{17,25},{25,17},{2,10},{10... | collective-permute-start | bytes 6291464 | tf_op jit(solution)/shard_map/ppermute | solution.py:1128
  285.6 172.0 %collective-permute-start.9 = (bf16[8,1024,128]{2,1,0:T(8,128)(2,1)}, bf16[8,1024,128]{2,1,0:T(8,128)(2,1)}, u32[]{:S(2)}, u32[]{:S(2)}) collective-permute-start(bf16[8,1024,128]{2,1,0:T(8,128)(2,1)} %get-tuple-element.56.mine_ref), channel_id=1, source_target_pairs={{0,8},{8,0},{16,24},{24,16},{1,9},{9,1},{17,25},{25,17},{2,10},{10... | collective-permute-start | bytes 6291464 | tf_op jit(solution)/shard_map/ppermute | solution.py:1128
  330.5 127.1 %collective-permute-start.10 = (bf16[8,1024,128]{2,1,0:T(8,128)(2,1)}, bf16[8,1024,128]{2,1,0:T(8,128)(2,1)}, u32[]{:S(2)}, u32[]{:S(2)}) collective-permute-start(bf16[8,1024,128]{2,1,0:T(8,128)(2,1)} %collective-permute-done.8.crossed_ref), channel_id=1, source_target_pairs={{0,8},{8,0},{16,24},{24,16},{1,9},{9,1},{17,25},{25,17},{2,10},{10... | collective-permute-start | bytes 6291464 | tf_op jit(solution)/shard_map/ppermute | solution.py:1128
  331.8 134.6 %collective-permute-start.12 = (bf16[8,128,1024]{2,1,0:T(8,128)(2,1)S(1)}, bf16[8,128,1024]{2,1,0:T(8,128)(2,1)}, u32[]{:S(2)}, u32[]{:S(2)}) collective-permute-start(bf16[8,128,1024]{2,1,0:T(8,128)(2,1)S(1)} %copy-done.4), channel_id=1, source_target_pairs={{0,8},{8,0},{16,24},{24,16},{1,9},{9,1},{17,25},{25,17},{2,10},{10... | collective-permute-start | bytes 6291464 | tf_op jit(solution)/shard_map/ppermute | solution.py:1128
  371.8 94.6 %collective-permute-start.13 = (bf16[8,128,1024]{2,1,0:T(8,128)(2,1)}, bf16[8,128,1024]{2,1,0:T(8,128)(2,1)}, u32[]{:S(2)}, u32[]{:S(2)}) collective-permute-start(bf16[8,128,1024]{2,1,0:T(8,128)(2,1)} %collective-permute-done.11.crossed_ref), channel_id=1, source_target_pairs={{0,8},{8,0},{16,24},{24,16},{1,9},{9,1},{17,25},{25,17},{2,10},{10... | collective-permute-start | bytes 6291464 | tf_op jit(solution)/shard_map/ppermute | solution.py:1128
  381.0 94.3 %collective-permute-start.4 = (bf16[512,256]{1,0:T(8,128)(2,1)S(1)}, bf16[512,256]{1,0:T(8,128)(2,1)S(1)}, u32[]{:S(2)}, u32[]{:S(2)}) collective-permute-start(bf16[512,256]{1,0:T(8,128)(2,1)S(1)} %slice.80), channel_id=1, source_target_pairs={{0,4},{4,0},{1,5},{5,1},{2,6},{6,2},{3,7},{7,3},{8,12},{12,8},{9,1... | collective-permute-start | bytes 786440 | tf_op jit(solution)/shard_map/ppermute | solution.py:1128
  466.4 10.8 %copy-start.13 = (bf16[16,32,1024]{2,1,0:T(8,128)(2,1)S(1)}, bf16[16,32,1024]{2,1,0:T(8,128)(2,1)}, u32[]{:S(2)}) copy-start(bf16[16,32,1024]{2,1,0:T(8,128)(2,1)} %copy-done.12) | copy-start | bytes 3145732
  (33 other events, 146.5 us)
Sparse Core Ops, SparseCore 0:
  236.7 43.4 reduce-scatter.1
Sparse Core Ops, SparseCore 1:
  380.1 61.1 all-reduce.3

commit v4 on v3

--- a/solution.py
+++ b/solution.py
@@ -736,22 +736,146 @@
     return residual, normed.reshape(2 * rows, width)
 
 
+UNIT = 512
+
+
 def residual_grad_kernel(
-    back_ref, route_ref, res_ref, up_ref, gain_ref, grad_ref, low_ref, second_ref, route_out,
+    back_ref, route_ref, res_ref, up_ref, gain_ref, wr_ref, marks_ref,
+    far_n, far_g, far_on, far_og, wg_hbm, wu_hbm, wd_hbm, pg_hbm, pu_hbm, pd_hbm,
+    grad_ref, low_ref, second_ref, route_out, sg_hbm, su_hbm, sd_hbm,
     from_left, from_right, to_right, to_left, sems, peer_sems, arrived, terms,
+    tokens_n, tokens_g, turned, kept_gates, gates_w, ups_w, downs_w, pair_g, pair_u, pair_d, ght, dgs, dus,
+    row_sems, weight_sems, pair_sems, out_sems,
 ):
     parts = back_ref.shape[1]
+    core = lax.rem(lax.axis_index("dp"), 2)
+    side = lax.axis_index("expert")
+    groups, group, width, hid = pair_g.shape
+    experts_all = wr_ref.shape[1]
     line = Line(parts + 1, lambda at: terms[at], from_left, from_right, to_right, to_left, sems)
     line.clear()
-    meet(line_partners() + [(True, {"expert": 1 - lax.axis_index("expert")})])
+    meet(line_partners() + [(True, {"expert": 1 - side})])
 
     def send(part, carry):
         peer_copy(back_ref.at[1, part], arrived.at[part], peer_sems, part).start()
         return carry
 
     lax.fori_loop(0, parts, send, 0)
+
+    half = tokens_n.shape[0] // 2
+    row_copies = [
+        pltpu.make_async_copy(source, target.at[pl.ds(place * half, half), :], row_sems.at[kind, place])
+        for place, pair in enumerate(((far_n, far_g), (far_on, far_og)))
+        for kind, (source, target) in enumerate(zip(pair, (tokens_n, tokens_g)))
+    ]
+    weight_copies, pair_copies, out_copies = [], [], []
+    for at in range(groups):
+        first = core * (groups * group) + at * group
+        weight_copies.append(
+            [
+                pltpu.make_async_copy(
+                    source.at[first + expert],
+                    target.at[at, :, pl.ds(expert * hid, hid)],
+                    weight_sems.at[at, kind, expert],
+                )
+                for expert in range(group)
+                for kind, (source, target) in enumerate(((wg_hbm, gates_w), (wu_hbm, ups_w)))
+            ]
+            + [pltpu.make_async_copy(wd_hbm.at[pl.ds(first, group)], downs_w.at[at], weight_sems.at[at, 2, 0])]
+        )
+        sources = (pg_hbm, pu_hbm, pd_hbm)
+        held = (pair_g, pair_u, pair_d)
+        targets = (sg_hbm, su_hbm, sd_hbm)
+        pair_copies.append(
+            [
+                pltpu.make_async_copy(sources[kind].at[pl.ds(at * group, group)], held[kind].at[at], pair_sems.at[at, kind])
+                for kind in range(3)
+            ]
+        )
+        out_copies.append(
+            [
+                pltpu.make_async_copy(held[kind].at[at], targets[kind].at[pl.ds(at * group, group)], out_sems.at[at, kind])
+                for kind in range(3)
+            ]
+        )
+    for copy in row_copies[:2] + weight_copies[0] + row_copies[2:] + pair_copies[0] + weight_copies[1] + pair_copies[1]:
+        copy.start()
     terms[parts] = route_ref[...]
     second_ref[...] = jnp.zeros(second_ref.shape, F32)
+    chunks = 2 * half // UNIT
+    units = chunks + 3
+
+    def compute(at):
+        for where in range(groups):
+            unit = at - where * units
+
+            @pl.when(unit == 0)
+            def _():
+                for copy in weight_copies[where]:
+                    copy.wait()
+
+            if where == 0:
+
+                @pl.when(unit == 0)
+                def _():
+                    for copy in row_copies[:2]:
+                        copy.wait()
+
+                @pl.when(unit == half // UNIT)
+                def _():
+                    for copy in row_copies[2:]:
+                        copy.wait()
+
+            @pl.when(unit == chunks)
+            def _():
+                for copy in pair_copies[where]:
+                    copy.wait()
+
+        where = at // units
+        unit = at - where * units
+
+        @pl.when(unit < chunks)
+        def _():
+            place = pl.multiple_of(unit * UNIT, UNIT)
+            rows = pl.ds(place, UNIT)
+            token = tokens_n[rows, :]
+
+            @pl.when(where == 0)
+            def _():
+                kept_gates[rows, :] = route_gates(token, marks_ref[rows, :], wr_ref[...])[1]
+                turned[:, rows] = token.T
+
+            down = downs_w[where].reshape(group * hid, width)
+            column = side * (experts_all // 2) + (core * groups + where) * group
+            pulled = matmul_nt(tokens_g[rows, :], down)
+            weight = spread_gates(kept_gates[rows, :], column, group, hid)
+            _, gated, gate_grad, up_grad = hidden_terms(token, pulled, weight, gates_w[where], ups_w[where])
+            ght[:, rows] = gated.T
+            dgs[rows, :] = gate_grad
+            dus[rows, :] = up_grad
+
+        @pl.when((unit >= chunks) & (unit < chunks + 2))
+        def _():
+            rows = pl.ds(pl.multiple_of((unit - chunks) * (width // 2), width // 2), width // 2)
+            for source, held in ((dgs, pair_g), (dus, pair_u)):
+                part = matmul(turned[rows, :], source[...])
+                for expert in range(group):
+                    more = part[:, expert * hid : (expert + 1) * hid]
+                    held[where, expert, rows, :] = (held[where, expert, rows, :].astype(F32) + more).astype(BF)
+
+        @pl.when(unit == chunks + 2)
+        def _():
+            part = matmul(ght[...], tokens_g[...])
+            for expert in range(group):
+                more = part[expert * hid : (expert + 1) * hid, :]
+                pair_d[where, expert] = (pair_d[where, expert].astype(F32) + more).astype(BF)
+
+        for where in range(groups):
+
+            @pl.when(at == where * units + units - 1)
+            def _():
+                for copy in out_copies[where]:
+                    copy.start()
 
     def body(at, carry):
         @pl.when(at < parts)
@@ -773,6 +897,10 @@
             grad_ref[part] = result
             low_ref[part] = result.astype(BF)
 
+        @pl.when((at >= FIRST_UNIT) & (at < FIRST_UNIT + groups * units))
+        def _():
+            compute(at - FIRST_UNIT)
+
         return carry
 
     lax.fori_loop(0, parts + 1 + LAG * line.last, body, 0)
@@ -784,36 +912,65 @@
         return carry
 
     lax.fori_loop(0, parts, wait, 0)
-
-
-def residual_gradient(back, route, residual, upstream, gain):
+    for copies in out_copies:
+        for copy in copies:
+            copy.wait()
+
+
+FIRST_UNIT = 3
+
+
+def residual_gradient(back, route, residual, upstream, gain, w_router, marks, far_rows, w_gate, w_up, w_down, pairs):
     rows, width = upstream.shape
     parts = rows // PART
-    grad, low, second, route = pl.pallas_call(
+    half, _, hid = pairs[0].shape
+    groups = half // GROUP
+    tokens = 2 * far_rows[0].shape[0]
+    any_spec = pl.BlockSpec(memory_space=pl.ANY)
+    grad, low, second, route, *sums = pl.pallas_call(
         residual_grad_kernel,
-        out_shape=(
+        out_shape=[
             jax.ShapeDtypeStruct((parts, PART, width), F32),
             jax.ShapeDtypeStruct((parts, PART, width), BF),
             jax.ShapeDtypeStruct((1, width), F32),
             jax.ShapeDtypeStruct(route.shape, F32),
-        ),
-        in_specs=[vmem_spec()] * 5,
-        out_specs=(vmem_spec(),) * 4,
+        ]
+        + [jax.ShapeDtypeStruct(pair.shape, BF) for pair in pairs],
+        in_specs=[vmem_spec()] * 7 + [any_spec] * 10,
+        out_specs=[vmem_spec()] * 4 + [any_spec] * 3,
         scratch_shapes=line_scratch(parts + 1, width)
         + [
             pltpu.SemaphoreType.DMA((2, parts)),
             pltpu.VMEM((parts, PART, width), BF),
             pltpu.VMEM((parts + 1, PART, width), F32),
+            pltpu.VMEM((tokens, width), BF),
+            pltpu.VMEM((tokens, width), BF),
+            pltpu.VMEM((width, tokens), BF),
+            pltpu.VMEM((tokens, w_router.shape[1]), F32),
+            pltpu.VMEM((groups, width, GROUP * hid), BF),
+            pltpu.VMEM((groups, width, GROUP * hid), BF),
+            pltpu.VMEM((groups, GROUP, hid, width), BF),
+            pltpu.VMEM((groups, GROUP, width, hid), BF),
+            pltpu.VMEM((groups, GROUP, width, hid), BF),
+            pltpu.VMEM((groups, GROUP, hid, width), BF),
+            pltpu.VMEM((GROUP * hid, tokens), BF),
+            pltpu.VMEM((tokens, GROUP * hid), BF),
+            pltpu.VMEM((tokens, GROUP * hid), BF),
+            pltpu.SemaphoreType.DMA((2, 2)),
+            pltpu.SemaphoreType.DMA((groups, 3, GROUP)),
+            pltpu.SemaphoreType.DMA((groups, 3)),
+            pltpu.SemaphoreType.DMA((groups, 3)),
         ],
         compiler_params=pltpu.CompilerParams(
-            collective_id=1, has_side_effects=True, vmem_limit_bytes=48 * MIB
+            collective_id=1, has_side_effects=True, vmem_limit_bytes=60 * MIB
         ),
         cost_estimate=LINK_COST,
         name="residual_grad",
     )(
-        back.reshape(2, parts, PART, width), route, residual, upstream.reshape(parts, PART, width), gain[None]
-    )
-    return grad, low.reshape(rows, width), second[0], route
+        back.reshape(2, parts, PART, width), route, residual, upstream.reshape(parts, PART, width), gain[None],
+        w_router, marks, *far_rows, w_gate, w_up, w_down, *pairs,
+    )
+    return grad, low.reshape(rows, width), second[0], route, sums
 
 
 def input_grad_kernel(
@@ -869,11 +1026,43 @@
 GROUP = 4
 
 
+def route_gates(token, marks, w_router):
+    experts_all = w_router.shape[1]
+    chosen = marks[:, :experts_all].astype(F32)
+    kept = marks[:, experts_all:].astype(F32)
+    logits = jnp.where(chosen > 0.0, matmul(token, w_router), masked_score)
+    raised = jnp.exp(logits - jnp.max(logits, axis=1, keepdims=True)) * chosen
+    gate = raised / jnp.sum(raised, axis=1, keepdims=True)
+    return gate, gate * kept
+
+
+def hidden_terms(token, pulled, weight, gate_weights, up_weights):
+    gate_in = matmul(token, gate_weights)
+    up_in = matmul(token, up_weights)
+    sig = 0.5 * jnp.tanh(0.5 * gate_in) + 0.5
+    silu = gate_in * sig
+    hidden = silu * up_in
+    gated = (hidden * weight).astype(BF)
+    scaled = pulled * weight
+    up_grad = (scaled * silu).astype(BF)
+    gate_grad = (scaled * up_in * (sig + silu * (1.0 - sig))).astype(BF)
+    return hidden, gated, gate_grad, up_grad
+
+
+def spread_gates(kept, column, group, hid):
+    lane = lax.broadcasted_iota(jnp.int32, (1, kept.shape[1]), 1)
+    weights = []
+    for expert in range(group):
+        gate = jnp.sum(jnp.where(lane == column + expert, kept, 0.0), axis=1, keepdims=True)
+        weights.append(jnp.broadcast_to(gate, (kept.shape[0], hid)))
+    return jnp.concatenate(weights, axis=1)
+
+
 def expert_kernel(
-    n_ref, g_ref, chosen_ref, kept_ref, wr_ref, wg_ref, wu_ref, wd_ref,
-    dwg_ref, dwu_ref, dwd_ref, mix_ref, back_ref, route_ref,
+    n_ref, g_ref, marks_ref, wr_ref, n_hbm, wg_ref, wu_ref, wd_ref,
+    dwg_ref, dwu_ref, dwd_ref, mix_ref, back_ref, route_ref, far_ref, far_other_ref,
     gates, kept_gates, gate_grads, mix, back, nt, wgs, wus, ght, dgs, dus,
-    out_g, out_u, out_d, in_g, in_u, in_d, sems,
+    out_g, out_u, out_d, in_g, in_u, in_d, sems, far_sems,
 ):
     step = pl.program_id(0)
     steps = pl.num_programs(0) // 2
@@ -881,6 +1070,7 @@
     dp = lax.axis_index("dp")
     core = lax.rem(dp, 2)
     other = {"dp": dp + 1 - 2 * core}
+    beside = {"dp": lax.rem(dp + 2, 4)}
     tokens, width = n_ref.shape
     experts_all = wr_ref.shape[1]
     group, _, hid = wg_ref.shape
@@ -897,19 +1087,25 @@
             for kind, (source, target) in enumerate(((out_g, in_g), (out_u, in_u), (out_d, in_d)))
         ]
 
+    def far_copy(kind, source, target, device):
+        return pltpu.make_async_remote_copy(
+            src_ref=source, dst_ref=target, send_sem=far_sems.at[0, kind], recv_sem=far_sems.at[1, kind],
+            device_id=device, device_id_type=MESH,
+        )
+
+    cross = far_copy(0, n_hbm, far_ref, beside)
+    share = far_copy(1, far_ref, far_other_ref, other)
+
     @pl.when(step == 0)
     def _():
-        meet([(True, other)])
+        meet([(True, other), (True, beside)])
+        cross.start()
 
         def start(at, carry):
             rows = pl.ds(pl.multiple_of(at * CHUNK, CHUNK), CHUNK)
-            chosen = chosen_ref[rows, :] > 0.0
-            logits = jnp.where(chosen, matmul(n_ref[rows, :], wr_ref[...]), masked_score)
-            raised = jnp.exp(logits - jnp.max(logits, axis=1, keepdims=True))
-            raised = jnp.where(chosen, raised, 0.0)
-            gate = raised / jnp.sum(raised, axis=1, keepdims=True)
+            gate, kept_gate = route_gates(n_ref[rows, :], marks_ref[rows, :], wr_ref[...])
             gates[rows, :] = gate
-            kept_gates[rows, :] = gate * kept_ref[rows, :]
+            kept_gates[rows, :] = kept_gate
             mix[rows, :] = jnp.zeros((CHUNK, width), F32)
             back[rows, :] = jnp.zeros((CHUNK, width), F32)
             gate_grads[rows, :] = jnp.zeros((CHUNK, experts_all), F32)
@@ -930,28 +1126,15 @@
         rows = slice(at * CHUNK, (at + 1) * CHUNK)
         token = n_ref[rows, :]
         down = wd_ref[...].reshape(group * hid, width)
-        gate_in = matmul(token, wgs[...])
-        up_in = matmul(token, wus[...])
         pulled = matmul_nt(g_ref[rows, :], down)
-        sig = 0.5 * jnp.tanh(0.5 * gate_in) + 0.5
-        silu = gate_in * sig
-        hidden = silu * up_in
-        kept = kept_gates[rows, :]
-        weights = []
+        weight = spread_gates(kept_gates[rows, :], column, group, hid)
+        hidden, gated, gate_grad, up_grad = hidden_terms(token, pulled, weight, wgs[...], wus[...])
         products = hidden * pulled
         grads = gate_grads[rows, :]
         for expert in range(group):
-            here = lane == column + expert
-            gate = jnp.sum(jnp.where(here, kept, 0.0), axis=1, keepdims=True)
-            weights.append(jnp.broadcast_to(gate, (CHUNK, hid)))
             product = jnp.sum(products[:, expert * hid : (expert + 1) * hid], axis=1, keepdims=True)
-            grads = grads + jnp.where(here, product, 0.0)
+            grads = grads + jnp.where(lane == column + expert, product, 0.0)
         gate_grads[rows, :] = grads
-        weight = jnp.concatenate(weights, axis=1)
-        gated = (hidden * weight).astype(BF)
-        pulled = pulled * weight
-        up_grad = (pulled * silu).astype(BF)
-        gate_grad = (pulled * up_in * (sig + silu * (1.0 - sig))).astype(BF)
         ght[:, rows] = gated.T
         dgs[rows, :] = gate_grad
         dus[rows, :] = up_grad
@@ -1003,6 +1186,8 @@
 
     @pl.when(step == 2 * steps - 1)
     def _():
+        cross.wait_recv()
+        share.start()
         route_ref[...] = jnp.zeros(route_ref.shape, F32)
 
         def finish(at, carry):
@@ -1016,9 +1201,11 @@
             return carry
 
         lax.fori_loop(0, chunks, finish, 0)
-
-
-def experts(normed, upstream, chosen, kept, w_router, w_gate, w_up, w_down):
+        cross.wait_send()
+        share.wait()
+
+
+def experts(normed, upstream, marks, w_router, w_gate, w_up, w_down):
     tokens, width = normed.shape
     count, _, hid = w_gate.shape
     half = count // 2
@@ -1032,8 +1219,10 @@
         return (jnp.where(step < steps, (1 - core) * steps + step, core * steps + step - steps), 0, 0)
 
     own = lambda step: (jnp.maximum(step - steps, 0), 0, 0)
-    args = [normed, upstream, chosen, kept, w_router]
+    args = [normed, upstream, marks, w_router]
     specs = [pl.BlockSpec(array.shape, whole, pipeline_mode=once) for array in args]
+    args += [normed]
+    specs += [pl.BlockSpec(memory_space=pl.ANY)]
     up_block, down_block = (GROUP, width, hid), (GROUP, hid, width)
     specs += [pl.BlockSpec(up_block, picked), pl.BlockSpec(up_block, picked), pl.BlockSpec(down_block, picked)]
     gate_scratch = pltpu.VMEM((tokens, experts_all), F32)
@@ -1052,6 +1241,8 @@
             jax.ShapeDtypeStruct((tokens, width), BF),
             jax.ShapeDtypeStruct((tokens, width), BF),
             jax.ShapeDtypeStruct((experts_all, width), F32),
+            jax.ShapeDtypeStruct((tokens, width), BF),
+            jax.ShapeDtypeStruct((tokens, width), BF),
         ],
         grid=(2 * steps,),
         in_specs=specs,
@@ -1062,6 +1253,8 @@
             pl.BlockSpec((tokens, width), whole, pipeline_mode=once),
             pl.BlockSpec((tokens, width), whole, pipeline_mode=once),
             pl.BlockSpec((experts_all, width), whole, pipeline_mode=once),
+            pl.BlockSpec(memory_space=pl.ANY),
+            pl.BlockSpec(memory_space=pl.ANY),
         ],
         scratch_shapes=[
             gate_scratch, gate_scratch, gate_scratch, rows_scratch, rows_scratch,
@@ -1074,7 +1267,7 @@
         ]
         + swap_scratch
         + swap_scratch
-        + [pltpu.SemaphoreType.DMA((2, 3, steps))],
+        + [pltpu.SemaphoreType.DMA((2, 3, steps)), pltpu.SemaphoreType.DMA((2, 2))],
         compiler_params=pltpu.CompilerParams(
             dimension_semantics=("arbitrary",), collective_id=3, has_side_effects=True, vmem_limit_bytes=60 * MIB
         ),
@@ -1087,40 +1280,41 @@
     )(*args, w_gate, w_up, w_down)
 
 
-def combine_kernel(core_ref, mine_ref, crossed_ref, other_ref, other_crossed_ref, out_ref):
+def widen_kernel(core_ref, mine_ref, other_ref, out_ref):
     here = pl.program_id(0) == 0
 
     @pl.when(here)
     def _():
-        out_ref[...] = mine_ref[...].astype(F32) + crossed_ref[...].astype(F32)
+        out_ref[...] = mine_ref[...].astype(F32)
 
     @pl.when(jnp.logical_not(here))
     def _():
-        out_ref[...] = other_ref[...].astype(F32) + other_crossed_ref[...].astype(F32)
-
-
-def combine(core, mine, crossed, other, other_crossed):
+        out_ref[...] = other_ref[...].astype(F32)
+
+
+def widen(core, mine, other):
     half, high, wide = mine.shape
-    step = 2
+    step = 4
     count = half // step
     block = (step, high, wide)
-    first = pl.BlockSpec(block, lambda part, at, core: (jnp.where(part == 0, at, count - 1), 0, 0))
-    second = pl.BlockSpec(block, lambda part, at, core: (jnp.where(part == 0, 0, at), 0, 0))
     return pl.pallas_call(
-        combine_kernel,
+        widen_kernel,
         out_shape=jax.ShapeDtypeStruct((2 * half, high, wide), F32),
         grid_spec=pltpu.PrefetchScalarGridSpec(
             num_scalar_prefetch=1,
             grid=(2, count),
-            in_specs=[first, first, second, second],
+            in_specs=[
+                pl.BlockSpec(block, lambda part, at, core: (jnp.where(part == 0, at, count - 1), 0, 0)),
+                pl.BlockSpec(block, lambda part, at, core: (jnp.where(part == 0, 0, at), 0, 0)),
+            ],
             out_specs=pl.BlockSpec(
                 block, lambda part, at, core: (jnp.where(part == 0, core[0], 1 - core[0]) * count + at, 0, 0)
             ),
         ),
         compiler_params=pltpu.CompilerParams(vmem_limit_bytes=32 * MIB),
-        cost_estimate=pl.CostEstimate(flops=4 * half * high * wide, bytes_accessed=16 * half * high * wide, transcendentals=0),
-        name="combine",
-    )(core, mine, crossed, other, other_crossed)
+        cost_estimate=pl.CostEstimate(flops=2 * half * high * wide, bytes_accessed=12 * half * high * wide, transcendentals=0),
+        name="widen",
+    )(core, mine, other)
 
 
 def swap(array, axis, bit):
@@ -1146,9 +1340,12 @@
     chosen = jnp.sum(hits.astype(F32), axis=1)
     kept = jnp.sum((hits & (slot_index >= 0)[:, :, None]).astype(F32), axis=1)
     marks = jnp.concatenate([chosen, kept], axis=1).astype(BF)
-    marks = jnp.concatenate([marks, swap(marks, "expert", 1)], axis=0).astype(F32)
-    chosen, kept = marks[:, :experts_all], marks[:, experts_all:]
+    marks = jnp.concatenate([marks, swap(marks, "expert", 1)], axis=0)
+    far_marks = swap(marks, "dp", 2)
+    far_marks = jnp.concatenate([far_marks, swap(far_marks, "dp", 1)], axis=0)
     upstream_all = jnp.concatenate([upstream, swap(upstream, "expert", 1)], axis=0)
+    far_up = swap(upstream_all, "dp", 2)
+    far_other_up = swap(far_up, "dp", 1)
 
     positions = side * rows + jnp.arange(rows, dtype=jnp.int32)
     cosine_table, sine_table = rope_tables(positions)
@@ -1172,14 +1369,16 @@
     attended, lse, part = attend(scal, query_rot, keys, values, w_output)
     residual, normed_all = residual_norm(part, block_input, second_gain)
 
-    dwg, dwu, dwd, mix, back, route = experts(
-        normed_all, upstream_all, chosen, kept, w_router, w_gate, w_up, w_down
-    )
-    pairs = (dwd, dwg, dwu)
-    crossed = [swap(item, "dp", 2) for item in pairs]
-    pairs_other = [swap(item, "dp", 1) for item in pairs]
-
-    residual_grad, residual_low, grad_second, route = residual_gradient(back, route, residual, upstream, second_gain)
+    normed_all, far_up, far_other_up, far_marks = lax.optimization_barrier(
+        (normed_all, far_up, far_other_up, far_marks)
+    )
+    dwg, dwu, dwd, mix, back, route, far_normed, far_other_normed = experts(
+        normed_all, upstream_all, marks, w_router, w_gate, w_up, w_down
+    )
+    residual_grad, residual_low, grad_second, route, sums = residual_gradient(
+        back, route, residual, upstream, second_gain, w_router, far_marks,
+        (far_normed, far_up, far_other_normed, far_other_up), w_gate, w_up, w_down, (dwg, dwu, dwd),
+    )
 
     query_grad, dk, dv, grad_output = attend_back(
         scal, query_rot, keys, values, lse, attended, residual_low, w_output, cosines, sines
@@ -1206,10 +1405,7 @@
     ).astype(BF)
 
     core_row = core[None].astype(jnp.int32)
-    expert_sums = [
-        combine(core_row, mine, other, away, swap(other, "dp", 1))
-        for mine, other, away in zip(pairs, crossed, pairs_other)
-    ]
+    expert_sums = [widen(core_row, item, swap(item, "dp", 1)) for item in sums]
     early = lax.psum((grad_output.astype(BF), route.astype(BF), grad_second.astype(BF)), ("dp", "expert"))
     late = lax.psum(
         (grad_query.astype(BF), grad_key.astype(BF), grad_value.astype(BF), grad_first.astype(BF)), ("dp", "expert")
@@ -1218,7 +1414,7 @@
     late = [item.astype(F32) for item in late]
     return (
         block_output, grad_input, late[3], late[0], late[1], late[2], early[0], early[2], early[1].T,
-        expert_sums[1], expert_sums[2], expert_sums[0],
+        expert_sums[0], expert_sums[1], expert_sums[2],
     )
 
 

time: 495 us -> 446 us (0.901); the launches traced: 486 us -> 443 us
  waiting for transfers between devices: 171 us -> 102 us
  Pallas kernels: 212 us -> 246 us
    ppermute x14 -> x12, waiting for transfers between devices: 134 us -> 63.2 us  [swap(): return lax.ppermute(array, axis, [(at, at ^ bit) for at in range(size)])]
    reduce_scatter x1, waiting for transfers between devices: 0.02 us -> 30.9 us  [fast_device(): mixed = lax.psum_scatter(mix, 'tensor', scatter_dimension=1, tiled=True)]
    psum x1, waiting for transfers between devices: 37.1 us -> 7.83 us  [fast_device(): lax.psum((grad_query.astype(BF), grad_key.astype(BF), grad_value.astype(B...]
    pallas_call x1, Pallas kernels: 55.4 us -> 73.5 us  [experts(): pl.pallas_call(expert_kernel, out_shape=[jax.ShapeDtypeStruct((half, widt...]
    pallas_call x4, Pallas kernels: 68.8 us -> 84.7 us  [the longest x1 66.2 us: residual_gradient(): pl.pallas_call(residual_grad_kernel, out_shape=[jax.ShapeDtypeStruct((par...]
    unnamed x85 -> x68, local copies, waits for them, and re-layouts: 9.58 us -> 12.6 us
    ppermute x14 -> x12, starting transfers between devices: 12.8 us -> 10.6 us  [swap(): return lax.ppermute(array, axis, [(at, at ^ bit) for at in range(size)])]
  transfers between devices with their start and end apart: 16 -> 14, of which waited for: 6 -> 5; matrix products, arithmetic and copies ran while one was open for 7% -> 9% of each run, Pallas kernels for 14% -> 14%
where the time goes in v4:
time: 446 us; the launch traced here: 443 us
  Pallas kernels  246 us (55%)
  waiting for transfers between devices  102 us (23%)
  other arithmetic  21.3 us (5%)
  local copies, waits for them, and re-layouts  19.2 us (4%)
  blocking collectives  16.9 us (4%)
  between operations  16.2 us (4%)
  starting transfers between devices  10.9 us (2%)
  matrix products  10.7 us (2%)
    pallas_call x1, Pallas kernels, experts(): pl.pallas_call(expert_kernel, out_shape=[jax.ShapeDtypeStruct((half, widt...  73.5 us
    pallas_call x1, Pallas kernels, residual_gradient(): pl.pallas_call(residual_grad_kernel, out_shape=[jax.ShapeDtypeStruct((par...  66.2 us
    ppermute x12, waiting for transfers between devices, swap(): return lax.ppermute(array, axis, [(at, at ^ bit) for at in range(size)])  63.2 us
    pallas_call x1, Pallas kernels, residual_norm(): pl.pallas_call(residual_kernel, out_shape=(jax.ShapeDtypeStruct((parts, P...  38.3 us
    reduce_scatter x1, waiting for transfers between devices, fast_device(): mixed = lax.psum_scatter(mix, 'tensor', scatter_dimension=1, tiled=True)  30.9 us
    pallas_call x1, Pallas kernels, input_gradient(): pl.pallas_call(input_grad_kernel, out_shape=(jax.ShapeDtypeStruct((parts,...  30.8 us
    pallas_call x3, Pallas kernels, widen(): pl.pallas_call(widen_kernel, out_shape=jax.ShapeDtypeStruct((2 * half, hi...  18.5 us
    psum x1, blocking collectives, fast_device(): lax.psum((grad_query.astype(BF), grad_key.astype(BF), grad_value.astype(B...  16.9 us
  transfers between devices with their start and end apart: 14, of which 5 were waited for; matrix products, arithmetic and copies ran while one was open for 9% of the time, Pallas kernels for 14%

profile of v4, /device:TPU:0, one launch (start us, length us, event | category | flops | bytes accessed | tf_op | source)
XLA Modules:
  0.0 443.4 jit_solution(783728298528731053)
XLA Ops:
  8.1 3.0 collective-permute-start.1
  13.3 2.3 constant_dynamic-update-slice_fusion.1
  16.5 19.0 %collective-permute-done.1 = bf16[512,1024]{1,0:T(8,128)(2,1)} collective-permute-done((bf16[512,1024]{1,0:T(8,128)(2,1)}, bf16[512,1024]{1,0:T(8,128)(2,1)}, u32[]{:S(2)}, u32[]{:S(2)}) %collective-permute-start.1) | collective-permute-done | bytes 1048608 | tf_op jit(solution)/shard_map/ppermute | solution.py:1322
  35.4 2.3 constant_dynamic-update-slice_fusion.g_ref
  37.7 2.0 collective-permute-start.2
  48.7 40.9 %collective-permute-done.5 = bf16[1024,64]{1,0:T(8,128)(2,1)} collective-permute-done((bf16[1024,64]{1,0:T(8,128)(2,1)}, bf16[1024,64]{1,0:T(8,128)(2,1)}, u32[]{:S(2)}, u32[]{:S(2)}) %collective-permute-start.5) | collective-permute-done | bytes 131104 | tf_op jit(solution)/shard_map/ppermute | solution.py:1322
  90.7 6.3 %attend.1 = (bf16[512,256]{1,0:T(8,128)(2,1)S(1)}, f32[512,128]{1,0:T(8,128)S(1)}, bf16[512,1024]{1,0:T(8,128)(2,1)S(1)}) custom-call(s32[3]{0:T(128)S(1)} %pad_add_fusion.scal_ref, bf16[512,256]{1,0:T(8,128)(2,1)S(1)} %copy.60.q_ref, bf16[1024,128]{1,0:T(8,128)(2,1)S(1)} %get-tuple-element.88.k_ref, bf16[1024,128]{1,0:T(8,128)(2,1)S(1)} %get-tuple-element.87.v_ref, ...), custom_call_target="tpu_custom_call" | custom-call | tf_op jit(solution)/shard_map/attend/pallas_call | solution.py:488
  97.6 38.3 %residual_norm.1 = (f32[16,32,1024]{2,1,0:T(8,128)S(1)}, bf16[2,16,32,1024]{3,2,1,0:T(8,128)(2,1)S(1)}) custom-call(bf16[16,32,1024]{2,1,0:T(8,128)(2,1)S(1)} %bitcast.39, bf16[16,32,1024]{2,1,0:T(8,128)(2,1)S(1)} %bitcast.35, f32[1,1024]{1,0:T(1,128)S(1)} %bitcast.41), custom_call_target="tpu_custom_call" | custom-call | flops 40000000000 | bytes 10000000 | tf_op jit(solution)/shard_map/residual_norm/pallas_call | solution.py:721
  138.7 1.8 pad_maximum_fusion.1.marks_ref
  140.5 73.5 %experts.1 = (bf16[8,1024,128]{2,1,0:T(8,128)(2,1)}, bf16[8,1024,128]{2,1,0:T(8,128)(2,1)}, bf16[8,128,1024]{2,1,0:T(8,128)(2,1)}, bf16[1024,1024]{1,0:T(8,128)(...) custom-call(bf16[1024,1024]{1,0:T(8,128)(2,1)} %bitcast.43, ...), custom_call_target="tpu_custom_call" | custom-call | flops 38654705664 | bytes 25165824 | tf_op jit(solution)/shard_map/experts/pallas_call | solution.py:1235
  214.0 66.2 %residual_grad.1 = (f32[16,32,1024]{2,1,0:T(8,128)}, bf16[16,32,1024]{2,1,0:T(8,128)(2,1)}, f32[1,1024]{1,0:T(1,128)}, f32[32,1024]{1,0:T(8,128)}, bf16[8,1024,1...) custom-call(bf16[2,16,32,1024]{3,2,1,0:T(8,128)(2,1)} %bitcast.57, ...), custom_call_target="tpu_custom_call" | custom-call | flops 40000000000 | bytes 10000000 | tf_op jit(solution)/shard_map/residual_grad/pallas_call | solution.py:930
  280.3 12.6 %attend_back.1 = (bf16[512,256]{1,0:T(8,128)(2,1)}, bf16[1024,128]{1,0:T(8,128)(2,1)}, bf16[1024,128]{1,0:T(8,128)(2,1)}, f32[256,1024]{1,0:T(8,128)}) custom-call(s32[3]{0:T(128)} %copy-done.15, bf16[512,256]{1,0:T(8,128)(2,1)} %copy-done.1, bf16[1024,128]{1,0:T(8,128)(2,1)} %copy-done.3, bf16[1024,128]{1,0:T(8,128)(2,1)} %copy-done.2, ...), custom_call_target="tpu_custom_call" | custom-call | tf_op jit(solution)/shard_map/attend_back/pallas_call | solution.py:556
  295.5 2.7 fusion.13
  298.2 3.3 collective-permute-done.7
  305.0 30.8 %input_grad.1 = (bf16[16,32,1024]{2,1,0:T(8,128)(2,1)S(1)}, f32[1,1024]{1,0:T(1,128)S(1)}) custom-call(f32[16,32,1024]{2,1,0:T(8,128)S(1)} %bitcast.34, bf16[16,32,1024]{2,1,0:T(8,128)(2,1)S(1)} %bitcast.36, f32[16,32,1024]{2,1,0:T(8,128)S(1)} %copy-done.19, f32[1,1024]{1,0:T(1,128)S(1)} %bitcast.42), custom_call_target="tpu_custom_call" | custom-call | flops 40000000000 | bytes 10000000 | tf_op jit(solution)/shard_map/input_grad/pallas_call | solution.py:1007
  338.4 2.1 convert_element_type.123
  342.1 2.7 convolution_convert_fusion
  347.6 30.9 %reduce-scatter.2.cloned.1.call-done = bf16[1024,256]{1,0:T(8,128)(2,1)} async-done(((bf16[1024,1024]{1,0:T(8,128)(2,1)}), bf16[1024,256]{1,0:T(8,128)(2,1)}) %reduce-scatter.2.cloned.1.call-update) | async-done | bytes 524304 | tf_op jit(solution)/shard_map/reduce_scatter | solution.py:1401
  381.0 16.9 %all-reduce = (bf16[1024]{0:T(1024)(128)(2,1)S(1)}, bf16[1024]{0:T(1024)(128)(2,1)S(1)}) all-reduce(bf16[1024]{0:T(1024)(128)(2,1)S(1)} %convert_reduce_fusion.3, bf16[1024]{0:T(1024)(128)(2,1)S(1)} %convert_reduce_fusion.2), channel_id=1, replica_groups=mesh['dp'=4,'expert'=2,'tensor'=4] {'dp','expert'}, use_global_device_ids=true, to_apply=%region_4.5 | all-reduce | flops 2048 | bytes 8192 | tf_op jit(solution)/shard_map/psum | solution.py:1410
  399.1 7.8 %all-reduce.4.cloned.1.call-done = (bf16[1024,256]{1,0:T(8,128)(2,1)}, bf16[1024,128]{1,0:T(8,128)(2,1)}, bf16[1024,128]{1,0:T(8,128)(2,1)}, bf16[256,1024]{1,0:T(8,128)(2,1)}, bf16[1024,32]{0,1:T(8,128)(2,1)}) async-done(((bf16[1024,256]{1,0:T(8,128)(2,1)}, bf16[1024,128]{1,0:T(8,128)(2,1)}, bf16[1024,128]{1,0:T(8,128)(2,1)}, bf16[256,1024]{1,0:T(8,128)(2,1)}, bf16[1024,32]{0,1:T(8,128)(2,1)}), ...) | async-done | bytes 1638416 | tf_op jit(solution)/shard_map/psum | solution.py:1410
  408.5 2.2 convert_element_type.118
  414.4 6.2 %widen.5 = f32[16,128,1024]{2,1,0:T(8,128)} custom-call(s32[1]{0:T(128)} %bitcast.22.core_ref, bf16[8,128,1024]{2,1,0:T(8,128)(2,1)S(1)} %copy-done.6, bf16[8,128,1024]{2,1,0:T(8,128)(2,1)} %collective-permute-done.11.other_ref), custom_call_target="tpu_custom_call" | custom-call | flops 2097152 | bytes 12582912 | tf_op jit(solution)/shard_map/widen/pallas_call | solution.py:1300
  420.7 6.1 %widen.4 = f32[16,1024,128]{2,1,0:T(8,128)} custom-call(s32[1]{0:T(128)} %bitcast.22.core_ref, bf16[8,1024,128]{2,1,0:T(8,128)(2,1)S(1)} %copy-done.5, bf16[8,1024,128]{2,1,0:T(8,128)(2,1)} %collective-permute-done.10.other_ref), custom_call_target="tpu_custom_call" | custom-call | flops 2097152 | bytes 12582912 | tf_op jit(solution)/shard_map/widen/pallas_call | solution.py:1300
  426.8 6.2 %widen.3 = f32[16,1024,128]{2,1,0:T(8,128)} custom-call(s32[1]{0:T(128)} %bitcast.22.core_ref, bf16[8,1024,128]{2,1,0:T(8,128)(2,1)S(1)} %copy-done.4, bf16[8,1024,128]{2,1,0:T(8,128)(2,1)} %collective-permute-done.9.other_ref), custom_call_target="tpu_custom_call" | custom-call | flops 2097152 | bytes 12582912 | tf_op jit(solution)/shard_map/widen/pallas_call | solution.py:1300
  (140 shorter events, 41.0 us)
Async XLA Ops:
  8.0 35.0 %copy-start = (bf16[1024,256]{1,0:T(8,128)(2,1)S(1)}, bf16[1024,256]{1,0:T(8,128)(2,1)}, u32[]{:S(2)}) copy-start(bf16[1024,256]{1,0:T(8,128)(2,1)} %param.17) | copy-start | bytes 1572868
  8.1 370.4 %reduce-scatter.2.cloned.1.call-start = ((), (), s32[]{:S(2)}) async-start(), calls=%async_computation.1 | async-start | bytes 2621440 | tf_op jit(solution)/shard_map/reduce_scatter | solution.py:1401
  8.1 27.3 %collective-permute-start.1 = (bf16[512,1024]{1,0:T(8,128)(2,1)}, bf16[512,1024]{1,0:T(8,128)(2,1)}, u32[]{:S(2)}, u32[]{:S(2)}) collective-permute-start(bf16[512,1024]{1,0:T(8,128)(2,1)} %param.29), channel_id=1, source_target_pairs={{0,4},{4,0},{1,5},{5,1},{2,6},{6,2},{3,7},{7,3},{8,12},{12,8},{9,1... | collective-permute-start | bytes 3145736 | tf_op jit(solution)/shard_map/ppermute | solution.py:1322
  13.1 30.6 %collective-permute-start.4 = (bf16[512,64]{1,0:T(8,128)(2,1)S(1)}, bf16[512,64]{1,0:T(8,128)(2,1)S(1)}, u32[]{:S(2)}, u32[]{:S(2)}) collective-permute-start(bf16[512,64]{1,0:T(8,128)(2,1)S(1)} %pad_maximum_fusion.6), channel_id=1, source_target_pairs={{0,4},{4,0},{1,5},{5,1},{2,6},{6,2},{3,7},{7,3},{8,12},{12,8},{9,1... | collective-permute-start | bytes 196616 | tf_op jit(solution)/shard_map/ppermute | solution.py:1322
  37.7 59.3 %collective-permute-start.2 = (bf16[1024,1024]{1,0:T(8,128)(2,1)}, bf16[1024,1024]{1,0:T(8,128)(2,1)}, u32[]{:S(2)}, u32[]{:S(2)}) collective-permute-start(bf16[1024,1024]{1,0:T(8,128)(2,1)} %constant_dynamic-update-slice_fusion.g_ref), channel_id=1, source_target_pairs={{0,16},{8,24},{16,0},{24,8},{1,17},{9,25},{17,1},{25,9},{2,18},{10... | collective-permute-start | bytes 6291464 | tf_op jit(solution)/shard_map/ppermute | solution.py:1322
  41.5 48.2 %collective-permute-start = (bf16[512,256]{1,0:T(8,128)(2,1)}, bf16[512,256]{1,0:T(8,128)(2,1)}, u32[]{:S(2)}, u32[]{:S(2)}) collective-permute-start(bf16[512,256]{1,0:T(8,128)(2,1)} %pad_maximum_fusion.3), channel_id=1, source_target_pairs={{0,4},{4,0},{1,5},{5,1},{2,6},{6,2},{3,7},{7,3},{8,12},{12,8},{9,1... | collective-permute-start | bytes 786440 | tf_op jit(solution)/shard_map/ppermute | solution.py:1322
  44.5 45.1 %collective-permute-start.5 = (bf16[1024,64]{1,0:T(8,128)(2,1)}, bf16[1024,64]{1,0:T(8,128)(2,1)}, u32[]{:S(2)}, u32[]{:S(2)}) collective-permute-start(bf16[1024,64]{1,0:T(8,128)(2,1)} %pad_maximum_fusion.4.marks_ref), channel_id=1, source_target_pairs={{0,16},{8,24},{16,0},{24,8},{1,17},{9,25},{17,1},{25,9},{2,18},{10... | collective-permute-start | bytes 393224 | tf_op jit(solution)/shard_map/ppermute | solution.py:1322
  46.8 43.9 %copy-start.7 = (bf16[256,1024]{1,0:T(8,128)(2,1)S(1)}, bf16[256,1024]{1,0:T(8,128)(2,1)}, u32[]{:S(2)}) copy-start(bf16[256,1024]{1,0:T(8,128)(2,1)} %wo_ref.3) | copy-start | bytes 1572868
  48.5 49.1 %copy-start.16 = (f32[1024]{0:T(1024)S(1)}, f32[1024]{0:T(1024)}, u32[]{:S(2)}) copy-start(f32[1024]{0:T(1024)} %param.21) | copy-start | bytes 12292
  48.6 87.3 %copy-start.1 = (bf16[512,256]{1,0:T(8,128)(2,1)}, bf16[512,256]{1,0:T(8,128)(2,1)S(1)}, u32[]{:S(2)}) copy-start(bf16[512,256]{1,0:T(8,128)(2,1)S(1)} %copy.60.q_ref) | copy-start | bytes 786436
  48.7 87.2 %copy-start.15 = (s32[3]{0:T(128)}, s32[3]{0:T(128)S(1)}, u32[]{:S(2)}) copy-start(s32[3]{0:T(128)S(1)} %pad_add_fusion.scal_ref) | copy-start | bytes 40
  89.6 49.0 %collective-permute-start.6 = (bf16[1024,64]{1,0:T(8,128)(2,1)}, bf16[1024,64]{1,0:T(8,128)(2,1)S(1)}, u32[]{:S(2)}, u32[]{:S(2)}) collective-permute-start(bf16[1024,64]{1,0:T(8,128)(2,1)} %collective-permute-done.5), channel_id=1, source_target_pairs={{0,8},{8,0},{16,24},{24,16},{1,9},{9,1},{17,25},{25,17},{2,10},{10... | collective-permute-start | bytes 393224 | tf_op jit(solution)/shard_map/ppermute | solution.py:1322
  90.7 45.3 %copy-start.2 = (bf16[1024,128]{1,0:T(8,128)(2,1)}, bf16[1024,128]{1,0:T(8,128)(2,1)S(1)}, u32[]{:S(2)}) copy-start(bf16[1024,128]{1,0:T(8,128)(2,1)S(1)} %get-tuple-element.87.v_ref) | copy-start | bytes 786436
  90.7 45.3 %copy-start.3 = (bf16[1024,128]{1,0:T(8,128)(2,1)}, bf16[1024,128]{1,0:T(8,128)(2,1)S(1)}, u32[]{:S(2)}) copy-start(bf16[1024,128]{1,0:T(8,128)(2,1)S(1)} %get-tuple-element.88.k_ref) | copy-start | bytes 786436
  97.0 39.0 %copy-start.12 = (bf16[512,256]{1,0:T(8,128)(2,1)}, bf16[512,256]{1,0:T(8,128)(2,1)S(1)}, u32[]{:S(2)}) copy-start(bf16[512,256]{1,0:T(8,128)(2,1)S(1)} %get-tuple-element.50.att_ref) | copy-start | bytes 786436
  97.0 39.0 %copy-start.13 = (f32[512,128]{1,0:T(8,128)}, f32[512,128]{1,0:T(8,128)S(1)}, u32[]{:S(2)}) copy-start(f32[512,128]{1,0:T(8,128)S(1)} %get-tuple-element.49.lse_ref) | copy-start | bytes 786436
  97.0 43.5 %collective-permute-start.3 = (bf16[1024,1024]{1,0:T(8,128)(2,1)}, bf16[1024,1024]{1,0:T(8,128)(2,1)}, u32[]{:S(2)}, u32[]{:S(2)}) collective-permute-start(bf16[1024,1024]{1,0:T(8,128)(2,1)} %collective-permute-done.2.far_g), channel_id=1, source_target_pairs={{0,8},{8,0},{16,24},{24,16},{1,9},{9,1},{17,25},{25,17},{2,10},{10... | collective-permute-start | bytes 6291464 | tf_op jit(solution)/shard_map/ppermute | solution.py:1322
  294.9 6.6 %collective-permute-start.7 = (bf16[512,256]{1,0:T(8,128)(2,1)S(1)}, bf16[512,256]{1,0:T(8,128)(2,1)S(1)}, u32[]{:S(2)}, u32[]{:S(2)}) collective-permute-start(bf16[512,256]{1,0:T(8,128)(2,1)S(1)} %slice.64), channel_id=1, source_target_pairs={{0,4},{4,0},{1,5},{5,1},{2,6},{6,2},{3,7},{7,3},{8,12},{12,8},{9,1... | collective-permute-start | bytes 786440 | tf_op jit(solution)/shard_map/ppermute | solution.py:1322
  336.8 70.1 %all-reduce.4.cloned.1.call-start = ((), (), s32[]{:S(2)}) async-start(), calls=%async_computation.2 | async-start | bytes 3276800 | tf_op jit(solution)/shard_map/psum | solution.py:1410
  337.1 77.4 %collective-permute-start.11 = (bf16[8,128,1024]{2,1,0:T(8,128)(2,1)}, bf16[8,128,1024]{2,1,0:T(8,128)(2,1)}, u32[]{:S(2)}, u32[]{:S(2)}) collective-permute-start(bf16[8,128,1024]{2,1,0:T(8,128)(2,1)} %get-tuple-element.75.mine_ref), channel_id=1, source_target_pairs={{0,8},{8,0},{16,24},{24,16},{1,9},{9,1},{17,25},{25,17},{2,10},{10... | collective-permute-start | bytes 6291464 | tf_op jit(solution)/shard_map/ppermute | solution.py:1322
  337.2 83.5 %collective-permute-start.10 = (bf16[8,1024,128]{2,1,0:T(8,128)(2,1)}, bf16[8,1024,128]{2,1,0:T(8,128)(2,1)}, u32[]{:S(2)}, u32[]{:S(2)}) collective-permute-start(bf16[8,1024,128]{2,1,0:T(8,128)(2,1)} %get-tuple-element.74.mine_ref), channel_id=1, source_target_pairs={{0,8},{8,0},{16,24},{24,16},{1,9},{9,1},{17,25},{25,17},{2,10},{10... | collective-permute-start | bytes 6291464 | tf_op jit(solution)/shard_map/ppermute | solution.py:1322
  338.4 88.4 %collective-permute-start.9 = (bf16[8,1024,128]{2,1,0:T(8,128)(2,1)S(1)}, bf16[8,1024,128]{2,1,0:T(8,128)(2,1)}, u32[]{:S(2)}, u32[]{:S(2)}) collective-permute-start(bf16[8,1024,128]{2,1,0:T(8,128)(2,1)S(1)} %copy-done.4), channel_id=1, source_target_pairs={{0,8},{8,0},{16,24},{24,16},{1,9},{9,1},{17,25},{25,17},{2,10},{10... | collective-permute-start | bytes 6291464 | tf_op jit(solution)/shard_map/ppermute | solution.py:1322
  346.2 34.8 %copy-start.28 = (f32[1,1024]{1,0:T(1,128)S(1)}, f32[1,1024]{1,0:T(1,128)}, u32[]{:S(2)}) copy-start(f32[1,1024]{1,0:T(1,128)} %get-tuple-element.71) | copy-start | bytes 12292
  379.4 53.5 %collective-permute-start.8 = (bf16[512,256]{1,0:T(8,128)(2,1)S(1)}, bf16[512,256]{1,0:T(8,128)(2,1)S(1)}, u32[]{:S(2)}, u32[]{:S(2)}) collective-permute-start(bf16[512,256]{1,0:T(8,128)(2,1)S(1)} %slice.70), channel_id=1, source_target_pairs={{0,4},{4,0},{1,5},{5,1},{2,6},{6,2},{3,7},{7,3},{8,12},{12,8},{9,1... | collective-permute-start | bytes 786440 | tf_op jit(solution)/shard_map/ppermute | solution.py:1322
  (22 other events, 141.8 us)
Sparse Core Ops, SparseCore 0:
  336.9 41.4 reduce-scatter.1
Sparse Core Ops, SparseCore 1:
  347.7 59.2 all-reduce.3

commit v5 on v4

--- a/solution.py
+++ b/solution.py
@@ -683,13 +683,44 @@
     return lax.rsqrt(jnp.mean(values * values, axis=-1, keepdims=True) + epsilon)
 
 
+def plain_copy(source, target, sems, at, device):
+    return pltpu.make_async_remote_copy(
+        src_ref=source, dst_ref=target, send_sem=sems.at[0, at], recv_sem=sems.at[1, at],
+        device_id=device, device_id_type=MESH,
+    )
+
+
+def beside():
+    return {"dp": lax.rem(lax.axis_index("dp") + 2, 4)}
+
+
+def other_core():
+    place = lax.axis_index("dp")
+    return {"dp": place + 1 - 2 * lax.rem(place, 2)}
+
+
 def residual_kernel(
-    part_ref, x_ref, gain_ref, res_ref, n_ref, from_left, from_right, to_right, to_left, sems, peer_sems
+    part_ref, x_ref, gain_ref, up_own, up_peer0, up_peer1, marks_ref,
+    res_ref, n_ref, up_all, far_peer, far_marks,
+    from_left, from_right, to_right, to_left, sems, peer_sems, far_sems, near_sems,
 ):
     parts = part_ref.shape[0]
     line = Line(parts, lambda at: part_ref[at].astype(F32), from_left, from_right, to_right, to_left, sems)
     line.clear()
-    meet(line_partners() + [(True, {"expert": 1 - lax.axis_index("expert")})])
+    meet(line_partners() + [(True, {"expert": 1 - lax.axis_index("expert")}), (True, beside())])
+    quarter = up_peer0.shape[0]
+    far_copies = [
+        plain_copy(marks_ref, far_marks, far_sems, 0, beside()),
+        plain_copy(up_peer0, far_peer.at[pl.ds(0, quarter), :], far_sems, 1, beside()),
+        plain_copy(up_peer1, far_peer.at[pl.ds(quarter, quarter), :], far_sems, 2, beside()),
+    ]
+    near_copies = [
+        pltpu.make_async_copy(up_own, up_all.at[pl.ds(0, 2 * quarter), :], near_sems.at[0]),
+        pltpu.make_async_copy(up_peer0, up_all.at[pl.ds(2 * quarter, quarter), :], near_sems.at[1]),
+        pltpu.make_async_copy(up_peer1, up_all.at[pl.ds(3 * quarter, quarter), :], near_sems.at[2]),
+    ]
+    for copy in far_copies + near_copies:
+        copy.start()
 
     def body(at, carry):
         line.step(at)
@@ -713,39 +744,50 @@
         return carry
 
     lax.fori_loop(0, parts, wait, 0)
-
-
-def residual_norm(part, block_input, gain):
+    for copy in far_copies + near_copies:
+        copy.wait()
+
+
+def residual_norm(part, block_input, gain, upstream, peer_up, marks):
     rows, width = block_input.shape
     parts = rows // PART
-    residual, normed = pl.pallas_call(
+    any_spec = pl.BlockSpec(memory_space=pl.ANY)
+    residual, normed, *rest = pl.pallas_call(
         residual_kernel,
         out_shape=(
             jax.ShapeDtypeStruct((parts, PART, width), F32),
             jax.ShapeDtypeStruct((2, parts, PART, width), BF),
+            jax.ShapeDtypeStruct((2 * rows, width), BF),
+            jax.ShapeDtypeStruct((rows, width), BF),
+            jax.ShapeDtypeStruct(marks.shape, BF),
         ),
-        in_specs=[vmem_spec()] * 3,
-        out_specs=(vmem_spec(),) * 2,
-        scratch_shapes=line_scratch(parts, width) + [pltpu.SemaphoreType.DMA((2, parts))],
+        in_specs=[vmem_spec()] * 3 + [any_spec] * 4,
+        out_specs=(vmem_spec(),) * 2 + (any_spec,) * 3,
+        scratch_shapes=line_scratch(parts, width)
+        + [pltpu.SemaphoreType.DMA((2, parts)), pltpu.SemaphoreType.DMA((2, 3)), pltpu.SemaphoreType.DMA((3,))],
         compiler_params=pltpu.CompilerParams(
             collective_id=0, has_side_effects=True, vmem_limit_bytes=40 * MIB
         ),
         cost_estimate=LINK_COST,
         name="residual_norm",
-    )(part.reshape(parts, PART, width), block_input.reshape(parts, PART, width), gain[None])
-    return residual, normed.reshape(2 * rows, width)
+    )(
+        part.reshape(parts, PART, width), block_input.reshape(parts, PART, width), gain[None],
+        upstream, *peer_up, marks,
+    )
+    return residual, normed.reshape(2 * rows, width), *rest
 
 
 UNIT = 512
 
 
 def residual_grad_kernel(
-    back_ref, route_ref, res_ref, up_ref, gain_ref, wr_ref, marks_ref,
-    far_n, far_g, far_on, far_og, wg_hbm, wu_hbm, wd_hbm, pg_hbm, pu_hbm, pd_hbm,
-    grad_ref, low_ref, second_ref, route_out, sg_hbm, su_hbm, sd_hbm,
+    back_ref, route_ref, res_ref, up_ref, gain_ref, wr_ref, mix_ref,
+    far_n, far_on, far_g0, far_g1, far_og0, far_og1, far_m, far_om,
+    wg_hbm, wu_hbm, wd_hbm, pg_hbm, pu_hbm, pd_hbm,
+    grad_ref, low_ref, second_ref, route_out, mixed_ref, sg_hbm, su_hbm, sd_hbm,
     from_left, from_right, to_right, to_left, sems, peer_sems, arrived, terms,
     tokens_n, tokens_g, turned, kept_gates, gates_w, ups_w, downs_w, pair_g, pair_u, pair_d, ght, dgs, dus,
-    row_sems, weight_sems, pair_sems, out_sems,
+    row_sems, weight_sems, pair_sems, out_sems, mix_arrived, mix_sems, marks_ref,
 ):
     parts = back_ref.shape[1]
     core = lax.rem(lax.axis_index("dp"), 2)
@@ -762,12 +804,22 @@
 
     lax.fori_loop(0, parts, send, 0)
 
+    def send_mix(part, carry):
+        peer_copy(mix_ref.at[1, part], mix_arrived.at[part], mix_sems, part).start()
+        return carry
+
+    lax.fori_loop(0, parts, send_mix, 0)
     half = tokens_n.shape[0] // 2
-    row_copies = [
-        pltpu.make_async_copy(source, target.at[pl.ds(place * half, half), :], row_sems.at[kind, place])
-        for place, pair in enumerate(((far_n, far_g), (far_on, far_og)))
-        for kind, (source, target) in enumerate(zip(pair, (tokens_n, tokens_g)))
-    ]
+    quarter = half // 2
+    row_copies = []
+    for place, (rows, first, second, marks) in enumerate(((far_n, far_g0, far_g1, far_m), (far_on, far_og0, far_og1, far_om))):
+        at = place * half
+        row_copies += [
+            pltpu.make_async_copy(rows, tokens_n.at[pl.ds(at, half), :], row_sems.at[0, place]),
+            pltpu.make_async_copy(first, tokens_g.at[pl.ds(at, quarter), :], row_sems.at[1, place]),
+            pltpu.make_async_copy(second, tokens_g.at[pl.ds(at + quarter, quarter), :], row_sems.at[2, place]),
+            pltpu.make_async_copy(marks, marks_ref.at[pl.ds(at, half), :], row_sems.at[3, place]),
+        ]
     weight_copies, pair_copies, out_copies = [], [], []
     for at in range(groups):
         first = core * (groups * group) + at * group
@@ -798,7 +850,7 @@
                 for kind in range(3)
             ]
         )
-    for copy in row_copies[:2] + weight_copies[0] + row_copies[2:] + pair_copies[0] + weight_copies[1] + pair_copies[1]:
+    for copy in row_copies[:4] + weight_copies[0] + row_copies[4:] + pair_copies[0] + weight_copies[1] + pair_copies[1]:
         copy.start()
     terms[parts] = route_ref[...]
     second_ref[...] = jnp.zeros(second_ref.shape, F32)
@@ -818,12 +870,12 @@
 
                 @pl.when(unit == 0)
                 def _():
-                    for copy in row_copies[:2]:
+                    for copy in row_copies[:4]:
                         copy.wait()
 
                 @pl.when(unit == half // UNIT)
                 def _():
-                    for copy in row_copies[2:]:
+                    for copy in row_copies[4:]:
                         copy.wait()
 
             @pl.when(unit == chunks)
@@ -897,6 +949,13 @@
             grad_ref[part] = result
             low_ref[part] = result.astype(BF)
 
+        mixed = at - MIX_STEP
+
+        @pl.when((mixed >= 0) & (mixed < parts))
+        def _():
+            peer_copy(mix_ref.at[1, mixed], mix_arrived.at[mixed], mix_sems, mixed).wait_recv()
+            mixed_ref[mixed] = (mix_ref[0, mixed].astype(F32) + mix_arrived[mixed].astype(F32)).astype(BF)
+
         @pl.when((at >= FIRST_UNIT) & (at < FIRST_UNIT + groups * units))
         def _():
             compute(at - FIRST_UNIT)
@@ -909,6 +968,7 @@
 
     def wait(part, carry):
         peer_copy(back_ref.at[1, part], arrived.at[part], peer_sems, part).wait_send()
+        peer_copy(mix_ref.at[1, part], mix_arrived.at[part], mix_sems, part).wait_send()
         return carry
 
     lax.fori_loop(0, parts, wait, 0)
@@ -918,26 +978,28 @@
 
 
 FIRST_UNIT = 3
-
-
-def residual_gradient(back, route, residual, upstream, gain, w_router, marks, far_rows, w_gate, w_up, w_down, pairs):
+MIX_STEP = 10
+
+
+def residual_gradient(back, mix, route, residual, upstream, gain, w_router, far_rows, w_gate, w_up, w_down, pairs):
     rows, width = upstream.shape
     parts = rows // PART
     half, _, hid = pairs[0].shape
     groups = half // GROUP
     tokens = 2 * far_rows[0].shape[0]
     any_spec = pl.BlockSpec(memory_space=pl.ANY)
-    grad, low, second, route, *sums = pl.pallas_call(
+    grad, low, second, route, mixed, *sums = pl.pallas_call(
         residual_grad_kernel,
         out_shape=[
             jax.ShapeDtypeStruct((parts, PART, width), F32),
             jax.ShapeDtypeStruct((parts, PART, width), BF),
             jax.ShapeDtypeStruct((1, width), F32),
             jax.ShapeDtypeStruct(route.shape, F32),
+            jax.ShapeDtypeStruct((parts, PART, width), BF),
         ]
         + [jax.ShapeDtypeStruct(pair.shape, BF) for pair in pairs],
-        in_specs=[vmem_spec()] * 7 + [any_spec] * 10,
-        out_specs=[vmem_spec()] * 4 + [any_spec] * 3,
+        in_specs=[vmem_spec()] * 7 + [any_spec] * 14,
+        out_specs=[vmem_spec()] * 5 + [any_spec] * 3,
         scratch_shapes=line_scratch(parts + 1, width)
         + [
             pltpu.SemaphoreType.DMA((2, parts)),
@@ -956,10 +1018,13 @@
             pltpu.VMEM((GROUP * hid, tokens), BF),
             pltpu.VMEM((tokens, GROUP * hid), BF),
             pltpu.VMEM((tokens, GROUP * hid), BF),
-            pltpu.SemaphoreType.DMA((2, 2)),
+            pltpu.SemaphoreType.DMA((4, 2)),
             pltpu.SemaphoreType.DMA((groups, 3, GROUP)),
             pltpu.SemaphoreType.DMA((groups, 3)),
             pltpu.SemaphoreType.DMA((groups, 3)),
+            pltpu.VMEM((parts, PART, width), BF),
+            pltpu.SemaphoreType.DMA((2, parts)),
+            pltpu.VMEM((tokens, 2 * w_router.shape[1]), BF),
         ],
         compiler_params=pltpu.CompilerParams(
             collective_id=1, has_side_effects=True, vmem_limit_bytes=60 * MIB
@@ -968,58 +1033,230 @@
         name="residual_grad",
     )(
         back.reshape(2, parts, PART, width), route, residual, upstream.reshape(parts, PART, width), gain[None],
-        w_router, marks, *far_rows, w_gate, w_up, w_down, *pairs,
-    )
-    return grad, low.reshape(rows, width), second[0], route, sums
+        w_router, mix.reshape(2, parts, PART, width), *far_rows, w_gate, w_up, w_down, *pairs,
+    )
+    return grad, low.reshape(rows, width), second, route, mixed.reshape(rows, width), sums
 
 
 def input_grad_kernel(
-    part_ref, x_ref, res_grad_ref, gain_ref, grad_ref, first_ref, from_left, from_right, to_right, to_left, sems
+    x_ref, res_grad_ref, gain_ref, n_ref, dq_ref, dk_ref, dv_ref, wq_ref, wk_ref, wv_ref, cos_ref, sin_ref,
+    dwo_ref, route_ref, second_ref,
+    grad_ref, gq_ref, gk_ref, gv_ref, go_ref, gr_ref, gs_ref, gf_ref,
+    from_left, from_right, to_right, to_left, sems, terms, kv_in, kv_sems,
+    wide, wide_core, wide_x, wide_y, wide_back, tall, tall_core, tall_x, tall_y, tall_back, rows2, rows_core, rows_x, rows_y, sum_sems,
 ):
-    parts = part_ref.shape[0]
-    line = Line(parts, lambda at: part_ref[at], from_left, from_right, to_right, to_left, sems)
+    parts = x_ref.shape[0]
+    rows = n_ref.shape[0]
+    width = n_ref.shape[1]
+    core = lax.rem(lax.axis_index("dp"), 2)
+    peer = {"expert": 1 - lax.axis_index("expert")}
+    kv = dk_ref.shape[1]
+    queries = dq_ref.shape[1]
+    line = Line(parts + 1, lambda at: terms[at], from_left, from_right, to_right, to_left, sems)
     line.clear()
-    meet(line_partners())
-    first_ref[...] = jnp.zeros(first_ref.shape, F32)
+    meet(line_partners() + [(True, peer), (True, beside()), (True, other_core())])
+    key_copy = plain_copy(dk_ref.at[pl.ds(rows, rows), :], kv_in.at[0], kv_sems, 0, peer)
+    value_copy = plain_copy(dv_ref.at[pl.ds(rows, rows), :], kv_in.at[1], kv_sems, 1, peer)
+    key_copy.start()
+    value_copy.start()
+
+    half_tall = tall.shape[1]
+    outs = dwo_ref.shape[0]
+    for at in range(2):
+        low, high = at * half_tall, (at + 1) * half_tall
+        top = min(high, outs)
+        tall[at, : top - low, :] = dwo_ref[low:top, :].astype(BF)
+        if high > outs:
+            tall[at, outs - low :, :] = route_ref[...].astype(BF)
+
+    tall_steps = [
+        plain_copy(tall.at[1 - core], tall_core, sum_sems, 0, other_core()),
+        plain_copy(tall.at[core], tall_y, sum_sems, 1, peer),
+        plain_copy(tall.at[core], tall_x, sum_sems, 2, beside()),
+        plain_copy(tall.at[core], tall_back, sum_sems, 3, other_core()),
+    ]
+    wide_steps = [
+        plain_copy(wide.at[1 - core], wide_core, sum_sems, 4, other_core()),
+        plain_copy(wide.at[core], wide_x, sum_sems, 5, beside()),
+        plain_copy(wide.at[core], wide_y, sum_sems, 6, peer),
+        plain_copy(wide.at[core], wide_back, sum_sems, 7, other_core()),
+    ]
+    rows_steps = [
+        plain_copy(rows2, rows_core, sum_sems, 8, other_core()),
+        plain_copy(rows2, rows_y, sum_sems, 9, peer),
+        plain_copy(rows2, rows_x, sum_sems, 10, beside()),
+    ]
+    tall_steps[0].start()
+
+    def add(held, arrived):
+        held[...] = (held[...].astype(F32) + arrived[...].astype(F32)).astype(BF)
+
+    query_grad = dq_ref[...]
+    by_rows = (parts, rows // parts, width)
+    terms[pl.ds(0, parts)] = matmul_nt(query_grad, wq_ref[...]).reshape(by_rows)
+    turned = n_ref[...].T
+    query_part = matmul(turned, query_grad).astype(BF)
+    for at in range(2):
+        wide[at, :, :queries] = query_part[at * width // 2 : (at + 1) * width // 2, :]
+    key_copy.wait_recv()
+    value_copy.wait_recv()
+    rotated = dk_ref[:rows, :].astype(F32) + kv_in[0].astype(F32)
+    lane = lax.broadcasted_iota(jnp.int32, (1, kv), 1)
+    first = lane % HEAD_SIZE < HEAD_SIZE // 2
+    key_grad = (rotated * cos_ref[...] - turn(rotated, first) * sin_ref[...]).astype(BF)
+    value_grad = (dv_ref[:rows, :].astype(F32) + kv_in[1].astype(F32)).astype(BF)
+    more = matmul_nt(key_grad, wk_ref[...]) + matmul_nt(value_grad, wv_ref[...])
+    terms[pl.ds(0, parts)] += more.reshape(by_rows)
+    both_part = matmul(turned, jnp.concatenate([key_grad, value_grad], axis=1)).astype(BF)
+    for at in range(2):
+        wide[at, :, queries:] = both_part[at * width // 2 : (at + 1) * width // 2, :]
+    wide_steps[0].start()
+
+    def gain_part(at, total):
+        values = x_ref[at].astype(F32)
+        return total + jnp.sum(terms[at] * (values * scale_of(values)), axis=0, keepdims=True)
+
+    first_sum = lax.fori_loop(0, parts, gain_part, jnp.zeros((1, width), F32))
+    pad = jnp.zeros((rows2.shape[0] - 2, width), F32)
+    rows2[...] = jnp.concatenate([first_sum, second_ref[...], pad], axis=0).astype(BF)
+    rows_steps[0].start()
+
+    def exchange(at):
+        @pl.when(at == 0)
+        def _():
+            rows_steps[0].wait()
+            add(rows2, rows_core)
+            rows_steps[1].start()
+            tall_steps[0].wait()
+            add(tall.at[core], tall_core)
+            tall_steps[1].start()
+
+        @pl.when(at == 1)
+        def _():
+            wide_steps[0].wait()
+            add(wide.at[core], wide_core)
+
+        @pl.when(at == 2)
+        def _():
+            rows_steps[1].wait()
+            add(rows2, rows_y)
+            rows_steps[2].start()
+            wide_steps[1].start()
+
+        @pl.when(at == 5)
+        def _():
+            rows_steps[2].wait()
+            add(rows2, rows_x)
+            summed = rows2[...].astype(F32)
+            terms[parts] = jnp.concatenate([summed[:1, :], jnp.zeros((PART - 1, width), F32)], axis=0)
+            gs_ref[...] = summed[1:2, :]
+
+        @pl.when(at == 8)
+        def _():
+            tall_steps[1].wait()
+            add(tall.at[core], tall_y)
+            tall_steps[2].start()
+
+        @pl.when(at == 11)
+        def _():
+            wide_steps[1].wait()
+            add(wide.at[core], wide_x)
+            wide_steps[2].start()
+
+        @pl.when(at == 18)
+        def _():
+            tall_steps[2].wait()
+            add(tall.at[core], tall_x)
+            tall_steps[3].start()
+
+        @pl.when(at == 20)
+        def _():
+            wide_steps[2].wait()
+            add(wide.at[core], wide_y)
+            wide_steps[3].start()
 
     def body(at, carry):
+        exchange(at)
         line.step(at)
         part = at - LAG * line.last
 
-        @pl.when(part >= 0)
+        @pl.when((part >= 0) & (part < parts))
         def _():
             grad = line.total(part)
             values = x_ref[part].astype(F32)
             scale = scale_of(values)
             unit = values * scale
-            first_ref[...] += jnp.sum(grad * unit, axis=0, keepdims=True)
             grad_ref[part] = (res_grad_ref[part] + norm_back(grad, unit, scale, gain_ref[...])).astype(BF)
 
         return carry
 
-    lax.fori_loop(0, parts + LAG * line.last, body, 0)
+    lax.fori_loop(0, parts + 1 + LAG * line.last, body, 0)
+    gf_ref[...] = line.total(parts)[:1, :]
     line.drain()
-
-
-def input_gradient(first_part, block_input, residual_grad, gain):
+    key_copy.wait_send()
+    value_copy.wait_send()
+    tall_steps[3].wait()
+    for at in range(2):
+        low, high = at * half_tall, (at + 1) * half_tall
+        top = min(high, outs)
+        summed = jnp.where(core == at, tall[at].astype(F32), tall_back[...].astype(F32))
+        go_ref[low:top, :] = summed[: top - low, :]
+        if high > outs:
+            gr_ref[...] = summed[outs - low :, :]
+    wide_steps[3].wait()
+    for at in range(2):
+        span = slice(at * width // 2, (at + 1) * width // 2)
+        summed = jnp.where(core == at, wide[at].astype(F32), wide_back[...].astype(F32))
+        gq_ref[span, :] = summed[:, :queries]
+        gk_ref[span, :] = summed[:, queries : queries + kv]
+        gv_ref[span, :] = summed[:, queries + kv :]
+
+
+def input_gradient(
+    block_input, residual_grad, gain, normed, dq, dk, dv, w_query, key_weight, value_weight, cosines, sines,
+    grad_output, route, second,
+):
     rows, width = block_input.shape
     parts = rows // PART
-    grad, first = pl.pallas_call(
+    columns = w_query.shape[1] + 2 * key_weight.shape[1]
+    tall = (grad_output.shape[0] + route.shape[0]) // 2
+    wide_half = pltpu.VMEM((width // 2, columns), BF)
+    tall_half = pltpu.VMEM((tall, width), BF)
+    tile = pltpu.VMEM((16, width), BF)
+    grad, *rest = pl.pallas_call(
         input_grad_kernel,
         out_shape=(
             jax.ShapeDtypeStruct((parts, PART, width), BF),
+            jax.ShapeDtypeStruct(w_query.shape, F32),
+            jax.ShapeDtypeStruct(key_weight.shape, F32),
+            jax.ShapeDtypeStruct(value_weight.shape, F32),
+            jax.ShapeDtypeStruct(grad_output.shape, F32),
+            jax.ShapeDtypeStruct(route.shape, F32),
+            jax.ShapeDtypeStruct((1, width), F32),
             jax.ShapeDtypeStruct((1, width), F32),
         ),
-        in_specs=[vmem_spec()] * 4,
-        out_specs=(vmem_spec(),) * 2,
-        scratch_shapes=line_scratch(parts, width),
+        in_specs=[vmem_spec()] * 15,
+        out_specs=(vmem_spec(),) * 8,
+        scratch_shapes=line_scratch(parts + 1, width)
+        + [
+            pltpu.VMEM((parts + 1, PART, width), F32),
+            pltpu.VMEM((2, rows, key_weight.shape[1]), BF),
+            pltpu.SemaphoreType.DMA((2, 2)),
+            pltpu.VMEM((2, width // 2, columns), BF), wide_half, wide_half, wide_half, wide_half,
+            pltpu.VMEM((2, tall, width), BF), tall_half, tall_half, tall_half, tall_half,
+            tile, tile, tile, tile,
+            pltpu.SemaphoreType.DMA((2, 11)),
+        ],
         compiler_params=pltpu.CompilerParams(
-            collective_id=2, has_side_effects=True, vmem_limit_bytes=40 * MIB
+            collective_id=2, has_side_effects=True, vmem_limit_bytes=56 * MIB
         ),
         cost_estimate=LINK_COST,
         name="input_grad",
-    )(first_part.reshape(parts, PART, width), block_input.reshape(parts, PART, width), residual_grad, gain[None])
-    return grad.reshape(rows, width), first[0]
+    )(
+        block_input.reshape(parts, PART, width), residual_grad, gain[None], normed, dq, dk, dv,
+        w_query, key_weight, value_weight, cosines, sines, grad_output, route, second,
+    )
+    return grad.reshape(rows, width), *rest
 
 
 CHUNK = 512
@@ -1059,8 +1296,8 @@
 
 
 def expert_kernel(
-    n_ref, g_ref, marks_ref, wr_ref, n_hbm, wg_ref, wu_ref, wd_ref,
-    dwg_ref, dwu_ref, dwd_ref, mix_ref, back_ref, route_ref, far_ref, far_other_ref,
+    n_ref, g_ref, marks_ref, wr_ref, n_hbm, far_g0, far_g1, far_m, wg_ref, wu_ref, wd_ref,
+    dwg_ref, dwu_ref, dwd_ref, mix_ref, back_ref, route_ref, far_n, far_on, far_og0, far_og1, far_om,
     gates, kept_gates, gate_grads, mix, back, nt, wgs, wus, ght, dgs, dus,
     out_g, out_u, out_d, in_g, in_u, in_d, sems, far_sems,
 ):
@@ -1069,8 +1306,7 @@
     side = lax.axis_index("expert")
     dp = lax.axis_index("dp")
     core = lax.rem(dp, 2)
-    other = {"dp": dp + 1 - 2 * core}
-    beside = {"dp": lax.rem(dp + 2, 4)}
+    other = other_core()
     tokens, width = n_ref.shape
     experts_all = wr_ref.shape[1]
     group, _, hid = wg_ref.shape
@@ -1087,19 +1323,25 @@
             for kind, (source, target) in enumerate(((out_g, in_g), (out_u, in_u), (out_d, in_d)))
         ]
 
-    def far_copy(kind, source, target, device):
-        return pltpu.make_async_remote_copy(
-            src_ref=source, dst_ref=target, send_sem=far_sems.at[0, kind], recv_sem=far_sems.at[1, kind],
-            device_id=device, device_id_type=MESH,
-        )
-
-    cross = far_copy(0, n_hbm, far_ref, beside)
-    share = far_copy(1, far_ref, far_other_ref, other)
+    half = tokens // 2
+    cross = [
+        plain_copy(n_hbm.at[pl.ds(at * half, half), :], far_n.at[pl.ds(at * half, half), :], far_sems, at, beside())
+        for at in range(2)
+    ]
+    share = [
+        plain_copy(far_n.at[pl.ds(at * half, half), :], far_on.at[pl.ds(at * half, half), :], far_sems, 2 + at, other)
+        for at in range(2)
+    ]
+    early = [
+        plain_copy(source, target, far_sems, 4 + at, other)
+        for at, (source, target) in enumerate(((far_g0, far_og0), (far_g1, far_og1), (far_m, far_om)))
+    ]
 
     @pl.when(step == 0)
     def _():
-        meet([(True, other), (True, beside)])
-        cross.start()
+        meet([(True, other), (True, beside())])
+        for copy in cross + early:
+            copy.start()
 
         def start(at, carry):
             rows = pl.ds(pl.multiple_of(at * CHUNK, CHUNK), CHUNK)
@@ -1186,8 +1428,9 @@
 
     @pl.when(step == 2 * steps - 1)
     def _():
-        cross.wait_recv()
-        share.start()
+        for at in range(2):
+            cross[at].wait_recv()
+            share[at].start()
         route_ref[...] = jnp.zeros(route_ref.shape, F32)
 
         def finish(at, carry):
@@ -1201,11 +1444,13 @@
             return carry
 
         lax.fori_loop(0, chunks, finish, 0)
-        cross.wait_send()
-        share.wait()
-
-
-def experts(normed, upstream, marks, w_router, w_gate, w_up, w_down):
+        for copy in cross:
+            copy.wait_send()
+        for copy in share + early:
+            copy.wait()
+
+
+def experts(normed, upstream, marks, w_router, far_own, far_peer, far_marks, w_gate, w_up, w_down):
     tokens, width = normed.shape
     count, _, hid = w_gate.shape
     half = count // 2
@@ -1221,8 +1466,8 @@
     own = lambda step: (jnp.maximum(step - steps, 0), 0, 0)
     args = [normed, upstream, marks, w_router]
     specs = [pl.BlockSpec(array.shape, whole, pipeline_mode=once) for array in args]
-    args += [normed]
-    specs += [pl.BlockSpec(memory_space=pl.ANY)]
+    args += [normed, far_own, far_peer, far_marks]
+    specs += [pl.BlockSpec(memory_space=pl.ANY)] * 4
     up_block, down_block = (GROUP, width, hid), (GROUP, hid, width)
     specs += [pl.BlockSpec(up_block, picked), pl.BlockSpec(up_block, picked), pl.BlockSpec(down_block, picked)]
     gate_scratch = pltpu.VMEM((tokens, experts_all), F32)
@@ -1243,6 +1488,9 @@
             jax.ShapeDtypeStruct((experts_all, width), F32),
             jax.ShapeDtypeStruct((tokens, width), BF),
             jax.ShapeDtypeStruct((tokens, width), BF),
+            jax.ShapeDtypeStruct(far_own.shape, BF),
+            jax.ShapeDtypeStruct(far_peer.shape, BF),
+            jax.ShapeDtypeStruct(far_marks.shape, BF),
         ],
         grid=(2 * steps,),
         in_specs=specs,
@@ -1253,9 +1501,8 @@
             pl.BlockSpec((tokens, width), whole, pipeline_mode=once),
             pl.BlockSpec((tokens, width), whole, pipeline_mode=once),
             pl.BlockSpec((experts_all, width), whole, pipeline_mode=once),
-            pl.BlockSpec(memory_space=pl.ANY),
-            pl.BlockSpec(memory_space=pl.ANY),
-        ],
+        ]
+        + [pl.BlockSpec(memory_space=pl.ANY)] * 5,
         scratch_shapes=[
             gate_scratch, gate_scratch, gate_scratch, rows_scratch, rows_scratch,
             pltpu.VMEM((width, tokens), BF),
@@ -1267,7 +1514,7 @@
         ]
         + swap_scratch
         + swap_scratch
-        + [pltpu.SemaphoreType.DMA((2, 3, steps)), pltpu.SemaphoreType.DMA((2, 2))],
+        + [pltpu.SemaphoreType.DMA((2, 3, steps)), pltpu.SemaphoreType.DMA((2, 7))],
         compiler_params=pltpu.CompilerParams(
             dimension_semantics=("arbitrary",), collective_id=3, has_side_effects=True, vmem_limit_bytes=60 * MIB
         ),
@@ -1341,11 +1588,8 @@
     kept = jnp.sum((hits & (slot_index >= 0)[:, :, None]).astype(F32), axis=1)
     marks = jnp.concatenate([chosen, kept], axis=1).astype(BF)
     marks = jnp.concatenate([marks, swap(marks, "expert", 1)], axis=0)
-    far_marks = swap(marks, "dp", 2)
-    far_marks = jnp.concatenate([far_marks, swap(far_marks, "dp", 1)], axis=0)
-    upstream_all = jnp.concatenate([upstream, swap(upstream, "expert", 1)], axis=0)
-    far_up = swap(upstream_all, "dp", 2)
-    far_other_up = swap(far_up, "dp", 1)
+    far_up = swap(upstream, "dp", 2)
+    peer_up = [swap(upstream[: rows // 2], "expert", 1)]
 
     positions = side * rows + jnp.arange(rows, dtype=jnp.int32)
     cosine_table, sine_table = rope_tables(positions)
@@ -1363,58 +1607,45 @@
     ).astype(BF).reshape(rows, local_kv * HEAD_SIZE)
     value_low = matmul(first_normed, value_weight).astype(BF)
     both = jnp.concatenate([key_rot, value_low], axis=1)
+    later, both = lax.optimization_barrier((upstream[rows // 2 :], both))
+    peer_up.append(swap(later, "expert", 1))
     both = jnp.concatenate([both, swap(both, "expert", 1)], axis=0)
     keys, values = both[:, : local_kv * HEAD_SIZE], both[:, local_kv * HEAD_SIZE :]
 
     attended, lse, part = attend(scal, query_rot, keys, values, w_output)
-    residual, normed_all = residual_norm(part, block_input, second_gain)
-
-    normed_all, far_up, far_other_up, far_marks = lax.optimization_barrier(
-        (normed_all, far_up, far_other_up, far_marks)
-    )
-    dwg, dwu, dwd, mix, back, route, far_normed, far_other_normed = experts(
-        normed_all, upstream_all, marks, w_router, w_gate, w_up, w_down
-    )
-    residual_grad, residual_low, grad_second, route, sums = residual_gradient(
-        back, route, residual, upstream, second_gain, w_router, far_marks,
-        (far_normed, far_up, far_other_normed, far_other_up), w_gate, w_up, w_down, (dwg, dwu, dwd),
-    )
+    part, far_up = lax.optimization_barrier((part, far_up))
+    residual, normed_all, upstream_all, far_peer_up, far_marks = residual_norm(
+        part, block_input, second_gain, upstream, peer_up, marks
+    )
+    dwg, dwu, dwd, mix, back, route, *far = experts(
+        normed_all, upstream_all, marks, w_router, far_up, far_peer_up, far_marks, w_gate, w_up, w_down
+    )
+    far_normed, far_other_normed, far_other_up, far_other_peer_up, far_other_marks = far
+    residual_grad, residual_low, grad_second, route, mixed, sums = residual_gradient(
+        back, mix, route, residual, upstream, second_gain, w_router,
+        (
+            far_normed, far_other_normed, far_up, far_peer_up, far_other_up, far_other_peer_up,
+            far_marks, far_other_marks,
+        ),
+        w_gate, w_up, w_down, (dwg, dwu, dwd),
+    )
+    mixed = lax.psum_scatter(mixed, "tensor", scatter_dimension=1, tiled=True)
 
     query_grad, dk, dv, grad_output = attend_back(
         scal, query_rot, keys, values, lse, attended, residual_low, w_output, cosines, sines
     )
-    dboth = jnp.concatenate([dk, dv], axis=1)
-    dboth = dboth[:rows].astype(F32) + swap(dboth[rows:], "expert", 1).astype(F32)
-    key_back, value_back = dboth[:, : local_kv * HEAD_SIZE], dboth[:, local_kv * HEAD_SIZE :]
-    key_grad = unrotate(
-        key_back.reshape(rows, local_kv, HEAD_SIZE), cosine_table, sine_table
-    ).astype(BF).reshape(rows, local_kv * HEAD_SIZE)
-    value_grad = value_back.astype(BF)
-    grad_query = matmul_tn(first_normed, query_grad)
-    grad_key = matmul_tn(first_normed, key_grad)
-    grad_value = matmul_tn(first_normed, value_grad)
-    first_part = (
-        matmul_nt(query_grad, w_query) + matmul_nt(key_grad, key_weight) + matmul_nt(value_grad, value_weight)
-    )
-    grad_input, grad_first = input_gradient(first_part, block_input, residual_grad, first_gain)
-    mix, grad_input = lax.optimization_barrier((mix, grad_input))
-    mixed = lax.psum_scatter(mix, "tensor", scatter_dimension=1, tiled=True)
-    mixed = mixed[:rows].astype(F32) + swap(mixed[rows:], "expert", 1).astype(F32)
+    grad_input, grad_query, grad_key, grad_value, grad_output, grad_router, grad_second, grad_first = input_gradient(
+        block_input, residual_grad, first_gain, first_normed, query_grad, dk, dv, w_query, key_weight, value_weight,
+        cosines, sines, grad_output, route, grad_second,
+    )
     block_output = (
-        lax.dynamic_slice_in_dim(residual.reshape(rows, width), feature_start, width // 4, 1) + mixed
+        lax.dynamic_slice_in_dim(residual.reshape(rows, width), feature_start, width // 4, 1) + mixed.astype(F32)
     ).astype(BF)
-
     core_row = core[None].astype(jnp.int32)
     expert_sums = [widen(core_row, item, swap(item, "dp", 1)) for item in sums]
-    early = lax.psum((grad_output.astype(BF), route.astype(BF), grad_second.astype(BF)), ("dp", "expert"))
-    late = lax.psum(
-        (grad_query.astype(BF), grad_key.astype(BF), grad_value.astype(BF), grad_first.astype(BF)), ("dp", "expert")
-    )
-    early = [item.astype(F32) for item in early]
-    late = [item.astype(F32) for item in late]
     return (
-        block_output, grad_input, late[3], late[0], late[1], late[2], early[0], early[2], early[1].T,
-        expert_sums[0], expert_sums[1], expert_sums[2],
+        block_output, grad_input, grad_first[0], grad_query, grad_key, grad_value, grad_output, grad_second[0],
+        grad_router.T, expert_sums[0], expert_sums[1], expert_sums[2],
     )
 
 

time: 446 us -> 342 us (0.77)
  waiting for transfers between devices: 102 us -> 22.9 us
  Pallas kernels: 246 us -> 265 us
  blocking collectives: 16.9 us -> 0 us
  other arithmetic: 21.3 us -> 4.85 us
  matrix products: 10.7 us -> 1.4 us
    ppermute x12 -> x8, waiting for transfers between devices: 63.2 us -> 22.9 us  [swap(): return lax.ppermute(array, axis, [(at, at ^ bit) for at in range(size)])]
    reduce_scatter x1, waiting for transfers between devices: 30.9 us -> 0.01 us  [fast_device(): mixed = lax.psum_scatter(mixed, 'tensor', scatter_dimension=1, tiled=True)]
    pallas_call x1, Pallas kernels: 30.8 us -> 54.9 us  [input_gradient(): pl.pallas_call(input_grad_kernel, out_shape=(jax.ShapeDtypeStruct((parts,...]
    psum x1 -> x0, blocking collectives: 16.9 us -> none  [fast_device(): lax.psum((grad_query.astype(BF), grad_key.astype(BF), grad_value.astype(B...]
    dot_general x6 -> x0, matrix products: 9.05 us -> none  [the longest x3 5.42 us: matmul_tn(): lax.dot_general(left, right, (((0,), (0,)), ((), ())), preferred_element_...]
    convert_element_type x9 -> x1, other arithmetic: 9.26 us -> 0.31 us  [fast_device(): first_normed = (first_unit * first_gain).astype(BF)]
    psum x1 -> x0, waiting for transfers between devices: 7.83 us -> none  [fast_device(): lax.psum((grad_query.astype(BF), grad_key.astype(BF), grad_value.astype(B...]
    pallas_call x3, Pallas kernels: 18.5 us -> 13.5 us  [widen(): pl.pallas_call(widen_kernel, out_shape=jax.ShapeDtypeStruct((2 * half, hi...]
  transfers between devices with their start and end apart: 14 -> 9, of which waited for: 5 -> 1; matrix products, arithmetic and copies ran while one was open for 9% -> 4% of each run, Pallas kernels for 14% -> 26%
where the time goes in v5:
time: 342 us; the launch traced here: 340 us
  Pallas kernels  265 us (77%)
  local copies, waits for them, and re-layouts  23.6 us (7%)
  waiting for transfers between devices  22.9 us (7%)
  between operations  14.7 us (4%)
  starting transfers between devices  7.74 us (2%)
  other arithmetic  4.85 us (1%)
    pallas_call x1, Pallas kernels, experts(): pl.pallas_call(expert_kernel, out_shape=[jax.ShapeDtypeStruct((half, widt...  73.5 us
    pallas_call x1, Pallas kernels, residual_gradient(): pl.pallas_call(residual_grad_kernel, out_shape=[jax.ShapeDtypeStruct((par...  66.8 us
    pallas_call x1, Pallas kernels, input_gradient(): pl.pallas_call(input_grad_kernel, out_shape=(jax.ShapeDtypeStruct((parts,...  54.9 us
    pallas_call x1, Pallas kernels, residual_norm(): pl.pallas_call(residual_kernel, out_shape=(jax.ShapeDtypeStruct((parts, P...  37.4 us
    ppermute x8, waiting for transfers between devices, swap(): return lax.ppermute(array, axis, [(at, at ^ bit) for at in range(size)])  22.9 us
    unnamed x86, local copies, waits for them, and re-layouts  16.3 us
    pallas_call x3, Pallas kernels, widen(): pl.pallas_call(widen_kernel, out_shape=jax.ShapeDtypeStruct((2 * half, hi...  13.5 us
    pallas_call x1, Pallas kernels, attend_back(): pl.pallas_call(attend_back_kernel, out_shape=(jax.ShapeDtypeStruct((rows,...  12.6 us
  transfers between devices with their start and end apart: 9, of which 1 were waited for; matrix products, arithmetic and copies ran while one was open for 4% of the time, Pallas kernels for 26%

profile of v5, /device:TPU:0, one launch (start us, length us, event | category | flops | bytes accessed | tf_op | source)
XLA Modules:
  0.0 340.3 jit_solution(17181665079270968963)
XLA Ops:
  7.2 3.0 collective-permute-start.1
  10.3 2.2 fusion.4
  15.6 1.5 collective-permute-start
  17.7 1.5 collective-permute-start.3
  21.4 1.7 constant_dynamic-update-slice_fusion.1
  26.0 22.9 %collective-permute-done.4 = bf16[512,64]{1,0:T(8,128)(2,1)S(1)} collective-permute-done((bf16[512,64]{1,0:T(8,128)(2,1)}, bf16[512,64]{1,0:T(8,128)(2,1)S(1)}, u32[]{:S(2)}, u32[]{:S(2)}) %collective-permute-start.4) | collective-permute-done | bytes 65568 | tf_op jit(solution)/shard_map/ppermute | solution.py:1569
  49.0 1.8 constant_dynamic-update-slice_fusion
  50.8 1.1 fusion.5
  51.9 6.3 %attend.1 = (bf16[512,256]{1,0:T(8,128)(2,1)S(1)}, f32[512,128]{1,0:T(8,128)S(1)}, bf16[512,1024]{1,0:T(8,128)(2,1)S(1)}) custom-call(s32[3]{0:T(128)S(1)} %pad_add_fusion.scal_ref, bf16[512,256]{1,0:T(8,128)(2,1)S(1)} %copy.62.q_ref, bf16[1024,128]{1,0:T(8,128)(2,1)S(1)} %get-tuple-element.105.k_ref, bf16[1024,128]{1,0:T(8,128)(2,1)S(1)} %get-tuple-element.104.v_ref, ...), custom_call_target="tpu_custom_call" | custom-call | tf_op jit(solution)/shard_map/attend/pallas_call | solution.py:488
  59.7 37.4 %residual_norm.1 = (f32[16,32,1024]{2,1,0:T(8,128)S(1)}, bf16[2,16,32,1024]{3,2,1,0:T(8,128)(2,1)S(1)}, bf16[1024,1024]{1,0:T(8,128)(2,1)S(1)}, bf16[512,1024]{1,0:T(8,128)(2,1)S(1)}, bf16[1024,64]{1,0:T(8,128)(2,1)S(1)}) custom-call(bf16[16,32,1024]{2,1,0:T(8,128)(2,1)S(1)} %bitcast.34, bf16[16,32,1024]{2,1,0:T(8,128)(2,1)S(1)} %bitcast.31, ...), custom_call_target="tpu_custom_call" | custom-call | flops 40000000000 | bytes 10000000 | tf_op jit(solution)/shard_map/residual_norm/pallas_call | solution.py:755
  97.1 1.3 copy-done.12
  98.4 1.3 copy-done.15
  99.7 1.3 copy-done.16
  102.7 73.5 %experts.1 = (bf16[8,1024,128]{2,1,0:T(8,128)(2,1)}, bf16[8,1024,128]{2,1,0:T(8,128)(2,1)}, bf16[8,128,1024]{2,1,0:T(8,128)(2,1)}, bf16[1024,1024]{1,0:T(8,128)(...) custom-call(bf16[1024,1024]{1,0:T(8,128)(2,1)} %bitcast.37, ...), custom_call_target="tpu_custom_call" | custom-call | flops 38654705664 | bytes 25165824 | tf_op jit(solution)/shard_map/experts/pallas_call | solution.py:1480
  176.2 66.8 %residual_grad.1 = (f32[16,32,1024]{2,1,0:T(8,128)}, bf16[16,32,1024]{2,1,0:T(8,128)(2,1)}, f32[1,1024]{1,0:T(1,128)}, f32[32,1024]{1,0:T(8,128)}, bf16[16,32,10...) custom-call(bf16[2,16,32,1024]{3,2,1,0:T(8,128)(2,1)} %bitcast.54, ...), custom_call_target="tpu_custom_call" | custom-call | flops 40000000000 | bytes 10000000 | tf_op jit(solution)/shard_map/residual_grad/pallas_call | solution.py:991
  243.8 12.6 %attend_back.1 = (bf16[512,256]{1,0:T(8,128)(2,1)}, bf16[1024,128]{1,0:T(8,128)(2,1)}, bf16[1024,128]{1,0:T(8,128)(2,1)}, f32[256,1024]{1,0:T(8,128)}) custom-call(s32[3]{0:T(128)} %copy-done.13, bf16[512,256]{1,0:T(8,128)(2,1)} %copy-done.1, bf16[1024,128]{1,0:T(8,128)(2,1)} %copy-done.3, bf16[1024,128]{1,0:T(8,128)(2,1)} %copy-done.2, ...), custom_call_target="tpu_custom_call" | custom-call | tf_op jit(solution)/shard_map/attend_back/pallas_call | solution.py:556
  256.4 54.9 %input_grad.1 = (bf16[16,32,1024]{2,1,0:T(8,128)(2,1)}, f32[1024,256]{1,0:T(8,128)}, f32[1024,128]{1,0:T(8,128)}, f32[1024,128]{1,0:T(8,128)}, f32[256,1024]{1,0...) custom-call(bf16[16,32,1024]{2,1,0:T(8,128)(2,1)} %bitcast.30, ...), custom_call_target="tpu_custom_call" | custom-call | flops 40000000000 | bytes 10000000 | tf_op jit(solution)/shard_map/input_grad/pallas_call | solution.py:1226
  311.3 6.2 %widen.3 = f32[16,1024,128]{2,1,0:T(8,128)} custom-call(s32[1]{0:T(128)} %bitcast.23.core_ref, bf16[8,1024,128]{2,1,0:T(8,128)(2,1)S(1)} %copy-done.6, bf16[8,1024,128]{2,1,0:T(8,128)(2,1)} %collective-permute-done.5.other_ref), custom_call_target="tpu_custom_call" | custom-call | flops 2097152 | bytes 12582912 | tf_op jit(solution)/shard_map/widen/pallas_call | solution.py:1547
  317.6 3.7 %widen.4 = f32[16,1024,128]{2,1,0:T(8,128)} custom-call(s32[1]{0:T(128)} %bitcast.23.core_ref, bf16[8,1024,128]{2,1,0:T(8,128)(2,1)S(1)} %copy-done.5, bf16[8,1024,128]{2,1,0:T(8,128)(2,1)S(1)} %collective-permute-done.6.other_ref), custom_call_target="tpu_custom_call" | custom-call | flops 2097152 | bytes 12582912 | tf_op jit(solution)/shard_map/widen/pallas_call | solution.py:1547
  321.2 3.7 %widen.5 = f32[16,128,1024]{2,1,0:T(8,128)} custom-call(s32[1]{0:T(128)} %bitcast.23.core_ref, bf16[8,128,1024]{2,1,0:T(8,128)(2,1)S(1)} %copy-done.4, bf16[8,128,1024]{2,1,0:T(8,128)(2,1)S(1)} %collective-permute-done.7.other_ref), custom_call_target="tpu_custom_call" | custom-call | flops 2097152 | bytes 12582912 | tf_op jit(solution)/shard_map/widen/pallas_call | solution.py:1547
  324.9 2.0 add_convert_fusion
  326.9 1.0 copy.82
  328.4 1.0 copy.84
  331.0 1.0 copy.87
  (121 shorter events, 16.0 us)
Async XLA Ops:
  7.2 317.7 %reduce-scatter.2.cloned.1.call-start = ((), (), s32[]{:S(2)}) async-start(), calls=%async_computation.1 | async-start | bytes 1310720 | tf_op jit(solution)/shard_map/reduce_scatter | solution.py:1632
  7.2 52.4 %collective-permute-start.1 = (bf16[512,1024]{1,0:T(8,128)(2,1)}, bf16[512,1024]{1,0:T(8,128)(2,1)}, u32[]{:S(2)}, u32[]{:S(2)}) collective-permute-start(bf16[512,1024]{1,0:T(8,128)(2,1)} %up_own.1), channel_id=1, source_target_pairs={{0,16},{8,24},{16,0},{24,8},{1,17},{9,25},{17,1},{25,9},{2,18},{10... | collective-permute-start | bytes 3145736 | tf_op jit(solution)/shard_map/ppermute | solution.py:1569
  13.4 7.4 %copy-start.19 = (bf16[512,1024]{1,0:T(8,128)(2,1)}, bf16[512,1024]{1,0:T(8,128)(2,1)S(1)}, u32[]{:S(2)}) copy-start(bf16[512,1024]{1,0:T(8,128)(2,1)S(1)} %fusion.2.n_ref) | copy-start | bytes 3145732
  13.5 5.7 %copy-start.32 = (s32[512,8]{0,1:T(8,128)S(1)}, s32[512,8]{0,1:T(8,128)}, u32[]{:S(2)}) copy-start(s32[512,8]{0,1:T(8,128)} %param.27) | copy-start | bytes 49156
  13.5 5.8 %copy-start.33 = (s32[512,8]{0,1:T(8,128)S(1)}, s32[512,8]{0,1:T(8,128)}, u32[]{:S(2)}) copy-start(s32[512,8]{0,1:T(8,128)} %param.26) | copy-start | bytes 49156
  13.9 7.0 %copy-start.27 = (bf16[1024,256]{1,0:T(8,128)(2,1)S(1)}, bf16[1024,256]{1,0:T(8,128)(2,1)}, u32[]{:S(2)}) copy-start(bf16[1024,256]{1,0:T(8,128)(2,1)} %wq_ref.1) | copy-start | bytes 1572868
  15.6 33.4 %collective-permute-start = (bf16[512,256]{1,0:T(8,128)(2,1)}, bf16[512,256]{1,0:T(8,128)(2,1)}, u32[]{:S(2)}, u32[]{:S(2)}) collective-permute-start(bf16[512,256]{1,0:T(8,128)(2,1)} %pad_maximum_fusion.1), channel_id=1, source_target_pairs={{0,4},{4,0},{1,5},{5,1},{2,6},{6,2},{3,7},{7,3},{8,12},{12,8},{9,1... | collective-permute-start | bytes 786440 | tf_op jit(solution)/shard_map/ppermute | solution.py:1569
  17.2 42.5 %collective-permute-start.2 = (bf16[256,1024]{1,0:T(8,128)(2,1)}, bf16[256,1024]{1,0:T(8,128)(2,1)}, u32[]{:S(2)}, u32[]{:S(2)}) collective-permute-start(bf16[256,1024]{1,0:T(8,128)(2,1)} %get-tuple-element.100), channel_id=1, source_target_pairs={{0,4},{4,0},{1,5},{5,1},{2,6},{6,2},{3,7},{7,3},{8,12},{12,8},{9,1... | collective-permute-start | bytes 1572872 | tf_op jit(solution)/shard_map/ppermute | solution.py:1569
  17.7 42.0 %collective-permute-start.3 = (bf16[256,1024]{1,0:T(8,128)(2,1)}, bf16[256,1024]{1,0:T(8,128)(2,1)}, u32[]{:S(2)}, u32[]{:S(2)}) collective-permute-start(bf16[256,1024]{1,0:T(8,128)(2,1)} %get-tuple-element.58), channel_id=1, source_target_pairs={{0,4},{4,0},{1,5},{5,1},{2,6},{6,2},{3,7},{7,3},{8,12},{12,8},{9,1... | collective-permute-start | bytes 1572872 | tf_op jit(solution)/shard_map/ppermute | solution.py:1569
  20.4 28.5 %collective-permute-start.4 = (bf16[512,64]{1,0:T(8,128)(2,1)}, bf16[512,64]{1,0:T(8,128)(2,1)S(1)}, u32[]{:S(2)}, u32[]{:S(2)}) collective-permute-start(bf16[512,64]{1,0:T(8,128)(2,1)} %pad_maximum_fusion.4), channel_id=1, source_target_pairs={{0,4},{4,0},{1,5},{5,1},{2,6},{6,2},{3,7},{7,3},{8,12},{12,8},{9,1... | collective-permute-start | bytes 196616 | tf_op jit(solution)/shard_map/ppermute | solution.py:1569
  23.2 25.7 %copy-start.21 = (bf16[512,32]{1,0:T(8,128)(2,1)S(1)}, bf16[512,32]{1,0:T(8,128)(2,1)}, u32[]{:S(2)}) copy-start(bf16[512,32]{1,0:T(8,128)(2,1)} %copy-done.20) | copy-start | bytes 98308
  23.3 28.6 %copy-start.13 = (s32[3]{0:T(128)}, s32[3]{0:T(128)S(1)}, u32[]{:S(2)}) copy-start(s32[3]{0:T(128)S(1)} %pad_add_fusion.scal_ref) | copy-start | bytes 40
  23.4 28.5 %copy-start.1 = (bf16[512,256]{1,0:T(8,128)(2,1)}, bf16[512,256]{1,0:T(8,128)(2,1)S(1)}, u32[]{:S(2)}) copy-start(bf16[512,256]{1,0:T(8,128)(2,1)S(1)} %copy.62.q_ref) | copy-start | bytes 786436
  23.4 28.5 %copy-start.7 = (bf16[256,1024]{1,0:T(8,128)(2,1)S(1)}, bf16[256,1024]{1,0:T(8,128)(2,1)}, u32[]{:S(2)}) copy-start(bf16[256,1024]{1,0:T(8,128)(2,1)} %wo_ref.3) | copy-start | bytes 1572868
  25.2 34.5 %copy-start.8 = (bf16[512,1024]{1,0:T(8,128)(2,1)S(1)}, bf16[512,1024]{1,0:T(8,128)(2,1)}, u32[]{:S(2)}) copy-start(bf16[512,1024]{1,0:T(8,128)(2,1)} %up_own.1) | copy-start | bytes 3145732
  25.2 34.5 %copy-start.14 = (f32[1024]{0:T(1024)S(1)}, f32[1024]{0:T(1024)}, u32[]{:S(2)}) copy-start(f32[1024]{0:T(1024)} %param.21) | copy-start | bytes 12292
  49.0 48.0 %copy-start.11 = (bf16[1024,64]{1,0:T(8,128)(2,1)}, bf16[1024,64]{1,0:T(8,128)(2,1)S(1)}, u32[]{:S(2)}) copy-start(bf16[1024,64]{1,0:T(8,128)(2,1)S(1)} %pad_maximum_fusion.2.marks_ref) | copy-start | bytes 393220
  51.9 45.2 %copy-start.2 = (bf16[1024,128]{1,0:T(8,128)(2,1)}, bf16[1024,128]{1,0:T(8,128)(2,1)S(1)}, u32[]{:S(2)}) copy-start(bf16[1024,128]{1,0:T(8,128)(2,1)S(1)} %get-tuple-element.104.v_ref) | copy-start | bytes 786436
  51.9 45.2 %copy-start.3 = (bf16[1024,128]{1,0:T(8,128)(2,1)}, bf16[1024,128]{1,0:T(8,128)(2,1)S(1)}, u32[]{:S(2)}) copy-start(bf16[1024,128]{1,0:T(8,128)(2,1)S(1)} %get-tuple-element.105.k_ref) | copy-start | bytes 786436
  243.1 68.2 %collective-permute-start.5 = (bf16[8,1024,128]{2,1,0:T(8,128)(2,1)}, bf16[8,1024,128]{2,1,0:T(8,128)(2,1)}, u32[]{:S(2)}, u32[]{:S(2)}) collective-permute-start(bf16[8,1024,128]{2,1,0:T(8,128)(2,1)} %get-tuple-element.95.mine_ref), channel_id=1, source_target_pairs={{0,8},{8,0},{16,24},{24,16},{1,9},{9,1},{17,25},{25,17},{2,10},{10... | collective-permute-start | bytes 6291464 | tf_op jit(solution)/shard_map/ppermute | solution.py:1569
  243.2 74.4 %collective-permute-start.6 = (bf16[8,1024,128]{2,1,0:T(8,128)(2,1)}, bf16[8,1024,128]{2,1,0:T(8,128)(2,1)S(1)}, u32[]{:S(2)}, u32[]{:S(2)}) collective-permute-start(bf16[8,1024,128]{2,1,0:T(8,128)(2,1)} %get-tuple-element.96.mine_ref), channel_id=1, source_target_pairs={{0,8},{8,0},{16,24},{24,16},{1,9},{9,1},{17,25},{25,17},{2,10},{10... | collective-permute-start | bytes 6291464 | tf_op jit(solution)/shard_map/ppermute | solution.py:1569
  243.7 77.5 %collective-permute-start.7 = (bf16[8,128,1024]{2,1,0:T(8,128)(2,1)}, bf16[8,128,1024]{2,1,0:T(8,128)(2,1)S(1)}, u32[]{:S(2)}, u32[]{:S(2)}) collective-permute-start(bf16[8,128,1024]{2,1,0:T(8,128)(2,1)} %get-tuple-element.97.mine_ref), channel_id=1, source_target_pairs={{0,8},{8,0},{16,24},{24,16},{1,9},{9,1},{17,25},{25,17},{2,10},{10... | collective-permute-start | bytes 6291464 | tf_op jit(solution)/shard_map/ppermute | solution.py:1569
  256.4 54.9 %copy-start.6 = (bf16[8,1024,128]{2,1,0:T(8,128)(2,1)S(1)}, bf16[8,1024,128]{2,1,0:T(8,128)(2,1)}, u32[]{:S(2)}) copy-start(bf16[8,1024,128]{2,1,0:T(8,128)(2,1)} %get-tuple-element.95.mine_ref) | copy-start | bytes 6291460
  311.3 6.2 %copy-start.5 = (bf16[8,1024,128]{2,1,0:T(8,128)(2,1)S(1)}, bf16[8,1024,128]{2,1,0:T(8,128)(2,1)}, u32[]{:S(2)}) copy-start(bf16[8,1024,128]{2,1,0:T(8,128)(2,1)} %get-tuple-element.96.mine_ref) | copy-start | bytes 6291460
  (23 other events, 58.8 us)
Sparse Core Ops, SparseCore 0:
  243.2 26.1 reduce-scatter.1

commit v6 on v5

--- a/solution.py
+++ b/solution.py
@@ -439,9 +439,9 @@
     return pl.BlockSpec(memory_space=pltpu.SMEM)
 
 
-def allowed_pairs(scal_ref, rows):
-    side = scal_ref[0]
-    here = lax.broadcasted_iota(jnp.int32, (rows, 1), 0)
+def allowed_pairs(offsets_ref, rows, start, count):
+    side = lax.axis_index("expert")
+    here = start + lax.broadcasted_iota(jnp.int32, (count, 1), 0)
     keys = lax.broadcasted_iota(jnp.int32, (1, 2 * rows), 1)
     query_place = side * rows + here
     key_place = jnp.where(keys < rows, side * rows + keys, (1 - side) * rows + keys - rows)
@@ -450,53 +450,13 @@
     def piece(places):
         window = places // span
         within = places - window * span
-        start = jnp.where(window == 0, scal_ref[1], scal_ref[2])
+        start = jnp.where(window == 0, offsets_ref[0, 0], offsets_ref[0, 1])
         inside = (within >= start) & (within < start + PIC)
         return jnp.where(inside, window, -1)
 
     query_piece = piece(query_place)
     key_piece = piece(key_place)
     return (key_place <= query_place) | ((key_piece == query_piece) & (query_piece >= 0))
-
-
-def attend_kernel(scal_ref, q_ref, k_ref, v_ref, wo_ref, att_ref, lse_ref, part_ref):
-    rows = q_ref.shape[0]
-    heads = q_ref.shape[1] // HEAD_SIZE
-    sharing = q_ref.shape[1] // k_ref.shape[1]
-    allowed = allowed_pairs(scal_ref, rows)
-    pieces = []
-    for head in range(heads):
-        at = head * HEAD_SIZE
-        kv = head // sharing * HEAD_SIZE
-        query = q_ref[:, at : at + HEAD_SIZE]
-        key = k_ref[:, kv : kv + HEAD_SIZE]
-        value = v_ref[:, kv : kv + HEAD_SIZE]
-        scores = jnp.where(allowed, matmul_nt(query, key) * (HEAD_SIZE**-0.5), masked_score)
-        peak = jnp.max(scores, axis=1, keepdims=True)
-        weights = jnp.exp(scores - peak)
-        total = jnp.sum(weights, axis=1, keepdims=True)
-        probs = (weights * (1.0 / total)).astype(BF)
-        pieces.append(matmul(probs, value))
-        lse_ref[:, head : head + 1] = peak + jnp.log(total)
-    attended = jnp.concatenate(pieces, axis=1).astype(BF)
-    att_ref[...] = attended
-    part_ref[...] = matmul(attended, wo_ref[...]).astype(BF)
-
-
-def attend(scal, query, key, value, w_output):
-    rows, wide = query.shape
-    return pl.pallas_call(
-        attend_kernel,
-        out_shape=(
-            jax.ShapeDtypeStruct((rows, wide), BF),
-            jax.ShapeDtypeStruct((rows, 128), F32),
-            jax.ShapeDtypeStruct((rows, w_output.shape[1]), BF),
-        ),
-        in_specs=[smem_spec()] + [vmem_spec()] * 4,
-        out_specs=(vmem_spec(),) * 3,
-        compiler_params=pltpu.CompilerParams(vmem_limit_bytes=48 * MIB),
-        name="attend",
-    )(scal, query, key, value, w_output)
 
 
 def turn(values, first):
@@ -518,7 +478,7 @@
     low = low_ref[...]
     dwo_ref[...] = matmul_tn(att_ref[...], low)
     att_grad = matmul_nt(low, wo_ref[...]).astype(BF)
-    allowed = allowed_pairs(scal_ref, rows)
+    allowed = allowed_pairs(scal_ref, rows, 0, rows)
     query_parts, key_parts, value_parts = [], [], []
     for head in range(heads):
         at = head * HEAD_SIZE
@@ -699,82 +659,166 @@
     return {"dp": place + 1 - 2 * lax.rem(place, 2)}
 
 
-def residual_kernel(
-    part_ref, x_ref, gain_ref, up_own, up_peer0, up_peer1, marks_ref,
-    res_ref, n_ref, up_all, far_peer, far_marks,
-    from_left, from_right, to_right, to_left, sems, peer_sems, far_sems, near_sems,
+EARLY = 160
+BAND = 256
+
+
+def front_kernel(
+    offsets_ref, x_ref, gain1_ref, gain2_ref, wq_ref, wk_ref, wv_ref, wo_ref, cos_ref, sin_ref, ids_ref, slots_ref, up_hbm,
+    n1_ref, q_ref, k_ref, v_ref, att_ref, lse_ref, res_ref, n_ref, marks_ref, far_marks, up_peer, far_up,
+    from_left, from_right, to_right, to_left, sems, peer_sems, far_sems, terms,
 ):
-    parts = part_ref.shape[0]
-    line = Line(parts, lambda at: part_ref[at].astype(F32), from_left, from_right, to_right, to_left, sems)
+    parts = x_ref.shape[0]
+    rows, width = n1_ref.shape
+    side = lax.axis_index("expert")
+    peer = {"expert": 1 - side}
+    line = Line(parts, lambda at: terms[at], from_left, from_right, to_right, to_left, sems)
+    meet(line_partners() + [(True, peer), (True, beside())])
+    early, late = pl.ds(0, EARLY), pl.ds(EARLY, rows - EARLY)
+    up_early = plain_copy(up_hbm.at[early, :], up_peer.at[early, :], far_sems, 0, peer)
+    up_late = plain_copy(up_hbm.at[late, :], up_peer.at[late, :], far_sems, 1, peer)
+    up_cross = plain_copy(up_hbm, far_up, far_sems, 2, beside())
+    key_copy = plain_copy(k_ref.at[0], k_ref.at[1], far_sems, 3, peer)
+    value_copy = plain_copy(v_ref.at[0], v_ref.at[1], far_sems, 4, peer)
+    marks_copy = plain_copy(marks_ref.at[0], marks_ref.at[1], far_sems, 5, peer)
+    marks_cross = plain_copy(marks_ref, far_marks, far_sems, 6, beside())
+    up_early.start()
+    up_cross.start()
     line.clear()
-    meet(line_partners() + [(True, {"expert": 1 - lax.axis_index("expert")}), (True, beside())])
-    quarter = up_peer0.shape[0]
-    far_copies = [
-        plain_copy(marks_ref, far_marks, far_sems, 0, beside()),
-        plain_copy(up_peer0, far_peer.at[pl.ds(0, quarter), :], far_sems, 1, beside()),
-        plain_copy(up_peer1, far_peer.at[pl.ds(quarter, quarter), :], far_sems, 2, beside()),
-    ]
-    near_copies = [
-        pltpu.make_async_copy(up_own, up_all.at[pl.ds(0, 2 * quarter), :], near_sems.at[0]),
-        pltpu.make_async_copy(up_peer0, up_all.at[pl.ds(2 * quarter, quarter), :], near_sems.at[1]),
-        pltpu.make_async_copy(up_peer1, up_all.at[pl.ds(3 * quarter, quarter), :], near_sems.at[2]),
-    ]
-    for copy in far_copies + near_copies:
-        copy.start()
+
+    values = x_ref[...].reshape(rows, width).astype(F32)
+    normed = (values * scale_of(values) * gain1_ref[...]).astype(BF)
+    n1_ref[...] = normed
+    queries, kv = q_ref.shape[1], k_ref.shape[2]
+
+    def rotate(array):
+        wide = array.shape[1]
+        lane = lax.broadcasted_iota(jnp.int32, (1, wide), 1)
+        first = lane % HEAD_SIZE < HEAD_SIZE // 2
+        cosines = jnp.concatenate([cos_ref[...]] * (wide // 128), axis=1)
+        sines = jnp.concatenate([sin_ref[...]] * (wide // 128), axis=1)
+        return (array * cosines + turn(array, first) * sines).astype(BF)
+
+    k_ref[0] = rotate(matmul(normed, wk_ref[...]))
+    key_copy.start()
+    v_ref[0] = matmul(normed, wv_ref[...]).astype(BF)
+    value_copy.start()
+    experts_all = marks_ref.shape[2] // 2
+    lane = lax.broadcasted_iota(jnp.int32, (1, experts_all), 1)
+    chosen = jnp.zeros((rows, experts_all), F32)
+    kept = jnp.zeros((rows, experts_all), F32)
+    for pick in range(ids_ref.shape[1]):
+        hit = ids_ref[:, pick : pick + 1] == lane
+        chosen = chosen + jnp.where(hit, 1.0, 0.0)
+        kept = kept + jnp.where(hit & (slots_ref[:, pick : pick + 1] >= 0), 1.0, 0.0)
+    marks_ref[0] = jnp.concatenate([chosen, kept], axis=1).astype(BF)
+    marks_copy.start()
+    up_late.start()
+    q_ref[...] = rotate(matmul(normed, wq_ref[...]))
+    key_copy.wait_recv()
+    value_copy.wait_recv()
+    sharing = queries // kv
+
+    def attend(at):
+        start = pl.multiple_of(at * BAND, BAND)
+        band = pl.ds(start, BAND)
+        allowed = allowed_pairs(offsets_ref, rows, start, BAND)
+        pieces = []
+        for head in range(queries // HEAD_SIZE):
+            kv_at = head // sharing * HEAD_SIZE
+            query = q_ref[band, head * HEAD_SIZE : (head + 1) * HEAD_SIZE]
+            key = k_ref[:, :, kv_at : kv_at + HEAD_SIZE].reshape(2 * rows, HEAD_SIZE)
+            value = v_ref[:, :, kv_at : kv_at + HEAD_SIZE].reshape(2 * rows, HEAD_SIZE)
+            scores = jnp.where(allowed, matmul_nt(query, key) * (HEAD_SIZE**-0.5), masked_score)
+            peak = jnp.max(scores, axis=1, keepdims=True)
+            weights = jnp.exp(scores - peak)
+            total = jnp.sum(weights, axis=1, keepdims=True)
+            pieces.append(matmul((weights * (1.0 / total)).astype(BF), value))
+            lse_ref[band, head : head + 1] = peak + jnp.log(total)
+        attended = jnp.concatenate(pieces, axis=1).astype(BF)
+        att_ref[band, :] = attended
+        count = BAND // PART
+        terms[pl.ds(at * count, count)] = matmul(attended, wo_ref[...]).reshape(count, PART, width)
 
     def body(at, carry):
-        line.step(at)
-        part = at - LAG * line.last
+        @pl.when(at < rows // BAND)
+        def _():
+            attend(at)
+
+        @pl.when(at == 3)
+        def _():
+            marks_copy.wait_recv()
+            marks_cross.start()
+
+        line.step(at - 1)
+        part = at - 1 - LAG * line.last
 
         @pl.when(part >= 0)
         def _():
             residual = x_ref[part].astype(F32) + line.total(part)
             res_ref[part] = residual
             unit = residual * scale_of(residual)
-            n_ref[0, part] = (unit * gain_ref[...]).astype(BF)
+            n_ref[0, part] = (unit * gain2_ref[...]).astype(BF)
             peer_copy(n_ref.at[0, part], n_ref.at[1, part], peer_sems, part).start()
 
         return carry
 
-    lax.fori_loop(0, parts + LAG * line.last, body, 0)
+    lax.fori_loop(0, 1 + parts + LAG * line.last, body, 0)
     line.drain()
+    for copy in (key_copy, value_copy, marks_copy):
+        copy.wait_send()
+    for copy in (up_early, up_late, up_cross, marks_cross):
+        copy.wait()
 
     def wait(part, carry):
         peer_copy(n_ref.at[0, part], n_ref.at[1, part], peer_sems, part).wait()
         return carry
 
     lax.fori_loop(0, parts, wait, 0)
-    for copy in far_copies + near_copies:
-        copy.wait()
-
-
-def residual_norm(part, block_input, gain, upstream, peer_up, marks):
+
+
+def front(
+    offsets, block_input, first_gain, second_gain, w_query, key_weight, value_weight, w_output, cosines, sines,
+    expert_ids, slot_index, upstream, experts_all,
+):
     rows, width = block_input.shape
     parts = rows // PART
+    queries, kv = w_query.shape[1], key_weight.shape[1]
     any_spec = pl.BlockSpec(memory_space=pl.ANY)
-    residual, normed, *rest = pl.pallas_call(
-        residual_kernel,
+    low = lambda *shape: jax.ShapeDtypeStruct(shape, BF)
+    return pl.pallas_call(
+        front_kernel,
         out_shape=(
+            low(rows, width),
+            low(rows, queries),
+            low(2, rows, kv),
+            low(2, rows, kv),
+            low(rows, queries),
+            jax.ShapeDtypeStruct((rows, 128), F32),
             jax.ShapeDtypeStruct((parts, PART, width), F32),
-            jax.ShapeDtypeStruct((2, parts, PART, width), BF),
-            jax.ShapeDtypeStruct((2 * rows, width), BF),
-            jax.ShapeDtypeStruct((rows, width), BF),
-            jax.ShapeDtypeStruct(marks.shape, BF),
+            low(2, parts, PART, width),
+            low(2, rows, 2 * experts_all),
+            low(2, rows, 2 * experts_all),
+            low(rows, width),
+            low(rows, width),
         ),
-        in_specs=[vmem_spec()] * 3 + [any_spec] * 4,
-        out_specs=(vmem_spec(),) * 2 + (any_spec,) * 3,
+        in_specs=[smem_spec()] + [vmem_spec()] * 11 + [any_spec],
+        out_specs=(vmem_spec(),) * 9 + (any_spec,) * 3,
         scratch_shapes=line_scratch(parts, width)
-        + [pltpu.SemaphoreType.DMA((2, parts)), pltpu.SemaphoreType.DMA((2, 3)), pltpu.SemaphoreType.DMA((3,))],
+        + [
+            pltpu.SemaphoreType.DMA((2, parts)),
+            pltpu.SemaphoreType.DMA((2, 7)),
+            pltpu.VMEM((parts, PART, width), F32),
+        ],
         compiler_params=pltpu.CompilerParams(
-            collective_id=0, has_side_effects=True, vmem_limit_bytes=40 * MIB
+            collective_id=0, has_side_effects=True, vmem_limit_bytes=60 * MIB
         ),
         cost_estimate=LINK_COST,
-        name="residual_norm",
+        name="front",
     )(
-        part.reshape(parts, PART, width), block_input.reshape(parts, PART, width), gain[None],
-        upstream, *peer_up, marks,
-    )
-    return residual, normed.reshape(2 * rows, width), *rest
+        offsets, block_input.reshape(parts, PART, width), first_gain[None], second_gain[None], w_query, key_weight,
+        value_weight, w_output, cosines, sines, expert_ids, slot_index, upstream,
+    )
 
 
 UNIT = 512
@@ -1248,7 +1292,7 @@
             pltpu.SemaphoreType.DMA((2, 11)),
         ],
         compiler_params=pltpu.CompilerParams(
-            collective_id=2, has_side_effects=True, vmem_limit_bytes=56 * MIB
+            collective_id=2, has_side_effects=True, vmem_limit_bytes=60 * MIB
         ),
         cost_estimate=LINK_COST,
         name="input_grad",
@@ -1296,10 +1340,10 @@
 
 
 def expert_kernel(
-    n_ref, g_ref, marks_ref, wr_ref, n_hbm, far_g0, far_g1, far_m, wg_ref, wu_ref, wd_ref,
-    dwg_ref, dwu_ref, dwd_ref, mix_ref, back_ref, route_ref, far_n, far_on, far_og0, far_og1, far_om,
+    n_ref, marks_ref, wr_ref, n_hbm, own_up, peer_up, far_g0, far_m, wg_ref, wu_ref, wd_ref,
+    dwg_ref, dwu_ref, dwd_ref, mix_ref, back_ref, route_ref, far_n, far_on, far_g1, far_og0, far_og1, far_om,
     gates, kept_gates, gate_grads, mix, back, nt, wgs, wus, ght, dgs, dus,
-    out_g, out_u, out_d, in_g, in_u, in_d, sems, far_sems,
+    out_g, out_u, out_d, in_g, in_u, in_d, sems, far_sems, g_ref, up_sems,
 ):
     step = pl.program_id(0)
     steps = pl.num_programs(0) // 2
@@ -1332,15 +1376,24 @@
         plain_copy(far_n.at[pl.ds(at * half, half), :], far_on.at[pl.ds(at * half, half), :], far_sems, 2 + at, other)
         for at in range(2)
     ]
+    peer = {"expert": 1 - side}
+    turn_up = plain_copy(far_g0, far_g1, far_sems, 4, peer)
+    share_up = plain_copy(far_g1, far_og1, far_sems, 5, other)
     early = [
-        plain_copy(source, target, far_sems, 4 + at, other)
-        for at, (source, target) in enumerate(((far_g0, far_og0), (far_g1, far_og1), (far_m, far_om)))
+        plain_copy(source, target, far_sems, 6 + at, other)
+        for at, (source, target) in enumerate(((far_g0, far_og0), (far_m, far_om)))
+    ]
+    loads = [
+        pltpu.make_async_copy(source, g_ref.at[pl.ds(at * half, half), :], up_sems.at[at])
+        for at, source in enumerate((own_up, peer_up))
     ]
 
     @pl.when(step == 0)
     def _():
-        meet([(True, other), (True, beside())])
-        for copy in cross + early:
+        for copy in loads:
+            copy.start()
+        meet([(True, other), (True, beside()), (True, peer)])
+        for copy in cross + early + [turn_up]:
             copy.start()
 
         def start(at, carry):
@@ -1356,6 +1409,15 @@
         lax.fori_loop(0, chunks, start, 0)
         for at in range(chunks):
             nt[:, at * CHUNK : (at + 1) * CHUNK] = n_ref[at * CHUNK : (at + 1) * CHUNK, :].T
+        for copy in loads:
+            copy.wait()
+
+    @pl.when(step == steps)
+    def _():
+        cross[0].wait_recv()
+        share[0].start()
+        turn_up.wait_recv()
+        share_up.start()
 
     for expert in range(group):
         wgs[:, expert * hid : (expert + 1) * hid] = wg_ref[expert]
@@ -1428,9 +1490,8 @@
 
     @pl.when(step == 2 * steps - 1)
     def _():
-        for at in range(2):
-            cross[at].wait_recv()
-            share[at].start()
+        cross[1].wait_recv()
+        share[1].start()
         route_ref[...] = jnp.zeros(route_ref.shape, F32)
 
         def finish(at, carry):
@@ -1444,13 +1505,13 @@
             return carry
 
         lax.fori_loop(0, chunks, finish, 0)
-        for copy in cross:
+        for copy in cross + [turn_up]:
             copy.wait_send()
-        for copy in share + early:
+        for copy in share + early + [share_up]:
             copy.wait()
 
 
-def experts(normed, upstream, marks, w_router, far_own, far_peer, far_marks, w_gate, w_up, w_down):
+def experts(normed, marks, w_router, upstream, peer_up, far_up, far_marks, w_gate, w_up, w_down):
     tokens, width = normed.shape
     count, _, hid = w_gate.shape
     half = count // 2
@@ -1464,10 +1525,10 @@
         return (jnp.where(step < steps, (1 - core) * steps + step, core * steps + step - steps), 0, 0)
 
     own = lambda step: (jnp.maximum(step - steps, 0), 0, 0)
-    args = [normed, upstream, marks, w_router]
+    args = [normed, marks, w_router]
     specs = [pl.BlockSpec(array.shape, whole, pipeline_mode=once) for array in args]
-    args += [normed, far_own, far_peer, far_marks]
-    specs += [pl.BlockSpec(memory_space=pl.ANY)] * 4
+    args += [normed, upstream, peer_up, far_up, far_marks]
+    specs += [pl.BlockSpec(memory_space=pl.ANY)] * 5
     up_block, down_block = (GROUP, width, hid), (GROUP, hid, width)
     specs += [pl.BlockSpec(up_block, picked), pl.BlockSpec(up_block, picked), pl.BlockSpec(down_block, picked)]
     gate_scratch = pltpu.VMEM((tokens, experts_all), F32)
@@ -1488,8 +1549,9 @@
             jax.ShapeDtypeStruct((experts_all, width), F32),
             jax.ShapeDtypeStruct((tokens, width), BF),
             jax.ShapeDtypeStruct((tokens, width), BF),
-            jax.ShapeDtypeStruct(far_own.shape, BF),
-            jax.ShapeDtypeStruct(far_peer.shape, BF),
+            jax.ShapeDtypeStruct(far_up.shape, BF),
+            jax.ShapeDtypeStruct(far_up.shape, BF),
+            jax.ShapeDtypeStruct(far_up.shape, BF),
             jax.ShapeDtypeStruct(far_marks.shape, BF),
         ],
         grid=(2 * steps,),
@@ -1502,7 +1564,7 @@
             pl.BlockSpec((tokens, width), whole, pipeline_mode=once),
             pl.BlockSpec((experts_all, width), whole, pipeline_mode=once),
         ]
-        + [pl.BlockSpec(memory_space=pl.ANY)] * 5,
+        + [pl.BlockSpec(memory_space=pl.ANY)] * 6,
         scratch_shapes=[
             gate_scratch, gate_scratch, gate_scratch, rows_scratch, rows_scratch,
             pltpu.VMEM((width, tokens), BF),
@@ -1514,7 +1576,7 @@
         ]
         + swap_scratch
         + swap_scratch
-        + [pltpu.SemaphoreType.DMA((2, 3, steps)), pltpu.SemaphoreType.DMA((2, 7))],
+        + [pltpu.SemaphoreType.DMA((2, 3, steps)), pltpu.SemaphoreType.DMA((2, 8)), pltpu.VMEM((tokens, width), BF), pltpu.SemaphoreType.DMA((2,))],
         compiler_params=pltpu.CompilerParams(
             dimension_semantics=("arbitrary",), collective_id=3, has_side_effects=True, vmem_limit_bytes=60 * MIB
         ),
@@ -1574,53 +1636,27 @@
     w_gate, w_up, w_down, expert_ids, slot_index, piece_start_offsets, upstream,
 ):
     rows, width = block_input.shape
-    local_heads = w_query.shape[1] // HEAD_SIZE
-    local_kv = key_weight.shape[1] // HEAD_SIZE
     experts_all = w_router.shape[1]
-    side = lax.axis_index("expert")
     core = lax.axis_index("dp") % 2
     feature_start = lax.axis_index("tensor") * (width // 4)
-    scal = jnp.concatenate([side[None].astype(jnp.int32), piece_start_offsets[0]])
-
-    axis_row = jnp.arange(experts_all, dtype=jnp.int32)[None, None, :]
-    hits = (expert_ids[:, :, None] == axis_row)
-    chosen = jnp.sum(hits.astype(F32), axis=1)
-    kept = jnp.sum((hits & (slot_index >= 0)[:, :, None]).astype(F32), axis=1)
-    marks = jnp.concatenate([chosen, kept], axis=1).astype(BF)
-    marks = jnp.concatenate([marks, swap(marks, "expert", 1)], axis=0)
-    far_up = swap(upstream, "dp", 2)
-    peer_up = [swap(upstream[: rows // 2], "expert", 1)]
-
-    positions = side * rows + jnp.arange(rows, dtype=jnp.int32)
+    positions = lax.axis_index("expert") * rows + jnp.arange(rows, dtype=jnp.int32)
     cosine_table, sine_table = rope_tables(positions)
     cosines = jnp.tile(cosine_table, (1, 4))
     sines = jnp.tile(sine_table, (1, 4))
-    inputs = block_input.astype(F32)
-    first_scale = norm_scale(inputs)
-    first_unit = inputs * first_scale
-    first_normed = (first_unit * first_gain).astype(BF)
-    query_rot = apply_rotary(
-        matmul(first_normed, w_query).reshape(rows, local_heads, HEAD_SIZE), cosine_table, sine_table
-    ).astype(BF).reshape(rows, local_heads * HEAD_SIZE)
-    key_rot = apply_rotary(
-        matmul(first_normed, key_weight).reshape(rows, local_kv, HEAD_SIZE), cosine_table, sine_table
-    ).astype(BF).reshape(rows, local_kv * HEAD_SIZE)
-    value_low = matmul(first_normed, value_weight).astype(BF)
-    both = jnp.concatenate([key_rot, value_low], axis=1)
-    later, both = lax.optimization_barrier((upstream[rows // 2 :], both))
-    peer_up.append(swap(later, "expert", 1))
-    both = jnp.concatenate([both, swap(both, "expert", 1)], axis=0)
-    keys, values = both[:, : local_kv * HEAD_SIZE], both[:, local_kv * HEAD_SIZE :]
-
-    attended, lse, part = attend(scal, query_rot, keys, values, w_output)
-    part, far_up = lax.optimization_barrier((part, far_up))
-    residual, normed_all, upstream_all, far_peer_up, far_marks = residual_norm(
-        part, block_input, second_gain, upstream, peer_up, marks
-    )
+    (
+        first_normed, query_rot, keys, values, attended, lse, residual, normed_all, marks, far_marks, peer_up, far_up,
+    ) = front(
+        piece_start_offsets, block_input, first_gain, second_gain, w_query, key_weight, value_weight, w_output,
+        cosines, sines, expert_ids, slot_index, upstream, experts_all,
+    )
+    keys, values = keys.reshape(2 * rows, -1), values.reshape(2 * rows, -1)
+    normed_all = normed_all.reshape(2 * rows, width)
+    marks = marks.reshape(2 * rows, 2 * experts_all)
+    far_marks = far_marks.reshape(2 * rows, 2 * experts_all)
     dwg, dwu, dwd, mix, back, route, *far = experts(
-        normed_all, upstream_all, marks, w_router, far_up, far_peer_up, far_marks, w_gate, w_up, w_down
-    )
-    far_normed, far_other_normed, far_other_up, far_other_peer_up, far_other_marks = far
+        normed_all, marks, w_router, upstream, peer_up, far_up, far_marks, w_gate, w_up, w_down
+    )
+    far_normed, far_other_normed, far_peer_up, far_other_up, far_other_peer_up, far_other_marks = far
     residual_grad, residual_low, grad_second, route, mixed, sums = residual_gradient(
         back, mix, route, residual, upstream, second_gain, w_router,
         (
@@ -1632,7 +1668,7 @@
     mixed = lax.psum_scatter(mixed, "tensor", scatter_dimension=1, tiled=True)
 
     query_grad, dk, dv, grad_output = attend_back(
-        scal, query_rot, keys, values, lse, attended, residual_low, w_output, cosines, sines
+        piece_start_offsets, query_rot, keys, values, lse, attended, residual_low, w_output, cosines, sines
     )
     grad_input, grad_query, grad_key, grad_value, grad_output, grad_router, grad_second, grad_first = input_gradient(
         block_input, residual_grad, first_gain, first_normed, query_grad, dk, dv, w_query, key_weight, value_weight,

time: 342 us -> 319 us (0.933)
  Pallas kernels: 265 us -> 290 us
  waiting for transfers between devices: 22.9 us -> 0.03 us
  local copies, waits for them, and re-layouts: 23.6 us -> 11.3 us
  starting transfers between devices: 7.74 us -> 0.69 us
    ppermute x8 -> x3, waiting for transfers between devices: 22.9 us -> 0.01 us  [swap(): return lax.ppermute(array, axis, [(at, at ^ bit) for at in range(size)])]
    pallas_call x2 -> x1, Pallas kernels: 43.7 us -> 65.3 us  [front(): pl.pallas_call(front_kernel, out_shape=(low(rows, width), low(rows, queri...]
    ppermute x8 -> x3, starting transfers between devices: 7.7 us -> 0.65 us  [swap(): return lax.ppermute(array, axis, [(at, at ^ bit) for at in range(size)])]
    unnamed x86 -> x37, local copies, waits for them, and re-layouts: 16.3 us -> 9.62 us
    pallas_call x3, Pallas kernels: 13.5 us -> 18.6 us  [widen(): pl.pallas_call(widen_kernel, out_shape=jax.ShapeDtypeStruct((2 * half, hi...]
  transfers between devices with their start and end apart: 9 -> 4, of which waited for: 1 -> 0; matrix products, arithmetic and copies ran while one was open for 4% -> 0% of each run, Pallas kernels for 26% -> 27%
where the time goes in v6:
time: 319 us
  Pallas kernels  290 us (91%)
  between operations  14.4 us (5%)
  local copies, waits for them, and re-layouts  11.3 us (4%)
    pallas_call x1, Pallas kernels, experts(): pl.pallas_call(expert_kernel, out_shape=[jax.ShapeDtypeStruct((half, widt...  71.8 us
    pallas_call x1, Pallas kernels, residual_gradient(): pl.pallas_call(residual_grad_kernel, out_shape=[jax.ShapeDtypeStruct((par...  67 us
    pallas_call x1, Pallas kernels, front(): pl.pallas_call(front_kernel, out_shape=(low(rows, width), low(rows, queri...  65.3 us
    pallas_call x1, Pallas kernels, input_gradient(): pl.pallas_call(input_grad_kernel, out_shape=(jax.ShapeDtypeStruct((parts,...  54.9 us
    pallas_call x3, Pallas kernels, widen(): pl.pallas_call(widen_kernel, out_shape=jax.ShapeDtypeStruct((2 * half, hi...  18.6 us
    pallas_call x1, Pallas kernels, attend_back(): pl.pallas_call(attend_back_kernel, out_shape=(jax.ShapeDtypeStruct((rows,...  12.6 us
    unnamed x37, local copies, waits for them, and re-layouts  9.62 us
  transfers between devices with their start and end apart: 4, of which 0 were waited for; matrix products, arithmetic and copies ran while one was open for 0% of the time, Pallas kernels for 27%

profile of v6, /device:TPU:0, one launch (start us, length us, event | category | flops | bytes accessed | tf_op | source)
XLA Modules:
  0.0 319.0 jit_solution(9738290441061465314)
XLA Ops:
  7.3 0.3 multiply_sine_fusion
  7.6 0.8 copy.31.cos_ref
  8.5 0.8 copy.32.sin_ref
  9.3 1.6 copy.33.ids_ref
  10.9 0.8 copy.34.slots_ref
  11.7 0.8 copy.35.wr_ref
  12.6 65.3 %front.1 = (bf16[512,1024]{1,0:T(8,128)(2,1)}, bf16[512,256]{1,0:T(8,128)(2,1)}, bf16[2,512,128]{2,1,0:T(8,128)(2,1)}, bf16[2,512,128]{2,1,0:T(8,128)(2,1)}, bf1...) custom-call(s32[1,2]{1,0:T(1,128)} %scal_ref.1, ...), custom_call_target="tpu_custom_call" | custom-call | flops 40000000000 | bytes 10000000 | tf_op jit(solution)/shard_map/front/pallas_call | solution.py:789
  77.9 71.8 %experts.1 = (bf16[8,1024,128]{2,1,0:T(8,128)(2,1)}, bf16[8,1024,128]{2,1,0:T(8,128)(2,1)}, bf16[8,128,1024]{2,1,0:T(8,128)(2,1)}, bf16[1024,1024]{1,0:T(8,128)(...) custom-call(bf16[1024,1024]{1,0:T(8,128)(2,1)} %bitcast.39, ...), custom_call_target="tpu_custom_call" | custom-call | flops 38654705664 | bytes 25165824 | tf_op jit(solution)/shard_map/experts/pallas_call | solution.py:1541
  149.7 67.0 %residual_grad.1 = (f32[16,32,1024]{2,1,0:T(8,128)}, bf16[16,32,1024]{2,1,0:T(8,128)(2,1)}, f32[1,1024]{1,0:T(1,128)}, f32[32,1024]{1,0:T(8,128)}, bf16[16,32,10...) custom-call(bf16[2,16,32,1024]{3,2,1,0:T(8,128)(2,1)} %bitcast.42, ...), custom_call_target="tpu_custom_call" | custom-call | flops 40000000000 | bytes 10000000 | tf_op jit(solution)/shard_map/residual_grad/pallas_call | solution.py:1035
  216.8 0.5 collective-permute-start.1
  217.3 12.6 %attend_back.1 = (bf16[512,256]{1,0:T(8,128)(2,1)}, bf16[1024,128]{1,0:T(8,128)(2,1)}, bf16[1024,128]{1,0:T(8,128)(2,1)}, f32[256,1024]{1,0:T(8,128)}) custom-call(s32[1,2]{1,0:T(1,128)} %scal_ref.1, bf16[512,256]{1,0:T(8,128)(2,1)} %get-tuple-element.77.q_ref, bf16[1024,128]{1,0:T(8,128)(2,1)} %bitcast.26, bf16[1024,128]{1,0:T(8,128)(2,1)} %bitcast.27, ...), custom_call_target="tpu_custom_call" | custom-call | tf_op jit(solution)/shard_map/attend_back/pallas_call | solution.py:516
  229.9 54.9 %input_grad.1 = (bf16[16,32,1024]{2,1,0:T(8,128)(2,1)}, f32[1024,256]{1,0:T(8,128)}, f32[1024,128]{1,0:T(8,128)}, f32[1024,128]{1,0:T(8,128)}, f32[256,1024]{1,0...) custom-call(bf16[16,32,1024]{2,1,0:T(8,128)(2,1)} %bitcast.34, ...), custom_call_target="tpu_custom_call" | custom-call | flops 40000000000 | bytes 10000000 | tf_op jit(solution)/shard_map/input_grad/pallas_call | solution.py:1270
  284.9 6.2 %widen.3 = f32[16,1024,128]{2,1,0:T(8,128)} custom-call(s32[1]{0:T(128)} %bitcast.20.core_ref, bf16[8,1024,128]{2,1,0:T(8,128)(2,1)S(1)} %copy-done.2, bf16[8,1024,128]{2,1,0:T(8,128)(2,1)} %collective-permute-done.other_ref), custom_call_target="tpu_custom_call" | custom-call | flops 2097152 | bytes 12582912 | tf_op jit(solution)/shard_map/widen/pallas_call | solution.py:1609
  291.2 6.2 %widen.4 = f32[16,1024,128]{2,1,0:T(8,128)} custom-call(s32[1]{0:T(128)} %bitcast.20.core_ref, bf16[8,1024,128]{2,1,0:T(8,128)(2,1)S(1)} %copy-done.1, bf16[8,1024,128]{2,1,0:T(8,128)(2,1)} %collective-permute-done.1.other_ref), custom_call_target="tpu_custom_call" | custom-call | flops 2097152 | bytes 12582912 | tf_op jit(solution)/shard_map/widen/pallas_call | solution.py:1609
  297.4 6.2 %widen.5 = f32[16,128,1024]{2,1,0:T(8,128)} custom-call(s32[1]{0:T(128)} %bitcast.20.core_ref, bf16[8,128,1024]{2,1,0:T(8,128)(2,1)S(1)} %copy-done, bf16[8,128,1024]{2,1,0:T(8,128)(2,1)} %collective-permute-done.2.other_ref), custom_call_target="tpu_custom_call" | custom-call | flops 2097152 | bytes 12582912 | tf_op jit(solution)/shard_map/widen/pallas_call | solution.py:1609
  303.6 2.0 add_convert_fusion
  305.5 1.0 copy.49
  306.5 0.6 copy.50
  307.1 1.0 copy.51
  308.1 0.8 copy.52
  308.9 0.8 copy.53
  309.7 1.0 copy.54
  310.6 0.6 copy.55
  311.2 0.7 copy.56
  (38 shorter events, 0.3 us)
Async XLA Ops:
  7.2 3.7 %copy-start.10 = (s32[512,8]{0,1:T(8,128)S(1)}, s32[512,8]{0,1:T(8,128)}, u32[]{:S(2)}) copy-start(s32[512,8]{0,1:T(8,128)} %param.27) | copy-start | bytes 49156
  7.2 4.5 %copy-start.9 = (bf16[1024,32]{0,1:T(8,128)(2,1)S(1)}, bf16[1024,32]{0,1:T(8,128)(2,1)}, u32[]{:S(2)}) copy-start(bf16[1024,32]{0,1:T(8,128)(2,1)} %param.22) | copy-start | bytes 196612
  7.2 296.4 %reduce-scatter.2.cloned.1.call-start = ((), (), s32[]{:S(2)}) async-start(), calls=%async_computation.1 | async-start | bytes 1310720 | tf_op jit(solution)/shard_map/reduce_scatter | solution.py:1668
  216.7 68.2 %collective-permute-start = (bf16[8,1024,128]{2,1,0:T(8,128)(2,1)}, bf16[8,1024,128]{2,1,0:T(8,128)(2,1)}, u32[]{:S(2)}, u32[]{:S(2)}) collective-permute-start(bf16[8,1024,128]{2,1,0:T(8,128)(2,1)} %get-tuple-element.97.mine_ref), channel_id=1, source_target_pairs={{0,8},{8,0},{16,24},{24,16},{1,9},{9,1},{17,25},{25,17},{2,10},{10... | collective-permute-start | bytes 6291464 | tf_op jit(solution)/shard_map/ppermute | solution.py:1631
  216.8 74.4 %collective-permute-start.1 = (bf16[8,1024,128]{2,1,0:T(8,128)(2,1)}, bf16[8,1024,128]{2,1,0:T(8,128)(2,1)}, u32[]{:S(2)}, u32[]{:S(2)}) collective-permute-start(bf16[8,1024,128]{2,1,0:T(8,128)(2,1)} %get-tuple-element.98.mine_ref), channel_id=1, source_target_pairs={{0,8},{8,0},{16,24},{24,16},{1,9},{9,1},{17,25},{25,17},{2,10},{10... | collective-permute-start | bytes 6291464 | tf_op jit(solution)/shard_map/ppermute | solution.py:1631
  217.2 80.1 %collective-permute-start.2 = (bf16[8,128,1024]{2,1,0:T(8,128)(2,1)}, bf16[8,128,1024]{2,1,0:T(8,128)(2,1)}, u32[]{:S(2)}, u32[]{:S(2)}) collective-permute-start(bf16[8,128,1024]{2,1,0:T(8,128)(2,1)} %get-tuple-element.99.mine_ref), channel_id=1, source_target_pairs={{0,8},{8,0},{16,24},{24,16},{1,9},{9,1},{17,25},{25,17},{2,10},{10... | collective-permute-start | bytes 6291464 | tf_op jit(solution)/shard_map/ppermute | solution.py:1631
  229.9 55.0 %copy-start.2 = (bf16[8,1024,128]{2,1,0:T(8,128)(2,1)S(1)}, bf16[8,1024,128]{2,1,0:T(8,128)(2,1)}, u32[]{:S(2)}) copy-start(bf16[8,1024,128]{2,1,0:T(8,128)(2,1)} %get-tuple-element.97.mine_ref) | copy-start | bytes 6291460
  284.9 6.2 %copy-start.1 = (bf16[8,1024,128]{2,1,0:T(8,128)(2,1)S(1)}, bf16[8,1024,128]{2,1,0:T(8,128)(2,1)}, u32[]{:S(2)}) copy-start(bf16[8,1024,128]{2,1,0:T(8,128)(2,1)} %get-tuple-element.98.mine_ref) | copy-start | bytes 6291460
  291.1 6.2 %copy-start = (bf16[8,128,1024]{2,1,0:T(8,128)(2,1)S(1)}, bf16[8,128,1024]{2,1,0:T(8,128)(2,1)}, u32[]{:S(2)}) copy-start(bf16[8,128,1024]{2,1,0:T(8,128)(2,1)} %get-tuple-element.99.mine_ref) | copy-start | bytes 6291460
  297.4 8.1 %copy-start.5 = (bf16[16,32,1024]{2,1,0:T(8,128)(2,1)S(1)}, bf16[16,32,1024]{2,1,0:T(8,128)(2,1)}, u32[]{:S(2)}) copy-start(bf16[16,32,1024]{2,1,0:T(8,128)(2,1)} %get-tuple-element.89) | copy-start | bytes 3145732
  303.5 3.0 copy-start.12
  303.5 3.5 %copy-start.4 = (f32[1024,256]{1,0:T(8,128)S(1)}, f32[1024,256]{1,0:T(8,128)}, u32[]{:S(2)}) copy-start(f32[1024,256]{1,0:T(8,128)} %get-tuple-element.117) | copy-start | bytes 3145732
  305.5 2.5 copy-start.7
  306.5 2.4 copy-start.6
  307.1 2.6 copy-start.3
  308.1 2.6 copy-start.11
  308.1 3.2 copy-start.8
Sparse Core Ops, SparseCore 0:
  216.8 25.9 reduce-scatter.1
